TPU v7x, 256 devices: a whole 4x4x8 slice. The times are simulated.
256 devices in a mesh: dp: 4 (over x), seq: 32 (over z_hi, y, core), head: 2 (over z_lo).
Axes of the slice: x: 4, y: 4, z: 8 (z_hi: 4, z_lo: 2; z = z_hi * 2 + z_lo), core: 2. Of those that a mesh axis runs over, the one named last changes fastest.
Arguments:
- latents: bfloat16 [4, 8192, 2048], P('dp', 'seq'), may hold values from -6 to 6
- w_qkv: bfloat16 [2048, 3, 1536], P(None, None, 'head'), may hold values from -0.125 to 0.125
- q_gain: float32 [128], replicated, may hold values from 0.1 to 1.9
- k_gain: float32 [128], replicated, may hold values from 0.1 to 1.9
- neighbours: int32 [128, 9], replicated, may hold values from -1 to 127, as said below
- grad_out: bfloat16 [4, 8192, 1536], P('dp', 'seq', 'head'), may hold values from -6 to 6
Outputs:
- attn_out: bfloat16 [4, 8192, 1536], P('dp', 'seq', 'head')
- grad_x: bfloat16 [4, 8192, 2048], P('dp', ('seq', 'head'))
- grad_w: float32 [2048, 3, 1536], P(('dp', 'seq'), None, 'head')
Inputs may be any that keep to these rules, and one draw needn't show every extreme that they name: `neighbours`: row t lists only tiles whose slab differs from that of t (t // 4) by at most one and whose position in the slab (index % 4) differs by at most one, each at most once; t itself is always listed.
All inputs are finite; a program needn't handle non-finite values.
Results may differ from a plain program's by a relative error of at most 0.017.
Values may be sent and summed in bfloat16 or wider, within the bound.
No kernel may reach another device: no remote copies, remote signals or barrier semaphores. Data moves between devices by JAX's collectives and lax.ppermute only.
A program may use at most 128 MiB of HBM per device.

v0:
```python
import math

import jax
import jax.numpy as jnp
from jax import lax
from jax.sharding import PartitionSpec as P

HD = 128
TILE = 64


EPS = 1e-06


def shifted(value, axis, steps):
    count = lax.axis_size(axis)
    initial, last = (max(0, -steps), min(count, count - steps))
    return lax.ppermute(value, axis, [(source, source + steps) for source in range(initial, last)])


def with_halo(block, sides, width):
    for axis, dim in sides:
        count = lax.axis_size(axis)
        forward = [(i, i + 1) for i in range(count - 1)]
        backward = [(target, source) for source, target in forward]
        low = lax.ppermute(
            lax.slice_in_dim(block, block.shape[dim] - width, None, axis=dim), axis, forward
        )
        high = lax.ppermute(lax.slice_in_dim(block, 0, width, axis=dim), axis, backward)
        block = jnp.concatenate([low, block, high], axis=dim)
    return block


def inv_rms(values):
    return lax.rsqrt(jnp.mean(values * values, axis=-1, keepdims=True) + EPS)


def norm_back(raw, inverse, gain, upstream):
    normed = raw * inverse
    weighted = upstream * gain
    return inverse * (weighted - normed * jnp.mean(weighted * normed, axis=-1, keepdims=True))


def tile_allowed(neighbours, query_first, query_count, key_first, key_count):
    tile_total = neighbours.shape[0]
    padded = jnp.pad(neighbours, ((query_count, query_count), (0, 0)), constant_values=-1)
    picked = lax.dynamic_slice_in_dim(padded, query_first + query_count, query_count, 0)
    query_ids = query_first + jnp.arange(query_count, dtype=jnp.int32)
    key_ids = key_first + jnp.arange(key_count, dtype=jnp.int32)
    query_valid = (query_ids >= 0) & (query_ids < tile_total)
    key_valid = (key_ids >= 0) & (key_ids < tile_total)
    hits = jnp.any(picked[:, :, None] == key_ids[None, None, :], axis=1)
    hits = hits & query_valid[:, None] & key_valid[None, :]
    block = jnp.where(hits, 1.0, 0.0).astype(jnp.float32)
    return jnp.repeat(jnp.repeat(block, TILE, axis=0), TILE, axis=1)


def send_rims(grad_parts, offset_by):
    return shifted(grad_parts, "seq", offset_by)


def local(latents, w_qkv, q_gain, k_gain, neighbours, grad_out):
    slab_tokens = latents[0]
    slab_rows = slab_tokens.shape[0]
    model_width = w_qkv.shape[0]
    head_width = w_qkv.shape[2]
    head_count = head_width // HD
    tiles_slab = slab_rows // TILE
    score_scale = 1.0 / math.sqrt(HD)
    flat_w = w_qkv.reshape(model_width, 3 * head_width)
    qkv = jnp.dot(slab_tokens, flat_w, preferred_element_type=jnp.float32).reshape(
        slab_rows, 3, head_count, HD
    )
    q_raw = qkv[:, 0]
    k_raw = qkv[:, 1]
    v_raw = qkv[:, 2]
    q_inv = inv_rms(q_raw)
    k_inv = inv_rms(k_raw)
    q_hat = (q_raw * q_inv * q_gain).astype(jnp.bfloat16)
    k_hat = (k_raw * k_inv * k_gain).astype(jnp.bfloat16)
    v_hat = v_raw.astype(jnp.bfloat16)
    stacked = jnp.stack(
        [k_hat.reshape(slab_rows, head_width), v_hat.reshape(slab_rows, head_width)], axis=1
    )
    widened = with_halo(stacked, (("seq", 0),), slab_rows)
    keys_wide = widened[:, 0].reshape(3 * slab_rows, head_count, HD)
    values_wide = widened[:, 1].reshape(3 * slab_rows, head_count, HD)
    seq_slab = lax.axis_index("seq")
    own_tile = seq_slab * tiles_slab
    first_tile = (seq_slab - 1) * tiles_slab
    allowed = tile_allowed(neighbours, own_tile, tiles_slab, first_tile, 3 * tiles_slab)
    scores = (
        jnp.einsum("qhe,khe->hqk", q_hat, keys_wide, preferred_element_type=jnp.float32)
        * score_scale
    )
    exponent = jnp.exp(scores) * allowed[None]
    row_total = jnp.sum(exponent, axis=-1)
    probs = exponent / row_total[..., None]
    probs_b = probs.astype(jnp.bfloat16)
    attended = jnp.einsum("hqk,khe->qhe", probs_b, values_wide, preferred_element_type=jnp.float32)
    attn_out = attended.astype(jnp.bfloat16).reshape(1, slab_rows, head_width)
    upstream = grad_out[0].reshape(slab_rows, head_count, HD)
    d_probs = jnp.einsum("qhe,khe->hqk", upstream, values_wide, preferred_element_type=jnp.float32)
    row_delta = jnp.sum(probs * d_probs, axis=-1)
    d_scores = (probs * (d_probs - row_delta[..., None]) * score_scale).astype(jnp.bfloat16)
    d_qhat = jnp.einsum("hqk,khe->qhe", d_scores, keys_wide, preferred_element_type=jnp.float32)
    d_kwide = jnp.einsum("hqk,qhe->khe", d_scores, q_hat, preferred_element_type=jnp.float32)
    d_vwide = jnp.einsum("hqk,qhe->khe", probs_b, upstream, preferred_element_type=jnp.float32)
    grad_parts = jnp.stack(
        [d_kwide.reshape(3 * slab_rows, head_width), d_vwide.reshape(3 * slab_rows, head_width)],
        axis=1,
    )
    from_below = send_rims(grad_parts[2 * slab_rows :], 1)
    from_above = send_rims(grad_parts[:slab_rows], -1)
    own_grads = grad_parts[slab_rows : 2 * slab_rows] + from_below + from_above
    d_khat = own_grads[:, 0].reshape(slab_rows, head_count, HD)
    d_value = own_grads[:, 1].reshape(slab_rows, head_count, HD)
    d_query = norm_back(q_raw, q_inv, q_gain, d_qhat)
    d_key = norm_back(k_raw, k_inv, k_gain, d_khat)
    d_qkv = (
        jnp.stack([d_query, d_key, d_value], axis=1)
        .astype(jnp.bfloat16)
        .reshape(slab_rows, 3 * head_width)
    )
    grad_rows = lax.psum_scatter(
        lax.dot_general(
            d_qkv, flat_w, (((1,), (1,)), ((), ())), preferred_element_type=jnp.float32
        ),
        "head",
        scatter_dimension=0,
        tiled=True,
    )
    grad_x = grad_rows.astype(jnp.bfloat16)[None]
    product = lax.dot_general(
        slab_tokens, d_qkv, (((0,), (0,)), ((), ())), preferred_element_type=jnp.float32
    )
    clip_share = lax.psum_scatter(
        product.reshape(
            model_width // lax.axis_size("dp") * lax.axis_size("dp"), 3, head_width
        ).astype(jnp.bfloat16),
        "dp",
        scatter_dimension=0,
        tiled=True,
    )
    grad_w = lax.psum_scatter(clip_share, "seq", scatter_dimension=0, tiled=True).astype(
        jnp.float32
    )
    return (attn_out, grad_x, grad_w)


def solution(mesh):
    in_specs = (P("dp", "seq", None), P(None, None, "head"), P(), P(), P(), P("dp", "seq", "head"))
    out_specs = (
        P("dp", "seq", "head"),
        P("dp", ("seq", "head"), None),
        P(("dp", "seq"), None, "head"),
    )
    return jax.shard_map(local, mesh=mesh, in_specs=in_specs, out_specs=out_specs, check_vma=False)
```

profile of v0, /device:TPU:6, one launch (start us, length us, event | category | flops | bytes accessed | tf_op | source)
XLA Modules:
  0.0 393.4 jit_solution(3830548987301960321)
XLA Ops:
  7.2 0.0 copy-start
  7.2 0.0 reduce-scatter.6.cloned.1.call-start
  7.2 12.8 %copy.29 = bf16[2048,3,768]{0,2,1:T(8,128)(2,1)} copy(bf16[2048,3,768]{2,0,1:T(8,128)(2,1)} %param.7) | data formatting | bytes 18874368 | tf_op args[1]
  20.1 0.0 copy-done
  20.1 5.3 %fusion.18 = f32[256,3,6,128]{0,3,2,1:T(8,128)S(1)} fusion(bf16[3,6,128,2048]{3,2,1,0:T(8,128)(2,1)} %bitcast.119, bf16[1,256,2048]{2,1,0:T(8,128)(2,1)S(1)} %copy-done), kind=kOutput, calls=%fused_computation.30 | convolution fusion | flops 2415919104 | bytes 12845056 | tf_op jit(solution)/shard_map/dot_general | solution.py:71
  25.3 0.0 copy-start.10
  25.3 0.1 multiply_reduce_fusion.1
  25.5 0.0 copy-start.5
  25.5 0.1 slice.42
  25.6 0.1 mul.180
  25.7 0.2 fusion.22
  25.9 0.0 copy-start.6
  25.9 0.4 copy-done.5
  26.3 1.0 pad_maximum_fusion.3
  27.2 1.3 collective-permute-start.1
  28.5 3.9 %collective-permute-start = (bf16[256,2,768]{0,2,1:T(8,128)(2,1)}, bf16[256,2,768]{0,2,1:T(8,128)(2,1)}, u32[]{:S(2)}, u32[]{:S(2)}) collective-permute-start(bf16[256,2,768]{0,2,1:T(8,128)(2,1)} %pad_maximum_fusion.3), channel_id=1, source_target_pairs={{0,2},{2,4},{4,6},{6,8},{8,10},{10,12},{12,14},{14,16},{16,18},{18... | collective-permute-start | bytes 2359304 | tf_op jit(solution)/shard_map/ppermute | solution.py:26
  32.5 0.1 pad_dynamic-slice_fusion
  32.6 0.1 compare_reduce_fusion
  32.7 0.1 and_select_fusion
  32.7 0.1 copy.32
  32.8 0.1 broadcast_in_dim.16
  32.9 0.1 reshape.161
  33.0 1.9 copy.34
  34.9 0.9 broadcast_in_dim.17
  35.9 2.3 copy.33
  38.2 0.0 collective-permute-done.1
  38.2 0.0 collective-permute-done
  38.2 1.8 pad_maximum_fusion
  40.0 0.0 copy-start.8
  40.0 0.0 copy-start.12
  40.1 0.2 fusion.39
  40.3 3.1 fusion.40
  43.3 0.0 copy-done.12
  43.3 1.4 fusion.5
  44.8 2.1 copy-done.1
  46.9 2.7 fusion.15
  49.6 16.3 %fusion.7 = f32[6,128,768]{2,1,0:T(8,128)} fusion(f32[6,768,256]{1,2,0:T(8,128)} %fusion.40, f32[256,3,6,128]{0,3,2,1:T(8,128)S(1)} %fusion.18, f32[128]{0:T(128)S(1)} %copy-done.12, f32[256,6]{0,1:T(8,128)S(1)} %get-tuple-element.22, f32[6,256,768]{2,1,0:T(8,128)} %copy-done.1, f32[6,256]{1,0:T(8,128)S(1)} %get-tuple-element.20, f32[256,768]{1,0:T(8,128)} %copy.33), kind=kOutput, calls=%fused_computation.16 | convolution fusion | flops 315558144 | bytes 23618048 | tf_op jit(solution)/shard_map/hqk,qhe->khe/dot_general | solution.py:107
  65.9 3.7 fusion.9
  69.7 6.8 %collective-permute-start.2 = (f32[256,2,768]{0,2,1:T(8,128)}, f32[256,2,768]{0,2,1:T(8,128)}, u32[]{:S(2)}, u32[]{:S(2)}) collective-permute-start(f32[256,2,768]{0,2,1:T(8,128)} %get-tuple-element.16), channel_id=1, source_target_pairs={{0,2},{2,4},{4,6},{6,8},{8,10},{10,12},{12,14},{14,16},{16,18},{18... | collective-permute-start | bytes 4718600 | tf_op jit(solution)/shard_map/ppermute | solution.py:18
  76.4 1.5 collective-permute-start.3
  77.9 15.3 %fusion.14 = f32[256,6,128]{0,2,1:T(8,128)} fusion(bf16[768,6,128]{0,2,1:T(8,128)(2,1)} %bitcast.133, f32[6,768,256]{1,2,0:T(8,128)} %fusion.40, f32[128]{0:T(128)S(1)} %copy-done.12, f32[6,256,768]{2,1,0:T(8,128)} %copy-done.1, f32[6,256]{1,0:T(8,128)S(1)} %get-tuple-element.20, f32[256,768]{1,0:T(8,128)} %copy.33), kind=kOutput, calls=%fused_computation.24 | convolution fusion | flops 315164928 | bytes 12196352 | tf_op jit(solution)/shard_map/hqk,khe->qhe/dot_general | solution.py:106
  93.2 0.0 collective-permute-done.2
  93.2 0.0 collective-permute-done.3
  93.2 2.7 fusion.12
  96.0 0.1 slice.51
  96.1 0.4 multiply_reduce_fusion
  96.4 0.2 fusion.27
  96.6 0.2 multiply_convert_fusion
  96.8 0.1 pad_maximum_fusion.2
  97.0 5.1 %convolution_convert_fusion = bf16[2304,2048]{1,0:T(8,128)(2,1)} fusion(bf16[256,2304]{0,1:T(8,128)(2,1)S(1)} %bitcast.122, bf16[1,256,2048]{2,1,0:T(8,128)(2,1)S(1)} %copy-done), kind=kOutput, calls=%fused_computation.1 | convolution fusion | flops 2420637696 | bytes 11665408 | tf_op jit(solution)/shard_map/dot_general | solution.py:134
  102.1 12.7 %copy.38 = bf16[2048,3,768]{2,0,1:T(8,128)(2,1)} copy(bf16[2048,3,768]{0,2,1:T(8,128)(2,1)} %bitcast.121) | data formatting | bytes 18874368 | tf_op jit(solution)/shard_map/convert_element_type | solution.py:140
  114.8 0.0 reduce-scatter.6.cloned.1.call-update
  114.8 0.0 reduce-scatter.4.cloned.1.call-start
  114.9 7.7 %fusion.41 = f32[256,2048]{1,0:T(8,128)} fusion(bf16[256,2304]{0,1:T(8,128)(2,1)S(1)} %bitcast.123, bf16[2048,2304]{0,1:T(8,128)(2,1)} %bitcast.120), kind=kOutput, calls=%fused_computation.71 | convolution fusion | flops 2415919104 | bytes 12713984 | tf_op jit(solution)/shard_map/dot_general | solution.py:126
  122.6 0.0 reduce-scatter.4.cloned.1.call-update
  122.7 0.0 reduce-scatter.8.cloned.1.call-start
  122.7 123.9 %reduce-scatter.6.cloned.1.call-done = bf16[512,3,768]{2,0,1:T(8,128)(2,1)} async-done(((bf16[2048,3,768]{2,0,1:T(8,128)(2,1)}), bf16[512,3,768]{2,0,1:T(8,128)(2,1)}) %reduce-scatter.6.cloned.1.call-update) | async-done | bytes 2359312 | tf_op jit(solution)/shard_map/reduce_scatter | solution.py:137
  246.6 0.0 reduce-scatter.8.cloned.1.call-update
  246.6 3.8 convolution_convert_fusion.1
  250.4 0.9 copy.39
  251.3 36.4 %reduce-scatter.4.cloned.1.call-done = f32[128,2048]{1,0:T(8,128)} async-done(((f32[256,2048]{1,0:T(8,128)}), f32[128,2048]{1,0:T(8,128)}) %reduce-scatter.4.cloned.1.call-update) | async-done | bytes 1048592 | tf_op jit(solution)/shard_map/reduce_scatter | solution.py:125
  287.7 2.1 convert_bitcast_fusion
  289.8 95.5 %reduce-scatter.8.cloned.1.call-done = bf16[16,3,768]{2,0,1:T(8,128)(2,1)} async-done(((bf16[512,3,768]{2,0,1:T(8,128)(2,1)}), bf16[16,3,768]{2,0,1:T(8,128)(2,1)}) %reduce-scatter.8.cloned.1.call-update) | async-done | bytes 73744 | tf_op jit(solution)/shard_map/reduce_scatter | solution.py:145
  385.3 1.6 convert_element_type.78
  (25 shorter events, 0.2 us)
Async XLA Ops:
  7.2 12.9 %copy-start = (bf16[1,256,2048]{2,1,0:T(8,128)(2,1)S(1)}, bf16[1,256,2048]{2,1,0:T(8,128)(2,1)}, u32[]{:S(2)}) copy-start(bf16[1,256,2048]{2,1,0:T(8,128)(2,1)} %param.6) | copy-start | bytes 3145732
  7.2 239.4 %reduce-scatter.6.cloned.1.call-start = ((), (), s32[]{:S(2)}) async-start(), calls=%async_computation.4 | async-start | bytes 11796480 | tf_op jit(solution)/shard_map/reduce_scatter | solution.py:137
  20.1 5.5 %copy-start.11 = (f32[128]{0:T(128)S(1)}, f32[128]{0:T(128)}, u32[]{:S(2)}) copy-start(f32[128]{0:T(128)} %param.9) | copy-start | bytes 1540
  25.3 7.2 %copy-start.10 = (s32[128,9]{0,1:T(8,128)S(1)}, s32[128,9]{0,1:T(8,128)}, u32[]{:S(2)}) copy-start(s32[128,9]{0,1:T(8,128)} %param.10) | copy-start | bytes 13828
  25.5 0.7 copy-start.5
  25.9 1.4 copy-start.6
  27.2 11.0 %collective-permute-start.1 = (bf16[256,2,768]{0,2,1:T(8,128)(2,1)}, bf16[256,2,768]{0,2,1:T(8,128)(2,1)}, u32[]{:S(2)}, u32[]{:S(2)}) collective-permute-start(bf16[256,2,768]{0,2,1:T(8,128)(2,1)} %pad_maximum_fusion.3), channel_id=1, source_target_pairs={{2,0},{4,2},{6,4},{8,6},{10,8},{12,10},{14,12},{16,14},{18,16},{20... | collective-permute-start | bytes 2359304 | tf_op jit(solution)/shard_map/ppermute | solution.py:29
  28.5 9.7 %collective-permute-start = (bf16[256,2,768]{0,2,1:T(8,128)(2,1)}, bf16[256,2,768]{0,2,1:T(8,128)(2,1)}, u32[]{:S(2)}, u32[]{:S(2)}) collective-permute-start(bf16[256,2,768]{0,2,1:T(8,128)(2,1)} %pad_maximum_fusion.3), channel_id=1, source_target_pairs={{0,2},{2,4},{4,6},{6,8},{8,10},{10,12},{12,14},{14,16},{16,18},{18... | collective-permute-start | bytes 2359304 | tf_op jit(solution)/shard_map/ppermute | solution.py:26
  38.2 2.0 copy-start.9
  40.0 3.3 copy-start.8
  40.0 3.3 copy-start.12
  40.2 3.1 copy-start.2
  40.2 4.5 %copy-start.4 = (bf16[768,1,768]{0,2,1:T(8,128)(2,1)}, bf16[768,1,768]{0,2,1:T(8,128)(2,1)S(1)}, u32[]{:S(2)}) copy-start(bf16[768,1,768]{0,2,1:T(8,128)(2,1)S(1)} %get-tuple-element.18) | copy-start | bytes 3538948
  44.8 2.2 copy-start.1
  69.7 23.6 %collective-permute-start.2 = (f32[256,2,768]{0,2,1:T(8,128)}, f32[256,2,768]{0,2,1:T(8,128)}, u32[]{:S(2)}, u32[]{:S(2)}) collective-permute-start(f32[256,2,768]{0,2,1:T(8,128)} %get-tuple-element.16), channel_id=1, source_target_pairs={{0,2},{2,4},{4,6},{6,8},{8,10},{10,12},{12,14},{14,16},{16,18},{18... | collective-permute-start | bytes 4718600 | tf_op jit(solution)/shard_map/ppermute | solution.py:18
  76.4 16.8 %collective-permute-start.3 = (f32[256,2,768]{0,2,1:T(8,128)}, f32[256,2,768]{0,2,1:T(8,128)}, u32[]{:S(2)}, u32[]{:S(2)}) collective-permute-start(f32[256,2,768]{0,2,1:T(8,128)} %get-tuple-element.17), channel_id=1, source_target_pairs={{2,0},{4,2},{6,4},{8,6},{10,8},{12,10},{14,12},{16,14},{18,16},{20... | collective-permute-start | bytes 4718600 | tf_op jit(solution)/shard_map/ppermute | solution.py:18
  93.2 2.8 copy-start.7
  114.8 172.9 %reduce-scatter.4.cloned.1.call-start = ((), (), s32[]{:S(2)}) async-start(), calls=%async_computation.3 | async-start | bytes 3145728 | tf_op jit(solution)/shard_map/reduce_scatter | solution.py:125
  114.9 131.7 %copy-start.3 = (bf16[768,1,768]{0,2,1:T(8,128)(2,1)S(1)}, bf16[768,1,768]{0,2,1:T(8,128)(2,1)}, u32[]{:S(2)}) copy-start(bf16[768,1,768]{0,2,1:T(8,128)(2,1)} %copy-done.2) | copy-start | bytes 3538948
  122.7 262.6 %reduce-scatter.8.cloned.1.call-start = ((), (), s32[]{:S(2)}) async-start(), calls=%async_computation.5 | async-start | bytes 2433024 | tf_op jit(solution)/shard_map/reduce_scatter | solution.py:145
Sparse Core Ops, SparseCore 0:
  115.0 131.5 reduce-scatter.5
  249.1 38.5 reduce-scatter.3
  292.1 93.1 reduce-scatter.7
where the time goes:
time: 394 us; the launch traced here: 393 us
  waiting for transfers between devices  256 us (65%)
  matrix products  60.7 us (15%)
  local copies, waits for them, and re-layouts  35 us (9%)
  other arithmetic  14.2 us (4%)
  between operations  14.1 us (4%)
  starting transfers between devices  13.6 us (3%)
    reduce_scatter x1, waiting for transfers between devices, local(): lax.psum_scatter(product.reshape(model_width // lax.axis_size('dp') * lax...  124 us
    reduce_scatter x1, waiting for transfers between devices, local(): lax.psum_scatter(clip_share, 'seq', scatter_dimension=0, tiled=True)  95.5 us
    reduce_scatter x1, waiting for transfers between devices, local(): lax.psum_scatter(lax.dot_general(d_qkv, flat_w, (((1,), (1,)), ((), ())),...  36.4 us
    unnamed x29, local copies, waits for them, and re-layouts  18.3 us
    dot_general x1, matrix products, local(): jnp.einsum('hqk,qhe->khe', d_scores, q_hat, preferred_element_type=jnp.fl...  16.3 us
    dot_general x1, matrix products, local(): jnp.einsum('hqk,khe->qhe', d_scores, keys_wide, preferred_element_type=jn...  15.3 us
    convert_element_type x1, local copies, waits for them, and re-layouts, local(): clip_share = lax.psum_scatter(product.reshape(model_width // lax.axis_siz...  12.7 us
    ppermute x2, starting transfers between devices, shifted(): lax.ppermute(value, axis, [(source, source + steps) for source in range(i...  8.24 us
  transfers between devices with their start and end apart: 7, of which 3 were waited for; matrix products, arithmetic and copies ran while one was open for 9% of the time, Pallas kernels for 0%

commit v1 on v0

v1 whole, which is shorter than its diff:
```python
import functools
import math

import jax
import jax.numpy as jnp
from jax import lax
from jax.experimental import pallas as pl
from jax.experimental.pallas import tpu as pltpu
from jax.sharding import PartitionSpec as P

HD = 128
TILE = 64
EPS = 1e-06
F32 = jnp.float32
BF16 = jnp.bfloat16
AXES = ("dp", "seq", "head")
SCALE = 1.0 / math.sqrt(HD)
EXP2_SCALE = SCALE * math.log2(math.e)
VMEM_LIMIT = 48 * 1024 * 1024


def permute(value, target):
    pairs = []
    for x in range(4):
        for seq in range(32):
            for head in range(2):
                place = target(x, seq // 8, (seq // 2) % 4, seq % 2, head)
                if place is None:
                    continue
                x2, zh2, y2, c2, h2 = place
                pairs.append(
                    (x * 64 + seq * 2 + head, x2 * 64 + (zh2 * 8 + y2 * 2 + c2) * 2 + h2)
                )
    return lax.ppermute(value, AXES, pairs)


def to_slab(step):
    def target(x, zh, y, c, h):
        seq = zh * 8 + y * 2 + c + step
        if not 0 <= seq < 32:
            return None
        return (x, seq // 8, (seq // 2) % 4, seq % 2, h)

    return target


def to_x(step):
    return lambda x, zh, y, c, h: ((x + step) % 4, zh, y, c, h)


def to_y(step):
    return lambda x, zh, y, c, h: (x, zh, (y + step) % 4, c, h)


def to_z(step):
    return lambda x, zh, y, c, h: (x, (zh + step) % 4, y, c, h)


def flip(x_bits=0, y_bits=0, core=0, head=0):
    return lambda x, zh, y, c, h: (x ^ x_bits, zh, y ^ y_bits, c ^ core, h ^ head)


def params(**more):
    return pltpu.CompilerParams(vmem_limit_bytes=VMEM_LIMIT, **more)


def cost(flops, moved, trans=0):
    return pl.CostEstimate(flops=flops, bytes_accessed=moved, transcendentals=trans)


def dot(a, b, dims):
    return lax.dot_general(a, b, (dims, ((), ())), preferred_element_type=F32)


NN = ((1,), (0,))
NT = ((1,), (1,))


def inv_rms(values):
    return lax.rsqrt(jnp.mean(values * values, axis=-1, keepdims=True) + EPS)


def project_kv_kernel(x_ref, wk_ref, wv_ref, gain_ref, kv_ref, raw_ref):
    x = x_ref[...]
    raw = dot(x, wk_ref[0], NN)
    raw_ref[...] = raw
    for i in range(raw.shape[1] // HD):
        part = raw[:, i * HD : (i + 1) * HD]
        kv_ref[0, :, i * HD : (i + 1) * HD] = (part * inv_rms(part) * gain_ref[...]).astype(BF16)
    kv_ref[1] = dot(x, wv_ref[0], NN).astype(BF16)


def project_kv(x, w, gain):
    rows, width = x.shape
    cols = w.shape[2]
    block = 2 * HD
    return pl.pallas_call(
        project_kv_kernel,
        grid=(cols // block,),
        in_specs=[
            pl.BlockSpec((rows, width), lambda i: (0, 0)),
            pl.BlockSpec((1, width, block), lambda i: (1, 0, i)),
            pl.BlockSpec((1, width, block), lambda i: (2, 0, i)),
            pl.BlockSpec((1, HD), lambda i: (0, 0)),
        ],
        out_specs=[
            pl.BlockSpec((2, rows, block), lambda i: (0, 0, i)),
            pl.BlockSpec((rows, block), lambda i: (0, i)),
        ],
        out_shape=[
            jax.ShapeDtypeStruct((2, rows, cols), BF16),
            jax.ShapeDtypeStruct((rows, cols), F32),
        ],
        compiler_params=params(),
        cost_estimate=cost(4 * rows * width * cols, 4 * width * cols),
        name="project_kv",
    )(x, w, w, gain)


def project_q_kernel(x_ref, w_ref, gain_ref, q_ref, raw_ref):
    raw = dot(x_ref[...], w_ref[0], NN)
    raw_ref[...] = raw
    for i in range(raw.shape[1] // HD):
        part = raw[:, i * HD : (i + 1) * HD]
        q_ref[:, i * HD : (i + 1) * HD] = (part * inv_rms(part) * gain_ref[...]).astype(BF16)


def project_q(x, w, gain):
    rows, width = x.shape
    cols = w.shape[2]
    block = 2 * HD
    return pl.pallas_call(
        project_q_kernel,
        grid=(cols // block,),
        in_specs=[
            pl.BlockSpec((rows, width), lambda i: (0, 0)),
            pl.BlockSpec((1, width, block), lambda i: (0, 0, i)),
            pl.BlockSpec((1, HD), lambda i: (0, 0)),
        ],
        out_specs=[
            pl.BlockSpec((rows, block), lambda i: (0, i)),
            pl.BlockSpec((rows, block), lambda i: (0, i)),
        ],
        out_shape=[
            jax.ShapeDtypeStruct((rows, cols), BF16),
            jax.ShapeDtypeStruct((rows, cols), F32),
        ],
        compiler_params=params(),
        cost_estimate=cost(2 * rows * width * cols, 2 * width * cols),
        name="project_q",
    )(x, w, gain)


def spread_rows_kernel(place_ref, x_ref, core_ref, a0_ref, a1_ref, b0_ref, b1_ref, own_ref, xt_ref):
    xt_ref[...] = x_ref[...].T
    x = place_ref[0]
    zh = place_ref[1]
    y = place_ref[2]
    c = place_ref[3]

    def source(xx, zz, yy, cc):
        return xt_ref[pl.ds(pl.multiple_of((((xx * 4 + zz) * 4 + yy) * 2 + cc) * 16, 16), 16), :]

    flips = (0, 3, 1, 2)
    for k in range(4):
        for s in range(4):
            for m in range(4):
                zz = lax.rem(zh + m, 4)
                ya, xa = lax.rem(y + k, 4), x ^ flips[s]
                xb, yb = lax.rem(x + k, 4), y ^ flips[s]
                row = ((k * 2 + s % 2) * 4 + m) * 16
                rows = slice(row, row + 16)
                same_a, other_a = source(xa, zz, ya, c), source(xa, zz, ya, 1 - c)
                same_b, other_b = source(xb, zz, yb, c), source(xb, zz, yb, 1 - c)
                if s < 2:
                    own_ref[0, rows, :] = same_a
                    own_ref[1, rows, :] = same_b
                    core_ref[0, rows, :] = other_a
                    core_ref[1, rows, :] = other_b
                else:
                    a0_ref[rows, :] = same_a
                    a1_ref[rows, :] = other_a
                    b0_ref[rows, :] = same_b
                    b1_ref[rows, :] = other_b


def spread_rows(x, place):
    tokens, width = x.shape
    rows = width // 4
    one = jax.ShapeDtypeStruct((rows, tokens), BF16)
    two = jax.ShapeDtypeStruct((2, rows, tokens), BF16)
    vmem = pl.BlockSpec(memory_space=pltpu.VMEM)
    return pl.pallas_call(
        spread_rows_kernel,
        in_specs=[pl.BlockSpec(memory_space=pltpu.SMEM), vmem],
        out_specs=[vmem] * 6,
        out_shape=[two, one, one, one, one, two],
        scratch_shapes=[pltpu.VMEM((width, tokens), BF16)],
        compiler_params=params(),
        cost_estimate=cost(0, 6 * tokens * width),
        name="spread_rows",
    )(place, x)


def norm_back(raw, gain, upstream):
    inverse = inv_rms(raw)
    normed = raw * inverse
    weighted = upstream * gain
    return inverse * (weighted - normed * jnp.mean(weighted * normed, axis=-1, keepdims=True))


def fill_mask(mask_ref, first, full_ref):
    for i in range(4):
        full_ref[i * TILE : (i + 1) * TILE, :] = jnp.broadcast_to(
            mask_ref[first + i : first + i + 1, :], (TILE, full_ref.shape[1])
        )


def queries_kernel(
    mask_ref, q_ref, raw_ref, gain_ref, g_ref, low_ref, own_ref, high_ref,
    out_ref, dq_ref, stats_ref, full_ref,
):
    @pl.when(pl.program_id(0) == 0)
    def _():
        fill_mask(mask_ref, 0, full_ref)

    for i in range(q_ref.shape[1] // HD):
        cols = slice(i * HD, (i + 1) * HD)
        q = q_ref[:, cols]
        g = g_ref[:, cols]
        keys = jnp.concatenate([low_ref[0, :, cols], own_ref[0, :, cols], high_ref[0, :, cols]], 0)
        values = jnp.concatenate([low_ref[1, :, cols], own_ref[1, :, cols], high_ref[1, :, cols]], 0)
        expo = jnp.exp2(dot(q, keys, NT) * EXP2_SCALE) * full_ref[...]
        inverse = 1.0 / jnp.sum(expo, axis=-1, keepdims=True)
        probs = expo * inverse
        out_ref[:, cols] = dot(probs.astype(BF16), values, NN).astype(BF16)
        d_probs = dot(g, values, NT)
        delta = jnp.sum(probs * d_probs, axis=-1, keepdims=True)
        d_scores = (probs * ((d_probs - delta) * SCALE)).astype(BF16)
        d_qhat = dot(d_scores, keys, NN)
        dq_ref[:, cols] = norm_back(raw_ref[:, cols], gain_ref[...], d_qhat).astype(BF16)
        lane = lax.broadcasted_iota(jnp.int32, (q.shape[0], HD), 1)
        both = jnp.where(lane == 0, inverse, jnp.where(lane == 1, delta, 0.0))
        stats_ref[i] = both.T[:8, :]


def queries(mask, q_hat, q_raw, gain, g, low, own, high):
    rows, cols = q_hat.shape
    block = 2 * HD
    flat = pl.BlockSpec((rows, block), lambda i: (0, i))
    pair = pl.BlockSpec((2, rows, block), lambda i: (0, 0, i))
    return pl.pallas_call(
        queries_kernel,
        grid=(cols // block,),
        in_specs=[
            pl.BlockSpec((8, 3 * rows), lambda i: (0, 0)),
            flat,
            flat,
            pl.BlockSpec((1, HD), lambda i: (0, 0)),
            flat,
            pair,
            pair,
            pair,
        ],
        out_specs=[flat, flat, pl.BlockSpec((2, 8, rows), lambda i: (i, 0, 0))],
        out_shape=[
            jax.ShapeDtypeStruct((rows, cols), BF16),
            jax.ShapeDtypeStruct((rows, cols), BF16),
            jax.ShapeDtypeStruct((cols // HD, 8, rows), F32),
        ],
        scratch_shapes=[pltpu.VMEM((rows, 3 * rows), F32)],
        compiler_params=params(),
        cost_estimate=cost(24 * rows * rows * cols, 20 * rows * cols, 3 * rows * rows * cols // HD),
        name="queries",
    )(mask, q_hat, q_raw, gain, g, low, own, high)


def keys_kernel(
    mask_ref, kv_ref, raw_ref, gain_ref, ql_ref, qo_ref, qh_ref, gl_ref, go_ref, gh_ref,
    sl_ref, so_ref, sh_ref, dq_ref, da_ref, db_ref, full_ref,
):
    step = pl.program_id(0)
    heads = qo_ref.shape[1] // HD
    half = 3 * HD

    @pl.when(step == 0)
    def _():
        fill_mask(mask_ref, 4, full_ref)
        da_ref[:, :half] = dq_ref[:, :half]
        db_ref[:, :half] = dq_ref[:, half:]

    for i in range(heads):
        cols = slice(i * HD, (i + 1) * HD)
        key = kv_ref[0, :, cols]
        value = kv_ref[1, :, cols]
        q_wide = jnp.concatenate([ql_ref[:, cols], qo_ref[:, cols], qh_ref[:, cols]], 0)
        g_wide = jnp.concatenate([gl_ref[:, cols], go_ref[:, cols], gh_ref[:, cols]], 0)
        stats = jnp.concatenate([sl_ref[i], so_ref[i], sh_ref[i]], axis=1)
        probs = jnp.exp2(dot(key, q_wide, NT) * EXP2_SCALE) * full_ref[...] * stats[0:1, :]
        d_value = dot(probs.astype(BF16), g_wide, NN)
        d_probs = dot(value, g_wide, NT)
        d_scores = (probs * ((d_probs - stats[1:2, :]) * SCALE)).astype(BF16)
        d_khat = dot(d_scores, q_wide, NN)
        at = pl.ds(pl.multiple_of(half + (step * heads + i) * HD, HD), HD)
        da_ref[:, at] = norm_back(raw_ref[:, cols], gain_ref[...], d_khat).astype(BF16)
        db_ref[:, at] = d_value.astype(BF16)


def keys(mask, kv, k_raw, gain, q3, g3, s3, dq):
    rows, cols = k_raw.shape
    block = 2 * HD
    flat = pl.BlockSpec((rows, block), lambda i: (0, i))
    stats = pl.BlockSpec((2, 8, rows), lambda i: (i, 0, 0))
    wide = pl.BlockSpec((rows, cols * 3 // 2), lambda i: (0, 0))
    return pl.pallas_call(
        keys_kernel,
        grid=(cols // block,),
        in_specs=[
            pl.BlockSpec((8, 3 * rows), lambda i: (0, 0)),
            pl.BlockSpec((2, rows, block), lambda i: (0, 0, i)),
            flat,
            pl.BlockSpec((1, HD), lambda i: (0, 0)),
            *[flat] * 6,
            *[stats] * 3,
            pl.BlockSpec((rows, cols), lambda i: (0, 0)),
        ],
        out_specs=[wide, wide],
        out_shape=[jax.ShapeDtypeStruct((rows, cols * 3 // 2), BF16)] * 2,
        scratch_shapes=[pltpu.VMEM((rows, 3 * rows), F32)],
        compiler_params=params(),
        cost_estimate=cost(24 * rows * rows * cols, 24 * rows * cols, 3 * rows * rows * cols // HD),
        name="keys",
    )(mask, kv, k_raw, gain, *q3, *g3, *s3, dq)


def input_grad_kernel(place_ref, da_ref, db_ref, w_ref, keep_ref, send_ref, acc_ref):
    half = da_ref.shape[1] // 3
    total = dot(da_ref[:, :half], w_ref[0, :, :half], NT)
    total += dot(db_ref[:, :half], w_ref[0, :, half:], NT)
    total += dot(da_ref[:, half:], w_ref[1], NT)
    total += dot(db_ref[:, half:], w_ref[2], NT)
    acc_ref[...] = total
    rows = keep_ref.shape[0]
    head = place_ref[4]
    keep_ref[...] = acc_ref[pl.ds(pl.multiple_of(head * rows, rows), rows), :]
    send_ref[...] = acc_ref[pl.ds(pl.multiple_of((1 - head) * rows, rows), rows), :].astype(BF16)


def input_grad(place, da, db, w):
    rows = da.shape[0]
    _, width, cols = w.shape
    block = 256
    whole = pl.BlockSpec(da.shape, lambda i: (0, 0))
    half = pl.BlockSpec((rows // 2, block), lambda i: (0, i))
    return pl.pallas_call(
        input_grad_kernel,
        grid=(width // block,),
        in_specs=[
            pl.BlockSpec(memory_space=pltpu.SMEM),
            whole,
            whole,
            pl.BlockSpec((3, block, cols), lambda i: (0, i, 0)),
        ],
        out_specs=[half, half],
        out_shape=[
            jax.ShapeDtypeStruct((rows // 2, width), F32),
            jax.ShapeDtypeStruct((rows // 2, width), BF16),
        ],
        scratch_shapes=[pltpu.VMEM((rows, block), F32)],
        compiler_params=params(),
        cost_estimate=cost(6 * rows * width * cols, 6 * width * cols),
        name="input_grad",
    )(place, da, db, w)


def weight_grad_kernel(*refs):
    lhs, rhs, outs = refs[:4], refs[4:8], refs[8:]
    for k in range(4):
        rows = slice(k * 128, (k + 1) * 128)
        total = None
        for left, right in zip(lhs, rhs):
            term = dot(left[rows, :] if len(left.shape) == 2 else left[0, rows, :],
                       right[...], NN)
            total = term if total is None else total + term
        outs[k][...] = total.astype(BF16)


def weight_grad(half, lhs, rhs):
    tokens, cols = rhs[0].shape
    block = 384
    specs = []
    for left in lhs:
        if left.ndim == 3:
            specs.append(pl.BlockSpec((1, *left.shape[1:]), lambda i: (half, 0, 0)))
        else:
            specs.append(pl.BlockSpec(left.shape, lambda i: (0, 0)))
    specs += [pl.BlockSpec((tokens, block), lambda i: (0, i))] * 4
    return pl.pallas_call(
        weight_grad_kernel,
        grid=(cols // block,),
        in_specs=specs,
        out_specs=[pl.BlockSpec((128, block), lambda i: (0, i))] * 4,
        out_shape=[jax.ShapeDtypeStruct((128, cols), BF16)] * 4,
        compiler_params=params(),
        cost_estimate=cost(8 * 512 * tokens * cols, 4 * 512 * cols + 8 * tokens * cols),
        name="weight_grad",
    )(*lhs, *rhs)


def tile_masks(neighbours, seq):
    tiles = neighbours.shape[0]
    padded = jnp.pad(neighbours, ((4, 4), (0, 0)), constant_values=-1)
    window = lax.dynamic_slice_in_dim(padded, seq * 4, 12, 0)
    own = seq * 4 + jnp.arange(4, dtype=jnp.int32)
    near = seq * 4 - 4 + jnp.arange(12, dtype=jnp.int32)
    by_query = jnp.any(window[4:8, :, None] == near[None, None, :], axis=1)
    by_query = by_query & ((near >= 0) & (near < tiles))[None, :]
    by_key = jnp.any(window[None, :, :] == own[:, None, None], axis=2)
    both = jnp.concatenate([by_query, by_key], axis=0).astype(F32)
    return jnp.repeat(both, TILE, axis=1)


def reduce4(own, others):
    total = own.astype(F32)
    for other in others:
        total = total + other.astype(F32)
    return total


def local(latents, w_qkv, q_gain, k_gain, neighbours, grad_out):
    x = latents[0]
    g = grad_out[0]
    w = jnp.transpose(w_qkv, (1, 0, 2))
    dp = lax.axis_index("dp")
    seq = lax.axis_index("seq")
    head = lax.axis_index("head")
    place = jnp.stack([dp, seq // 8, (seq // 2) % 4, seq % 2, head]).astype(jnp.int32)
    q_gain = q_gain.reshape(1, HD)
    k_gain = k_gain.reshape(1, HD)

    g_low = permute(g, to_slab(1))
    g_high = permute(g, to_slab(-1))
    kv, k_raw = project_kv(x, w, k_gain)
    kv_low = permute(kv, to_slab(1))
    kv_high = permute(kv, to_slab(-1))
    q_hat, q_raw = project_q(x, w, q_gain)
    q_low = permute(q_hat, to_slab(1))
    q_high = permute(q_hat, to_slab(-1))

    to_core, to_a0, to_a1, to_b0, to_b1, own_rows = spread_rows(x, place)
    core_rows = permute(to_core, flip(core=1))
    a0 = permute(to_a0, flip(x_bits=1))
    a1 = permute(to_a1, flip(x_bits=1, core=1))
    b0 = permute(to_b0, flip(y_bits=1))
    b1 = permute(to_b1, flip(y_bits=1, core=1))

    mask = tile_masks(neighbours, seq)
    attn_out, dq, stats = queries(mask, q_hat, q_raw, q_gain, g, kv_low, kv, kv_high)
    s_low = permute(stats, to_slab(1))
    s_high = permute(stats, to_slab(-1))
    da, db = keys(
        mask, kv, k_raw, k_gain, (q_low, q_hat, q_high), (g_low, g, g_high),
        (s_low, stats, s_high), dq,
    )

    dax = permute(da, flip(x_bits=1))
    dby = permute(db, flip(y_bits=1))
    dac = permute(da, flip(core=1))
    dbc = permute(db, flip(core=1))
    keep, send = input_grad(place, da, db, w)
    got = permute(send, flip(head=1))
    daxc = permute(dax, flip(core=1))
    dbyc = permute(dby, flip(core=1))

    pa = weight_grad(0, (own_rows, core_rows, a0, a1), (da, dac, dax, daxc))
    pb = weight_grad(1, (own_rows, core_rows, b0, b1), (db, dbc, dby, dbyc))
    ra = [permute(pa[k], to_y(k)) for k in (1, 3, 2)]
    rb = [permute(pb[k], to_x(k)) for k in (1, 3, 2)]
    sa = reduce4(pa[0], ra)
    sb = reduce4(pb[0], rb)
    ca = permute(sa[64:].astype(BF16), flip(x_bits=3))
    cb = permute(sb[64:].astype(BF16), flip(y_bits=3))
    ta = sa[:64] + ca.astype(F32)
    tb = sb[:64] + cb.astype(F32)
    both = jnp.concatenate([ta, tb], axis=1).reshape(4, 16, -1).astype(BF16)
    rz = [permute(both[m], to_z(m)) for m in (1, 3, 2)]
    total = reduce4(both[0], rz)
    part = total.shape[1] // 6
    grad_w = jnp.stack(
        [
            jnp.concatenate([total[:, :part], total[:, 3 * part : 4 * part]], axis=1),
            total[:, part : 3 * part],
            total[:, 4 * part :],
        ],
        axis=0,
    )
    grad_x = (keep + got.astype(F32)).astype(BF16)
    return (attn_out[None], grad_x[None], jnp.transpose(grad_w, (1, 0, 2)))


def solution(mesh):
    in_specs = (P("dp", "seq", None), P(None, None, "head"), P(), P(), P(), P("dp", "seq", "head"))
    out_specs = (
        P("dp", "seq", "head"),
        P("dp", ("seq", "head"), None),
        P(("dp", "seq"), None, "head"),
    )
    return jax.shard_map(local, mesh=mesh, in_specs=in_specs, out_specs=out_specs, check_vma=False)
```

time: 394 us -> 164 us (0.42)
  waiting for transfers between devices: 256 us -> 49.5 us
  matrix products: 60.7 us -> 0 us
  starting transfers between devices: 13.6 us -> 65.6 us
  Pallas kernels: 0 us -> 37.2 us
  local copies, waits for them, and re-layouts: 35 us -> 6.37 us
  between operations: 14.1 us -> 0.97 us
  other arithmetic: 14.2 us -> 2.2 us
    reduce_scatter x3 -> x0, waiting for transfers between devices: 256 us -> none  [the longest x1 124 us: local(): lax.psum_scatter(product.reshape(model_width // lax.axis_size('dp') * lax...]
    dot_general x9 -> x0, matrix products: 60.7 us -> none  [the longest x1 16.3 us: local(): jnp.einsum('hqk,qhe->khe', d_scores, q_hat, preferred_element_type=jnp.fl...]
    ppermute x4 -> x31, starting transfers between devices: 13.5 us -> 65.6 us  [permute(): return lax.ppermute(value, AXES, pairs)]
    ppermute x4 -> x31, waiting for transfers between devices: 0.01 us -> 49.5 us  [permute(): return lax.ppermute(value, AXES, pairs)]
    pallas_call x0 -> x8, Pallas kernels: none -> 37.2 us  [the longest x1 8.34 us: input_grad(): pl.pallas_call(input_grad_kernel, grid=(width // block,), in_specs=[pl.Bl...]
    convert_element_type x1 -> x0, local copies, waits for them, and re-layouts: 12.7 us -> none  [local(): clip_share = lax.psum_scatter(product.reshape(model_width // lax.axis_siz...]
    unnamed x29 -> x24, local copies, waits for them, and re-layouts: 18.3 us -> 5.92 us
    another operation x5 -> x3, other arithmetic: 5.18 us -> 0.06 us  [the longest x1 3.72 us: local(): jnp.stack([d_kwide.reshape(3 * slab_rows, head_width), d_vwide.reshape(3...]
  transfers between devices with their start and end apart: 7 -> 31, of which waited for: 3 -> 12; matrix products, arithmetic and copies ran while one was open for 9% -> 1% of each run, Pallas kernels for 0% -> 16%
where the time goes in v1:
time: 164 us; the launch traced here: 162 us
  starting transfers between devices  65.6 us (40%)
  waiting for transfers between devices  49.5 us (30%)
  Pallas kernels  37.2 us (23%)
  local copies, waits for them, and re-layouts  6.37 us (4%)
  other arithmetic  2.2 us (1%)
    ppermute x31, starting transfers between devices, permute(): return lax.ppermute(value, AXES, pairs)  65.6 us
    ppermute x31, waiting for transfers between devices, permute(): return lax.ppermute(value, AXES, pairs)  49.5 us
    pallas_call x1, Pallas kernels, input_grad(): pl.pallas_call(input_grad_kernel, grid=(width // block,), in_specs=[pl.Bl...  8.34 us
    pallas_call x1, Pallas kernels, queries(): pl.pallas_call(queries_kernel, grid=(cols // block,), in_specs=[pl.BlockS...  7.45 us
    unnamed x24, local copies, waits for them, and re-layouts  5.92 us
    pallas_call x2, Pallas kernels, weight_grad(): pl.pallas_call(weight_grad_kernel, grid=(cols // block,), in_specs=specs,...  5.91 us
    pallas_call x1, Pallas kernels, keys(): pl.pallas_call(keys_kernel, grid=(cols // block,), in_specs=[pl.BlockSpec...  5.74 us
    pallas_call x1, Pallas kernels, project_kv(): pl.pallas_call(project_kv_kernel, grid=(cols // block,), in_specs=[pl.Blo...  4.81 us
  transfers between devices with their start and end apart: 31, of which 12 were waited for; matrix products, arithmetic and copies ran while one was open for 1% of the time, Pallas kernels for 16%

profile of v1, /device:TPU:6, one launch (start us, length us, event | category | flops | bytes accessed | tf_op | source)
XLA Modules:
  0.0 161.9 jit_solution(18049138428558086068)
XLA Ops:
  0.6 1.2 copy-done
  1.9 0.7 copy-done.6
  2.5 4.8 %project_kv.1 = (bf16[2,256,768]{2,1,0:T(8,128)(2,1)S(1)}, f32[256,768]{1,0:T(8,128)S(1)}) custom-call(bf16[256,2048]{1,0:T(8,128)(2,1)S(1)} %bitcast.21, bf16[3,2048,768]{2,1,0:T(8,128)(2,1)} %bitcast.32, bf16[3,2048,768]{2,1,0:T(8,128)(2,1)} %bitcast.33, f32[1,128]{1,0:T(1,128)S(1)} %bitcast.28), custom_call_target="tpu_custom_call" | custom-call | flops 1610612736 | bytes 6291456 | tf_op jit(solution)/shard_map/project_kv/pallas_call | solution.py:97
  7.4 2.8 %collective-permute-start = (bf16[2,256,768]{2,1,0:T(8,128)(2,1)S(1)}, bf16[2,256,768]{2,1,0:T(8,128)(2,1)}, u32[]{:S(2)}, u32[]{:S(2)}) collective-permute-start(bf16[2,256,768]{2,1,0:T(8,128)(2,1)S(1)} %get-tuple-element.30.own_ref.kv_ref), channel_id=1, source_target_pairs={{0,2},{1,3},{2,4},{3,5},{4,6},{5,7},{6,8},{7,9},{8,10},{9,11},{10,... | collective-permute-start | bytes 2359304 | tf_op jit(solution)/shard_map/ppermute | solution.py:34
  10.1 1.3 collective-permute-start.1
  11.5 3.7 %project_q.1 = (bf16[256,768]{1,0:T(8,128)(2,1)S(1)}, f32[256,768]{1,0:T(8,128)S(1)}) custom-call(bf16[256,2048]{1,0:T(8,128)(2,1)S(1)} %bitcast.22, bf16[3,2048,768]{2,1,0:T(8,128)(2,1)} %bitcast.34, f32[1,128]{1,0:T(1,128)S(1)} %bitcast.30), custom_call_target="tpu_custom_call" | custom-call | flops 805306368 | bytes 3145728 | tf_op jit(solution)/shard_map/project_q/pallas_call | solution.py:132
  15.2 0.9 copy-done.9
  16.0 4.3 %collective-permute-start.2 = (bf16[256,768]{1,0:T(8,128)(2,1)S(1)}, bf16[256,768]{1,0:T(8,128)(2,1)}, u32[]{:S(2)}, u32[]{:S(2)}) collective-permute-start(bf16[256,768]{1,0:T(8,128)(2,1)S(1)} %get-tuple-element.28.q_ref.qo_ref), channel_id=1, source_target_pairs={{0,2},{1,3},{2,4},{3,5},{4,6},{5,7},{6,8},{7,9},{8,10},{9,11},{10,... | collective-permute-start | bytes 1179656 | tf_op jit(solution)/shard_map/ppermute | solution.py:34
  20.3 1.3 collective-permute-start.3
  21.6 4.3 %collective-permute-start.4 = (bf16[256,768]{1,0:T(8,128)(2,1)S(1)}, bf16[256,768]{1,0:T(8,128)(2,1)}, u32[]{:S(2)}, u32[]{:S(2)}) collective-permute-start(bf16[256,768]{1,0:T(8,128)(2,1)S(1)} %bitcast.24), channel_id=1, source_target_pairs={{0,2},{1,3},{2,4},{3,5},{4,6},{5,7},{6,8},{7,9},{8,10},{9,11},{10,... | collective-permute-start | bytes 1179656 | tf_op jit(solution)/shard_map/ppermute | solution.py:34
  25.9 0.1 pad_dynamic-slice_fusion.1
  26.0 0.1 compare_reduce_fusion.1
  26.2 1.3 collective-permute-start.5
  27.5 0.1 compare_reduce_fusion
  27.7 0.1 reshape.44.mask_ref
  27.7 1.1 copy-done.10
  28.9 7.4 %queries.1 = (bf16[256,768]{1,0:T(8,128)(2,1)}, bf16[256,768]{1,0:T(8,128)(2,1)S(1)}, f32[6,8,256]{2,1,0:T(8,128)S(1)}) custom-call(f32[8,768]{1,0:T(8,128)S(1)} %reshape.44.mask_ref, bf16[256,768]{1,0:T(8,128)(2,1)S(1)} %get-tuple-element.28.q_ref.qo_ref, f32[256,768]{1,0:T(8,128)S(1)} %copy-done.10, f32[1,128]{1,0:T(1,128)S(1)} %bitcast.31, ...), custom_call_target="tpu_custom_call" | custom-call | flops 1207959552 | bytes 3932160 | tf_op jit(solution)/shard_map/queries/pallas_call | solution.py:252
  36.3 3.6 %collective-permute-start.6 = (f32[6,8,256]{2,1,0:T(8,128)S(1)}, f32[6,8,256]{2,1,0:T(8,128)S(1)}, u32[]{:S(2)}, u32[]{:S(2)}) collective-permute-start(f32[6,8,256]{2,1,0:T(8,128)S(1)} %get-tuple-element.33.so_ref), channel_id=1, source_target_pairs={{0,2},{1,3},{2,4},{3,5},{4,6},{5,7},{6,8},{7,9},{8,10},{9,11},{10,... | collective-permute-start | bytes 147464 | tf_op jit(solution)/shard_map/ppermute | solution.py:34
  39.9 1.3 collective-permute-start.7
  41.3 3.0 %collective-permute-done.7.sh_ref = f32[6,8,256]{2,1,0:T(8,128)S(1)} collective-permute-done((f32[6,8,256]{2,1,0:T(8,128)S(1)}, f32[6,8,256]{2,1,0:T(8,128)S(1)}, u32[]{:S(2)}, u32[]{:S(2)}) %collective-permute-start.7) | collective-permute-done | bytes 49184 | tf_op jit(solution)/shard_map/ppermute | solution.py:34
  44.3 1.0 copy-done.3
  45.3 1.0 copy-done.5
  46.3 5.7 %keys.1 = (bf16[256,1152]{1,0:T(8,128)(2,1)S(1)}, bf16[256,1152]{1,0:T(8,128)(2,1)}) custom-call(f32[8,768]{1,0:T(8,128)S(1)} %reshape.44.mask_ref, bf16[2,256,768]{2,1,0:T(8,128)(2,1)S(1)} %get-tuple-element.30.own_ref.kv_ref, f32[256,768]{1,0:T(8,128)S(1)} %get-tuple-element.32.raw_ref, f32[1,128]{1,0:T(1,128)S(1)} %bitcast.29, ...), custom_call_target="tpu_custom_call" | custom-call | flops 1207959552 | bytes 4718592 | tf_op jit(solution)/shard_map/keys/pallas_call | solution.py:315
  52.0 2.6 %collective-permute-start.22 = (bf16[256,1152]{1,0:T(8,128)(2,1)}, bf16[256,1152]{1,0:T(8,128)(2,1)S(1)}, u32[]{:S(2)}, u32[]{:S(2)}) collective-permute-start(bf16[256,1152]{1,0:T(8,128)(2,1)} %get-tuple-element.36.db_ref.refs_4_), channel_id=1, source_target_pairs={{0,4},{1,5},{2,6},{3,7},{4,0},{5,1},{6,2},{7,3},{8,12},{9,13},{10,... | collective-permute-start | bytes 1769480 | tf_op jit(solution)/shard_map/ppermute | solution.py:34
  54.6 0.8 collective-permute-start.13
  55.5 0.1 stack.35.place_ref
  55.6 1.3 spread_rows.1
  56.8 0.1 collective-permute-start.19
  56.9 1.3 collective-permute-start.21
  58.3 9.7 %collective-permute-done.22.refs_6_ = bf16[256,1152]{1,0:T(8,128)(2,1)S(1)} collective-permute-done((bf16[256,1152]{1,0:T(8,128)(2,1)}, bf16[256,1152]{1,0:T(8,128)(2,1)S(1)}, u32[]{:S(2)}, u32[]{:S(2)}) %collective-permute-start.22) | collective-permute-done | bytes 589856 | tf_op jit(solution)/shard_map/ppermute | solution.py:34
  68.0 2.4 %collective-permute-start.23 = (bf16[256,1152]{1,0:T(8,128)(2,1)S(1)}, bf16[256,1152]{1,0:T(8,128)(2,1)S(1)}, u32[]{:S(2)}, u32[]{:S(2)}) collective-permute-start(bf16[256,1152]{1,0:T(8,128)(2,1)S(1)} %collective-permute-done.22.refs_6_), channel_id=1, source_target_pairs={{0,2},{1,3},{2,0},{3,1},{4,6},{5,7},{6,4},{7,5},{8,10},{9,11},{10,... | collective-permute-start | bytes 1769480 | tf_op jit(solution)/shard_map/ppermute | solution.py:34
  70.4 3.1 %collective-permute-done.19.refs_2_ = bf16[512,256]{1,0:T(8,128)(2,1)S(1)} collective-permute-done((bf16[512,256]{1,0:T(8,128)(2,1)S(1)}, bf16[512,256]{1,0:T(8,128)(2,1)S(1)}, u32[]{:S(2)}, u32[]{:S(2)}) %collective-permute-start.19) | collective-permute-done | bytes 262176 | tf_op jit(solution)/shard_map/ppermute | solution.py:34
  73.5 2.6 %collective-permute-start.20 = (bf16[512,256]{1,0:T(8,128)(2,1)S(1)}, bf16[512,256]{1,0:T(8,128)(2,1)S(1)}, u32[]{:S(2)}, u32[]{:S(2)}) collective-permute-start(bf16[512,256]{1,0:T(8,128)(2,1)S(1)} %get-tuple-element.48), channel_id=1, source_target_pairs={{0,6},{1,7},{2,4},{3,5},{4,2},{5,3},{6,0},{7,1},{8,14},{9,15},{10,... | collective-permute-start | bytes 786440 | tf_op jit(solution)/shard_map/ppermute | solution.py:34
  76.1 6.6 %collective-permute-done.20.refs_3_ = bf16[512,256]{1,0:T(8,128)(2,1)S(1)} collective-permute-done((bf16[512,256]{1,0:T(8,128)(2,1)S(1)}, bf16[512,256]{1,0:T(8,128)(2,1)S(1)}, u32[]{:S(2)}, u32[]{:S(2)}) %collective-permute-start.20) | collective-permute-done | bytes 262176 | tf_op jit(solution)/shard_map/ppermute | solution.py:34
  82.7 0.1 collective-permute-start.12
  82.8 0.4 collective-permute-start.14
  83.2 0.8 collective-permute-start.10
  84.0 0.6 collective-permute-start.11
  84.7 3.4 %weight_grad.3 = (bf16[128,1152]{1,0:T(8,128)(2,1)S(1)}, bf16[128,1152]{1,0:T(8,128)(2,1)S(1)}, bf16[128,1152]{1,0:T(8,128)(2,1)S(1)}, bf16[128,1152]{1,0:T(8,128)(2,1)S(1)}) custom-call(bf16[2,512,256]{2,1,0:T(8,128)(2,1)S(1)} %get-tuple-element.39.refs_0_, bf16[2,512,256]{2,1,0:T(8,128)(2,1)S(1)} %collective-permute-done.9.refs_1_, ...), custom_call_target="tpu_custom_call" | custom-call | flops 1207959552 | bytes 4718592 | tf_op jit(solution)/shard_map/weight_grad/pallas_call | solution.py:398
  88.0 0.7 collective-permute-start.24
  88.7 3.6 %collective-permute-done.10.refs_2_ = bf16[512,256]{1,0:T(8,128)(2,1)S(1)} collective-permute-done((bf16[512,256]{1,0:T(8,128)(2,1)S(1)}, bf16[512,256]{1,0:T(8,128)(2,1)S(1)}, u32[]{:S(2)}, u32[]{:S(2)}) %collective-permute-start.10) | collective-permute-done | bytes 262176 | tf_op jit(solution)/shard_map/ppermute | solution.py:34
  92.3 0.8 collective-permute-start.25
  93.2 3.1 %collective-permute-done.11.refs_3_ = bf16[512,256]{1,0:T(8,128)(2,1)S(1)} collective-permute-done((bf16[512,256]{1,0:T(8,128)(2,1)S(1)}, bf16[512,256]{1,0:T(8,128)(2,1)S(1)}, u32[]{:S(2)}, u32[]{:S(2)}) %collective-permute-start.11) | collective-permute-done | bytes 262176 | tf_op jit(solution)/shard_map/ppermute | solution.py:34
  96.3 1.4 collective-permute-start.26
  97.7 8.3 %input_grad.1 = (f32[128,2048]{1,0:T(8,128)S(1)}, bf16[128,2048]{1,0:T(8,128)(2,1)S(1)}) custom-call(s32[5]{0:T(128)S(1)} %stack.35.place_ref, bf16[256,1152]{1,0:T(8,128)(2,1)S(1)} %get-tuple-element.35.da_ref.refs_4_, bf16[256,1152]{1,0:T(8,128)(2,1)} %get-tuple-element.36.db_ref.refs_4_, bf16[3,2048,768]{2,1,0:T(8,128)(2,1)} %bitcast.35), custom_call_target="tpu_custom_call" | custom-call | flops 2415919104 | bytes 9437184 | tf_op jit(solution)/shard_map/input_grad/pallas_call | solution.py:355
  106.1 2.0 %collective-permute-start.8 = (bf16[128,2048]{1,0:T(8,128)(2,1)S(1)}, bf16[128,2048]{1,0:T(8,128)(2,1)S(1)}, u32[]{:S(2)}, u32[]{:S(2)}) collective-permute-start(bf16[128,2048]{1,0:T(8,128)(2,1)S(1)} %get-tuple-element.38), channel_id=1, source_target_pairs={{0,1},{1,0},{2,3},{3,2},{4,5},{5,4},{6,7},{7,6},{8,9},{9,8},{10,11... | collective-permute-start | bytes 1572872 | tf_op jit(solution)/shard_map/ppermute | solution.py:34
  108.0 2.5 %weight_grad.2 = (bf16[128,1152]{1,0:T(8,128)(2,1)S(1)}, bf16[128,1152]{1,0:T(8,128)(2,1)S(1)}, bf16[128,1152]{1,0:T(8,128)(2,1)S(1)}, bf16[128,1152]{1,0:T(8,128)(2,1)S(1)}) custom-call(bf16[2,512,256]{2,1,0:T(8,128)(2,1)S(1)} %get-tuple-element.39.refs_0_, bf16[2,512,256]{2,1,0:T(8,128)(2,1)S(1)} %collective-permute-done.9.refs_1_, ...), custom_call_target="tpu_custom_call" | custom-call | flops 1207959552 | bytes 4718592 | tf_op jit(solution)/shard_map/weight_grad/pallas_call | solution.py:398
  110.6 2.1 %collective-permute-start.15 = (bf16[128,1152]{1,0:T(8,128)(2,1)S(1)}, bf16[128,1152]{1,0:T(8,128)(2,1)S(1)}, u32[]{:S(2)}, u32[]{:S(2)}) collective-permute-start(bf16[128,1152]{1,0:T(8,128)(2,1)S(1)} %get-tuple-element.44), channel_id=1, source_target_pairs={{0,4},{1,5},{2,6},{3,7},{4,8},{5,9},{6,10},{7,11},{8,12},{9,13},{1... | collective-permute-start | bytes 884744 | tf_op jit(solution)/shard_map/ppermute | solution.py:34
  112.7 9.0 %collective-permute-start.16 = (bf16[128,1152]{1,0:T(8,128)(2,1)S(1)}, bf16[128,1152]{1,0:T(8,128)(2,1)S(1)}, u32[]{:S(2)}, u32[]{:S(2)}) collective-permute-start(bf16[128,1152]{1,0:T(8,128)(2,1)S(1)} %get-tuple-element.45), channel_id=1, source_target_pairs={{0,12},{1,13},{2,14},{3,15},{4,0},{5,1},{6,2},{7,3},{8,4},{9,5},{1... | collective-permute-start | bytes 884744 | tf_op jit(solution)/shard_map/ppermute | solution.py:34
  121.7 3.2 %collective-permute-start.17 = (bf16[128,1152]{1,0:T(8,128)(2,1)S(1)}, bf16[128,1152]{1,0:T(8,128)(2,1)S(1)}, u32[]{:S(2)}, u32[]{:S(2)}) collective-permute-start(bf16[128,1152]{1,0:T(8,128)(2,1)S(1)} %get-tuple-element.46), channel_id=1, source_target_pairs={{0,8},{1,9},{2,10},{3,11},{4,12},{5,13},{6,14},{7,15},{8,0},{9,1},... | collective-permute-start | bytes 884744 | tf_op jit(solution)/shard_map/ppermute | solution.py:34
  124.9 0.1 convert_add_fusion
  125.1 0.8 collective-permute-start.27
  125.8 3.5 %collective-permute-done.15 = bf16[128,1152]{1,0:T(8,128)(2,1)S(1)} collective-permute-done((bf16[128,1152]{1,0:T(8,128)(2,1)S(1)}, bf16[128,1152]{1,0:T(8,128)(2,1)S(1)}, u32[]{:S(2)}, u32[]{:S(2)}) %collective-permute-start.15) | collective-permute-done | bytes 294944 | tf_op jit(solution)/shard_map/ppermute | solution.py:34
  129.3 1.0 collective-permute-done.16
  130.4 6.7 %collective-permute-done.17 = bf16[128,1152]{1,0:T(8,128)(2,1)S(1)} collective-permute-done((bf16[128,1152]{1,0:T(8,128)(2,1)S(1)}, bf16[128,1152]{1,0:T(8,128)(2,1)S(1)}, u32[]{:S(2)}, u32[]{:S(2)}) %collective-permute-start.17) | collective-permute-done | bytes 294944 | tf_op jit(solution)/shard_map/ppermute | solution.py:34
  137.1 0.1 convert_add_fusion.1
  137.2 2.6 %collective-permute-start.18 = (bf16[64,1152]{1,0:T(8,128)(2,1)S(1)}, bf16[64,1152]{1,0:T(8,128)(2,1)S(1)}, u32[]{:S(2)}, u32[]{:S(2)}) collective-permute-start(bf16[64,1152]{1,0:T(8,128)(2,1)S(1)} %slice.103), channel_id=1, source_target_pairs={{0,192},{1,193},{2,194},{3,195},{4,196},{5,197},{6,198},{7,199},{8... | collective-permute-start | bytes 442376 | tf_op jit(solution)/shard_map/ppermute | solution.py:34
  139.8 4.6 %collective-permute-done.18 = bf16[64,1152]{1,0:T(8,128)(2,1)S(1)} collective-permute-done((bf16[64,1152]{1,0:T(8,128)(2,1)S(1)}, bf16[64,1152]{1,0:T(8,128)(2,1)S(1)}, u32[]{:S(2)}, u32[]{:S(2)}) %collective-permute-start.18) | collective-permute-done | bytes 147488 | tf_op jit(solution)/shard_map/ppermute | solution.py:34
  144.5 7.3 %collective-permute-start.28 = (bf16[16,2304]{1,0:T(8,128)(2,1)S(1)}, bf16[16,2304]{1,0:T(8,128)(2,1)S(1)}, u32[]{:S(2)}, u32[]{:S(2)}) collective-permute-start(bf16[16,2304]{1,0:T(8,128)(2,1)S(1)} %get-tuple-element.53), channel_id=1, source_target_pairs={{0,16},{1,17},{2,18},{3,19},{4,20},{5,21},{6,22},{7,23},{8,24},{9,... | collective-permute-start | bytes 221192 | tf_op jit(solution)/shard_map/ppermute | solution.py:34
  151.7 3.9 %collective-permute-start.30 = (bf16[16,2304]{1,0:T(8,128)(2,1)S(1)}, bf16[16,2304]{1,0:T(8,128)(2,1)S(1)}, u32[]{:S(2)}, u32[]{:S(2)}) collective-permute-start(bf16[16,2304]{1,0:T(8,128)(2,1)S(1)} %get-tuple-element.54), channel_id=1, source_target_pairs={{0,32},{1,33},{2,34},{3,35},{4,36},{5,37},{6,38},{7,39},{8,40},{9,... | collective-permute-start | bytes 221192 | tf_op jit(solution)/shard_map/ppermute | solution.py:34
  155.6 0.9 fusion
  156.6 1.1 collective-permute-done.29
  157.7 3.5 %collective-permute-done.30 = bf16[16,2304]{1,0:T(8,128)(2,1)S(1)} collective-permute-done((bf16[16,2304]{1,0:T(8,128)(2,1)S(1)}, bf16[16,2304]{1,0:T(8,128)(2,1)S(1)}, u32[]{:S(2)}, u32[]{:S(2)}) %collective-permute-start.30) | collective-permute-done | bytes 73760 | tf_op jit(solution)/shard_map/ppermute | solution.py:34
  161.2 0.7 maximum_bitcast_fusion
  (55 shorter events, 0.5 us)
Async XLA Ops:
  0.6 1.2 copy-start
  1.9 0.7 copy-start.6
  2.5 8.9 %copy-start.8 = (f32[128]{0:T(128)S(1)}, f32[128]{0:T(128)}, u32[]{:S(2)}) copy-start(f32[128]{0:T(128)} %param.8) | copy-start | bytes 1540
  7.3 14.3 %copy-start.2 = (bf16[1,256,768]{2,1,0:T(8,128)(2,1)S(1)}, bf16[1,256,768]{2,1,0:T(8,128)(2,1)}, u32[]{:S(2)}) copy-start(bf16[1,256,768]{2,1,0:T(8,128)(2,1)} %param.11) | copy-start | bytes 1179652
  7.3 18.5 %copy-start.11 = (s32[128,9]{0,1:T(8,128)S(1)}, s32[128,9]{0,1:T(8,128)}, u32[]{:S(2)}) copy-start(s32[128,9]{0,1:T(8,128)} %param.10) | copy-start | bytes 13828
  7.4 36.9 %copy-start.7 = (f32[128]{0:T(128)S(1)}, f32[128]{0:T(128)}, u32[]{:S(2)}) copy-start(f32[128]{0:T(128)} %param.9) | copy-start | bytes 1540
  7.4 18.8 %collective-permute-start = (bf16[2,256,768]{2,1,0:T(8,128)(2,1)S(1)}, bf16[2,256,768]{2,1,0:T(8,128)(2,1)}, u32[]{:S(2)}, u32[]{:S(2)}) collective-permute-start(bf16[2,256,768]{2,1,0:T(8,128)(2,1)S(1)} %get-tuple-element.30.own_ref.kv_ref), channel_id=1, source_target_pairs={{0,2},{1,3},{2,4},{3,5},{4,6},{5,7},{6,8},{7,9},{8,10},{9,11},{10,... | collective-permute-start | bytes 2359304 | tf_op jit(solution)/shard_map/ppermute | solution.py:34
  10.1 17.6 %collective-permute-start.1 = (bf16[2,256,768]{2,1,0:T(8,128)(2,1)S(1)}, bf16[2,256,768]{2,1,0:T(8,128)(2,1)}, u32[]{:S(2)}, u32[]{:S(2)}) collective-permute-start(bf16[2,256,768]{2,1,0:T(8,128)(2,1)S(1)} %get-tuple-element.30.own_ref.kv_ref), channel_id=1, source_target_pairs={{2,0},{3,1},{4,2},{5,3},{6,4},{7,5},{8,6},{9,7},{10,8},{11,9},{12,... | collective-permute-start | bytes 2359304 | tf_op jit(solution)/shard_map/ppermute | solution.py:34
  11.4 44.1 %copy-start.1 = (bf16[1,256,2048]{2,1,0:T(8,128)(2,1)S(1)}, bf16[1,256,2048]{2,1,0:T(8,128)(2,1)}, u32[]{:S(2)}) copy-start(bf16[1,256,2048]{2,1,0:T(8,128)(2,1)} %param.6) | copy-start | bytes 3145732
  15.1 0.9 copy-start.9
  16.0 28.2 %copy-start.4 = (bf16[256,768]{1,0:T(8,128)(2,1)}, bf16[256,768]{1,0:T(8,128)(2,1)S(1)}, u32[]{:S(2)}) copy-start(bf16[256,768]{1,0:T(8,128)(2,1)S(1)} %get-tuple-element.28.q_ref.qo_ref) | copy-start | bytes 1179652
  16.0 23.9 %collective-permute-start.2 = (bf16[256,768]{1,0:T(8,128)(2,1)S(1)}, bf16[256,768]{1,0:T(8,128)(2,1)}, u32[]{:S(2)}, u32[]{:S(2)}) collective-permute-start(bf16[256,768]{1,0:T(8,128)(2,1)S(1)} %get-tuple-element.28.q_ref.qo_ref), channel_id=1, source_target_pairs={{0,2},{1,3},{2,4},{3,5},{4,6},{5,7},{6,8},{7,9},{8,10},{9,11},{10,... | collective-permute-start | bytes 1179656 | tf_op jit(solution)/shard_map/ppermute | solution.py:34
  20.3 20.9 %collective-permute-start.3 = (bf16[256,768]{1,0:T(8,128)(2,1)S(1)}, bf16[256,768]{1,0:T(8,128)(2,1)}, u32[]{:S(2)}, u32[]{:S(2)}) collective-permute-start(bf16[256,768]{1,0:T(8,128)(2,1)S(1)} %get-tuple-element.28.q_ref.qo_ref), channel_id=1, source_target_pairs={{2,0},{3,1},{4,2},{5,3},{6,4},{7,5},{8,6},{9,7},{10,8},{11,9},{12,... | collective-permute-start | bytes 1179656 | tf_op jit(solution)/shard_map/ppermute | solution.py:34
  21.6 19.6 %collective-permute-start.4 = (bf16[256,768]{1,0:T(8,128)(2,1)S(1)}, bf16[256,768]{1,0:T(8,128)(2,1)}, u32[]{:S(2)}, u32[]{:S(2)}) collective-permute-start(bf16[256,768]{1,0:T(8,128)(2,1)S(1)} %bitcast.24), channel_id=1, source_target_pairs={{0,2},{1,3},{2,4},{3,5},{4,6},{5,7},{6,8},{7,9},{8,10},{9,11},{10,... | collective-permute-start | bytes 1179656 | tf_op jit(solution)/shard_map/ppermute | solution.py:34
  26.2 15.1 %collective-permute-start.5 = (bf16[256,768]{1,0:T(8,128)(2,1)S(1)}, bf16[256,768]{1,0:T(8,128)(2,1)}, u32[]{:S(2)}, u32[]{:S(2)}) collective-permute-start(bf16[256,768]{1,0:T(8,128)(2,1)S(1)} %bitcast.25), channel_id=1, source_target_pairs={{2,0},{3,1},{4,2},{5,3},{6,4},{7,5},{8,6},{9,7},{10,8},{11,9},{12,... | collective-permute-start | bytes 1179656 | tf_op jit(solution)/shard_map/ppermute | solution.py:34
  27.7 1.1 copy-start.10
  36.3 4.9 %collective-permute-start.6 = (f32[6,8,256]{2,1,0:T(8,128)S(1)}, f32[6,8,256]{2,1,0:T(8,128)S(1)}, u32[]{:S(2)}, u32[]{:S(2)}) collective-permute-start(f32[6,8,256]{2,1,0:T(8,128)S(1)} %get-tuple-element.33.so_ref), channel_id=1, source_target_pairs={{0,2},{1,3},{2,4},{3,5},{4,6},{5,7},{6,8},{7,9},{8,10},{9,11},{10,... | collective-permute-start | bytes 147464 | tf_op jit(solution)/shard_map/ppermute | solution.py:34
  39.9 4.3 %collective-permute-start.7 = (f32[6,8,256]{2,1,0:T(8,128)S(1)}, f32[6,8,256]{2,1,0:T(8,128)S(1)}, u32[]{:S(2)}, u32[]{:S(2)}) collective-permute-start(f32[6,8,256]{2,1,0:T(8,128)S(1)} %get-tuple-element.33.so_ref), channel_id=1, source_target_pairs={{2,0},{3,1},{4,2},{5,3},{6,4},{7,5},{8,6},{9,7},{10,8},{11,9},{12,... | collective-permute-start | bytes 147464 | tf_op jit(solution)/shard_map/ppermute | solution.py:34
  44.3 1.0 copy-start.3
  45.3 1.0 copy-start.5
  52.0 16.0 %collective-permute-start.22 = (bf16[256,1152]{1,0:T(8,128)(2,1)}, bf16[256,1152]{1,0:T(8,128)(2,1)S(1)}, u32[]{:S(2)}, u32[]{:S(2)}) collective-permute-start(bf16[256,1152]{1,0:T(8,128)(2,1)} %get-tuple-element.36.db_ref.refs_4_), channel_id=1, source_target_pairs={{0,4},{1,5},{2,6},{3,7},{4,0},{5,1},{6,2},{7,3},{8,12},{9,13},{10,... | collective-permute-start | bytes 1769480 | tf_op jit(solution)/shard_map/ppermute | solution.py:34
  54.6 28.1 %collective-permute-start.13 = (bf16[256,1152]{1,0:T(8,128)(2,1)S(1)}, bf16[256,1152]{1,0:T(8,128)(2,1)S(1)}, u32[]{:S(2)}, u32[]{:S(2)}) collective-permute-start(bf16[256,1152]{1,0:T(8,128)(2,1)S(1)} %get-tuple-element.35.da_ref.refs_4_), channel_id=1, source_target_pairs={{0,64},{1,65},{2,66},{3,67},{4,68},{5,69},{6,70},{7,71},{8,72},{9,... | collective-permute-start | bytes 1769480 | tf_op jit(solution)/shard_map/ppermute | solution.py:34
  56.8 16.7 %collective-permute-start.19 = (bf16[512,256]{1,0:T(8,128)(2,1)S(1)}, bf16[512,256]{1,0:T(8,128)(2,1)S(1)}, u32[]{:S(2)}, u32[]{:S(2)}) collective-permute-start(bf16[512,256]{1,0:T(8,128)(2,1)S(1)} %get-tuple-element.47), channel_id=1, source_target_pairs={{0,4},{1,5},{2,6},{3,7},{4,0},{5,1},{6,2},{7,3},{8,12},{9,13},{10,... | collective-permute-start | bytes 786440 | tf_op jit(solution)/shard_map/ppermute | solution.py:34
  56.9 27.1 %collective-permute-start.21 = (bf16[256,1152]{1,0:T(8,128)(2,1)}, bf16[256,1152]{1,0:T(8,128)(2,1)S(1)}, u32[]{:S(2)}, u32[]{:S(2)}) collective-permute-start(bf16[256,1152]{1,0:T(8,128)(2,1)} %get-tuple-element.36.db_ref.refs_4_), channel_id=1, source_target_pairs={{0,2},{1,3},{2,0},{3,1},{4,6},{5,7},{6,4},{7,5},{8,10},{9,11},{10,... | collective-permute-start | bytes 1769480 | tf_op jit(solution)/shard_map/ppermute | solution.py:34
  58.2 24.9 %collective-permute-start.9 = (bf16[2,512,256]{2,1,0:T(8,128)(2,1)S(1)}, bf16[2,512,256]{2,1,0:T(8,128)(2,1)S(1)}, u32[]{:S(2)}, u32[]{:S(2)}) collective-permute-start(bf16[2,512,256]{2,1,0:T(8,128)(2,1)S(1)} %get-tuple-element.40), channel_id=1, source_target_pairs={{0,2},{1,3},{2,0},{3,1},{4,6},{5,7},{6,4},{7,5},{8,10},{9,11},{10,... | collective-permute-start | bytes 1572872 | tf_op jit(solution)/shard_map/ppermute | solution.py:34
  68.0 16.7 %collective-permute-start.23 = (bf16[256,1152]{1,0:T(8,128)(2,1)S(1)}, bf16[256,1152]{1,0:T(8,128)(2,1)S(1)}, u32[]{:S(2)}, u32[]{:S(2)}) collective-permute-start(bf16[256,1152]{1,0:T(8,128)(2,1)S(1)} %collective-permute-done.22.refs_6_), channel_id=1, source_target_pairs={{0,2},{1,3},{2,0},{3,1},{4,6},{5,7},{6,4},{7,5},{8,10},{9,11},{10,... | collective-permute-start | bytes 1769480 | tf_op jit(solution)/shard_map/ppermute | solution.py:34
  73.5 9.2 %collective-permute-start.20 = (bf16[512,256]{1,0:T(8,128)(2,1)S(1)}, bf16[512,256]{1,0:T(8,128)(2,1)S(1)}, u32[]{:S(2)}, u32[]{:S(2)}) collective-permute-start(bf16[512,256]{1,0:T(8,128)(2,1)S(1)} %get-tuple-element.48), channel_id=1, source_target_pairs={{0,6},{1,7},{2,4},{3,5},{4,2},{5,3},{6,0},{7,1},{8,14},{9,15},{10,... | collective-permute-start | bytes 786440 | tf_op jit(solution)/shard_map/ppermute | solution.py:34
  82.7 23.4 %collective-permute-start.12 = (bf16[256,1152]{1,0:T(8,128)(2,1)S(1)}, bf16[256,1152]{1,0:T(8,128)(2,1)S(1)}, u32[]{:S(2)}, u32[]{:S(2)}) collective-permute-start(bf16[256,1152]{1,0:T(8,128)(2,1)S(1)} %get-tuple-element.35.da_ref.refs_4_), channel_id=1, source_target_pairs={{0,2},{1,3},{2,0},{3,1},{4,6},{5,7},{6,4},{7,5},{8,10},{9,11},{10,... | collective-permute-start | bytes 1769480 | tf_op jit(solution)/shard_map/ppermute | solution.py:34
  82.8 25.2 %collective-permute-start.14 = (bf16[256,1152]{1,0:T(8,128)(2,1)S(1)}, bf16[256,1152]{1,0:T(8,128)(2,1)S(1)}, u32[]{:S(2)}, u32[]{:S(2)}) collective-permute-start(bf16[256,1152]{1,0:T(8,128)(2,1)S(1)} %collective-permute-done.13.refs_6_), channel_id=1, source_target_pairs={{0,2},{1,3},{2,0},{3,1},{4,6},{5,7},{6,4},{7,5},{8,10},{9,11},{10,... | collective-permute-start | bytes 1769480 | tf_op jit(solution)/shard_map/ppermute | solution.py:34
  83.2 9.2 %collective-permute-start.10 = (bf16[512,256]{1,0:T(8,128)(2,1)S(1)}, bf16[512,256]{1,0:T(8,128)(2,1)S(1)}, u32[]{:S(2)}, u32[]{:S(2)}) collective-permute-start(bf16[512,256]{1,0:T(8,128)(2,1)S(1)} %get-tuple-element.41), channel_id=1, source_target_pairs={{0,64},{1,65},{2,66},{3,67},{4,68},{5,69},{6,70},{7,71},{8,72},{9,... | collective-permute-start | bytes 786440 | tf_op jit(solution)/shard_map/ppermute | solution.py:34
  84.0 12.3 %collective-permute-start.11 = (bf16[512,256]{1,0:T(8,128)(2,1)S(1)}, bf16[512,256]{1,0:T(8,128)(2,1)S(1)}, u32[]{:S(2)}, u32[]{:S(2)}) collective-permute-start(bf16[512,256]{1,0:T(8,128)(2,1)S(1)} %get-tuple-element.42), channel_id=1, source_target_pairs={{0,66},{1,67},{2,64},{3,65},{4,70},{5,71},{6,68},{7,69},{8,74},{9,... | collective-permute-start | bytes 786440 | tf_op jit(solution)/shard_map/ppermute | solution.py:34
  88.0 24.6 %collective-permute-start.24 = (bf16[128,1152]{1,0:T(8,128)(2,1)S(1)}, bf16[128,1152]{1,0:T(8,128)(2,1)S(1)}, u32[]{:S(2)}, u32[]{:S(2)}) collective-permute-start(bf16[128,1152]{1,0:T(8,128)(2,1)S(1)} %get-tuple-element.50), channel_id=1, source_target_pairs={{0,64},{1,65},{2,66},{3,67},{4,68},{5,69},{6,70},{7,71},{8,72},{9,... | collective-permute-start | bytes 884744 | tf_op jit(solution)/shard_map/ppermute | solution.py:34
  92.3 29.4 %collective-permute-start.25 = (bf16[128,1152]{1,0:T(8,128)(2,1)S(1)}, bf16[128,1152]{1,0:T(8,128)(2,1)S(1)}, u32[]{:S(2)}, u32[]{:S(2)}) collective-permute-start(bf16[128,1152]{1,0:T(8,128)(2,1)S(1)} %get-tuple-element.51), channel_id=1, source_target_pairs={{0,192},{1,193},{2,194},{3,195},{4,196},{5,197},{6,198},{7,199},{8... | collective-permute-start | bytes 884744 | tf_op jit(solution)/shard_map/ppermute | solution.py:34
  96.3 28.6 %collective-permute-start.26 = (bf16[128,1152]{1,0:T(8,128)(2,1)S(1)}, bf16[128,1152]{1,0:T(8,128)(2,1)S(1)}, u32[]{:S(2)}, u32[]{:S(2)}) collective-permute-start(bf16[128,1152]{1,0:T(8,128)(2,1)S(1)} %get-tuple-element.52), channel_id=1, source_target_pairs={{0,128},{1,129},{2,130},{3,131},{4,132},{5,133},{6,134},{7,135},{8... | collective-permute-start | bytes 884744 | tf_op jit(solution)/shard_map/ppermute | solution.py:34
  106.1 49.6 %collective-permute-start.8 = (bf16[128,2048]{1,0:T(8,128)(2,1)S(1)}, bf16[128,2048]{1,0:T(8,128)(2,1)S(1)}, u32[]{:S(2)}, u32[]{:S(2)}) collective-permute-start(bf16[128,2048]{1,0:T(8,128)(2,1)S(1)} %get-tuple-element.38), channel_id=1, source_target_pairs={{0,1},{1,0},{2,3},{3,2},{4,5},{5,4},{6,7},{7,6},{8,9},{9,8},{10,11... | collective-permute-start | bytes 1572872 | tf_op jit(solution)/shard_map/ppermute | solution.py:34
  110.6 18.7 %collective-permute-start.15 = (bf16[128,1152]{1,0:T(8,128)(2,1)S(1)}, bf16[128,1152]{1,0:T(8,128)(2,1)S(1)}, u32[]{:S(2)}, u32[]{:S(2)}) collective-permute-start(bf16[128,1152]{1,0:T(8,128)(2,1)S(1)} %get-tuple-element.44), channel_id=1, source_target_pairs={{0,4},{1,5},{2,6},{3,7},{4,8},{5,9},{6,10},{7,11},{8,12},{9,13},{1... | collective-permute-start | bytes 884744 | tf_op jit(solution)/shard_map/ppermute | solution.py:34
  112.7 17.7 %collective-permute-start.16 = (bf16[128,1152]{1,0:T(8,128)(2,1)S(1)}, bf16[128,1152]{1,0:T(8,128)(2,1)S(1)}, u32[]{:S(2)}, u32[]{:S(2)}) collective-permute-start(bf16[128,1152]{1,0:T(8,128)(2,1)S(1)} %get-tuple-element.45), channel_id=1, source_target_pairs={{0,12},{1,13},{2,14},{3,15},{4,0},{5,1},{6,2},{7,3},{8,4},{9,5},{1... | collective-permute-start | bytes 884744 | tf_op jit(solution)/shard_map/ppermute | solution.py:34
  121.7 15.3 %collective-permute-start.17 = (bf16[128,1152]{1,0:T(8,128)(2,1)S(1)}, bf16[128,1152]{1,0:T(8,128)(2,1)S(1)}, u32[]{:S(2)}, u32[]{:S(2)}) collective-permute-start(bf16[128,1152]{1,0:T(8,128)(2,1)S(1)} %get-tuple-element.46), channel_id=1, source_target_pairs={{0,8},{1,9},{2,10},{3,11},{4,12},{5,13},{6,14},{7,15},{8,0},{9,1},... | collective-permute-start | bytes 884744 | tf_op jit(solution)/shard_map/ppermute | solution.py:34
  125.1 14.7 %collective-permute-start.27 = (bf16[64,1152]{1,0:T(8,128)(2,1)S(1)}, bf16[64,1152]{1,0:T(8,128)(2,1)S(1)}, u32[]{:S(2)}, u32[]{:S(2)}) collective-permute-start(bf16[64,1152]{1,0:T(8,128)(2,1)S(1)} %slice.102), channel_id=1, source_target_pairs={{0,12},{1,13},{2,14},{3,15},{4,8},{5,9},{6,10},{7,11},{8,4},{9,5},... | collective-permute-start | bytes 442376 | tf_op jit(solution)/shard_map/ppermute | solution.py:34
  137.2 7.2 %collective-permute-start.18 = (bf16[64,1152]{1,0:T(8,128)(2,1)S(1)}, bf16[64,1152]{1,0:T(8,128)(2,1)S(1)}, u32[]{:S(2)}, u32[]{:S(2)}) collective-permute-start(bf16[64,1152]{1,0:T(8,128)(2,1)S(1)} %slice.103), channel_id=1, source_target_pairs={{0,192},{1,193},{2,194},{3,195},{4,196},{5,197},{6,198},{7,199},{8... | collective-permute-start | bytes 442376 | tf_op jit(solution)/shard_map/ppermute | solution.py:34
  144.5 12.1 %collective-permute-start.28 = (bf16[16,2304]{1,0:T(8,128)(2,1)S(1)}, bf16[16,2304]{1,0:T(8,128)(2,1)S(1)}, u32[]{:S(2)}, u32[]{:S(2)}) collective-permute-start(bf16[16,2304]{1,0:T(8,128)(2,1)S(1)} %get-tuple-element.53), channel_id=1, source_target_pairs={{0,16},{1,17},{2,18},{3,19},{4,20},{5,21},{6,22},{7,23},{8,24},{9,... | collective-permute-start | bytes 221192 | tf_op jit(solution)/shard_map/ppermute | solution.py:34
  151.7 5.9 %collective-permute-start.29 = (bf16[16,2304]{1,0:T(8,128)(2,1)S(1)}, bf16[16,2304]{1,0:T(8,128)(2,1)S(1)}, u32[]{:S(2)}, u32[]{:S(2)}) collective-permute-start(bf16[16,2304]{1,0:T(8,128)(2,1)S(1)} %get-tuple-element.55), channel_id=1, source_target_pairs={{0,48},{1,49},{2,50},{3,51},{4,52},{5,53},{6,54},{7,55},{8,56},{9,... | collective-permute-start | bytes 221192 | tf_op jit(solution)/shard_map/ppermute | solution.py:34
  151.7 9.4 %collective-permute-start.30 = (bf16[16,2304]{1,0:T(8,128)(2,1)S(1)}, bf16[16,2304]{1,0:T(8,128)(2,1)S(1)}, u32[]{:S(2)}, u32[]{:S(2)}) collective-permute-start(bf16[16,2304]{1,0:T(8,128)(2,1)S(1)} %get-tuple-element.54), channel_id=1, source_target_pairs={{0,32},{1,33},{2,34},{3,35},{4,36},{5,37},{6,38},{7,39},{8,40},{9,... | collective-permute-start | bytes 221192 | tf_op jit(solution)/shard_map/ppermute | solution.py:34

commit v2 on v1

--- a/solution.py
+++ b/solution.py
@@ -34,6 +34,10 @@
     return lax.ppermute(value, AXES, pairs)
 
 
+def after(*values):
+    return lax.optimization_barrier(values)
+
+
 def to_slab(step):
     def target(x, zh, y, c, h):
         seq = zh * 8 + y * 2 + c + step
@@ -117,15 +121,16 @@
     )(x, w, w, gain)
 
 
-def project_q_kernel(x_ref, w_ref, gain_ref, q_ref, raw_ref):
+def project_q_kernel(x_ref, w_ref, gain_ref, g_ref, qg_ref, raw_ref):
     raw = dot(x_ref[...], w_ref[0], NN)
     raw_ref[...] = raw
     for i in range(raw.shape[1] // HD):
         part = raw[:, i * HD : (i + 1) * HD]
-        q_ref[:, i * HD : (i + 1) * HD] = (part * inv_rms(part) * gain_ref[...]).astype(BF16)
-
-
-def project_q(x, w, gain):
+        qg_ref[0, :, i * HD : (i + 1) * HD] = (part * inv_rms(part) * gain_ref[...]).astype(BF16)
+    qg_ref[1] = g_ref[...]
+
+
+def project_q(x, w, gain, g):
     rows, width = x.shape
     cols = w.shape[2]
     block = 2 * HD
@@ -136,19 +141,20 @@
             pl.BlockSpec((rows, width), lambda i: (0, 0)),
             pl.BlockSpec((1, width, block), lambda i: (0, 0, i)),
             pl.BlockSpec((1, HD), lambda i: (0, 0)),
+            pl.BlockSpec((rows, block), lambda i: (0, i)),
         ],
         out_specs=[
+            pl.BlockSpec((2, rows, block), lambda i: (0, 0, i)),
             pl.BlockSpec((rows, block), lambda i: (0, i)),
-            pl.BlockSpec((rows, block), lambda i: (0, i)),
         ],
         out_shape=[
-            jax.ShapeDtypeStruct((rows, cols), BF16),
+            jax.ShapeDtypeStruct((2, rows, cols), BF16),
             jax.ShapeDtypeStruct((rows, cols), F32),
         ],
         compiler_params=params(),
         cost_estimate=cost(2 * rows * width * cols, 2 * width * cols),
         name="project_q",
-    )(x, w, gain)
+    )(x, w, gain, g)
 
 
 def spread_rows_kernel(place_ref, x_ref, core_ref, a0_ref, a1_ref, b0_ref, b1_ref, own_ref, xt_ref):
@@ -161,27 +167,24 @@
     def source(xx, zz, yy, cc):
         return xt_ref[pl.ds(pl.multiple_of((((xx * 4 + zz) * 4 + yy) * 2 + cc) * 16, 16), 16), :]
 
-    flips = (0, 3, 1, 2)
-    for k in range(4):
-        for s in range(4):
+    for part, (s, order) in enumerate(((0, (0, 3)), (0, (1, 2)), (1, (0, 1)), (1, (3, 2)))):
+        for k in range(2):
             for m in range(4):
                 zz = lax.rem(zh + m, 4)
-                ya, xa = lax.rem(y + k, 4), x ^ flips[s]
-                xb, yb = lax.rem(x + k, 4), y ^ flips[s]
-                row = ((k * 2 + s % 2) * 4 + m) * 16
+                row = ((part * 2 + k) * 4 + m) * 16
                 rows = slice(row, row + 16)
-                same_a, other_a = source(xa, zz, ya, c), source(xa, zz, ya, 1 - c)
-                same_b, other_b = source(xb, zz, yb, c), source(xb, zz, yb, 1 - c)
-                if s < 2:
-                    own_ref[0, rows, :] = same_a
-                    own_ref[1, rows, :] = same_b
-                    core_ref[0, rows, :] = other_a
-                    core_ref[1, rows, :] = other_b
-                else:
-                    a0_ref[rows, :] = same_a
-                    a1_ref[rows, :] = other_a
-                    b0_ref[rows, :] = same_b
-                    b1_ref[rows, :] = other_b
+                for near in range(2):
+                    pair = (0, 3)[s] ^ (1 - near)
+                    for cc in range(2):
+                        core = c if cc == 0 else 1 - c
+                        from_a = source(x ^ pair, zz, y ^ order[k], core)
+                        from_b = source(x ^ order[k], zz, y ^ pair, core)
+                        if near:
+                            (own_ref, core_ref)[cc][0, rows, :] = from_a
+                            (own_ref, core_ref)[cc][1, rows, :] = from_b
+                        else:
+                            (a0_ref, a1_ref)[cc][rows, :] = from_a
+                            (b0_ref, b1_ref)[cc][rows, :] = from_b
 
 
 def spread_rows(x, place):
@@ -217,17 +220,17 @@
 
 
 def queries_kernel(
-    mask_ref, q_ref, raw_ref, gain_ref, g_ref, low_ref, own_ref, high_ref,
+    mask_ref, qg_ref, raw_ref, gain_ref, low_ref, own_ref, high_ref,
     out_ref, dq_ref, stats_ref, full_ref,
 ):
     @pl.when(pl.program_id(0) == 0)
     def _():
         fill_mask(mask_ref, 0, full_ref)
 
-    for i in range(q_ref.shape[1] // HD):
+    for i in range(qg_ref.shape[2] // HD):
         cols = slice(i * HD, (i + 1) * HD)
-        q = q_ref[:, cols]
-        g = g_ref[:, cols]
+        q = qg_ref[0, :, cols]
+        g = qg_ref[1, :, cols]
         keys = jnp.concatenate([low_ref[0, :, cols], own_ref[0, :, cols], high_ref[0, :, cols]], 0)
         values = jnp.concatenate([low_ref[1, :, cols], own_ref[1, :, cols], high_ref[1, :, cols]], 0)
         expo = jnp.exp2(dot(q, keys, NT) * EXP2_SCALE) * full_ref[...]
@@ -244,8 +247,8 @@
         stats_ref[i] = both.T[:8, :]
 
 
-def queries(mask, q_hat, q_raw, gain, g, low, own, high):
-    rows, cols = q_hat.shape
+def queries(mask, qg, q_raw, gain, low, own, high):
+    rows, cols = q_raw.shape
     block = 2 * HD
     flat = pl.BlockSpec((rows, block), lambda i: (0, i))
     pair = pl.BlockSpec((2, rows, block), lambda i: (0, 0, i))
@@ -254,10 +257,9 @@
         grid=(cols // block,),
         in_specs=[
             pl.BlockSpec((8, 3 * rows), lambda i: (0, 0)),
-            flat,
+            pair,
             flat,
             pl.BlockSpec((1, HD), lambda i: (0, 0)),
-            flat,
             pair,
             pair,
             pair,
@@ -272,15 +274,15 @@
         compiler_params=params(),
         cost_estimate=cost(24 * rows * rows * cols, 20 * rows * cols, 3 * rows * rows * cols // HD),
         name="queries",
-    )(mask, q_hat, q_raw, gain, g, low, own, high)
+    )(mask, qg, q_raw, gain, low, own, high)
 
 
 def keys_kernel(
-    mask_ref, kv_ref, raw_ref, gain_ref, ql_ref, qo_ref, qh_ref, gl_ref, go_ref, gh_ref,
+    mask_ref, kv_ref, raw_ref, gain_ref, low_ref, own_ref, high_ref,
     sl_ref, so_ref, sh_ref, dq_ref, da_ref, db_ref, full_ref,
 ):
     step = pl.program_id(0)
-    heads = qo_ref.shape[1] // HD
+    heads = own_ref.shape[2] // HD
     half = 3 * HD
 
     @pl.when(step == 0)
@@ -293,8 +295,8 @@
         cols = slice(i * HD, (i + 1) * HD)
         key = kv_ref[0, :, cols]
         value = kv_ref[1, :, cols]
-        q_wide = jnp.concatenate([ql_ref[:, cols], qo_ref[:, cols], qh_ref[:, cols]], 0)
-        g_wide = jnp.concatenate([gl_ref[:, cols], go_ref[:, cols], gh_ref[:, cols]], 0)
+        q_wide = jnp.concatenate([low_ref[0, :, cols], own_ref[0, :, cols], high_ref[0, :, cols]], 0)
+        g_wide = jnp.concatenate([low_ref[1, :, cols], own_ref[1, :, cols], high_ref[1, :, cols]], 0)
         stats = jnp.concatenate([sl_ref[i], so_ref[i], sh_ref[i]], axis=1)
         probs = jnp.exp2(dot(key, q_wide, NT) * EXP2_SCALE) * full_ref[...] * stats[0:1, :]
         d_value = dot(probs.astype(BF16), g_wide, NN)
@@ -306,10 +308,11 @@
         db_ref[:, at] = d_value.astype(BF16)
 
 
-def keys(mask, kv, k_raw, gain, q3, g3, s3, dq):
+def keys(mask, kv, k_raw, gain, qg3, s3, dq):
     rows, cols = k_raw.shape
     block = 2 * HD
     flat = pl.BlockSpec((rows, block), lambda i: (0, i))
+    pair = pl.BlockSpec((2, rows, block), lambda i: (0, 0, i))
     stats = pl.BlockSpec((2, 8, rows), lambda i: (i, 0, 0))
     wide = pl.BlockSpec((rows, cols * 3 // 2), lambda i: (0, 0))
     return pl.pallas_call(
@@ -317,10 +320,10 @@
         grid=(cols // block,),
         in_specs=[
             pl.BlockSpec((8, 3 * rows), lambda i: (0, 0)),
-            pl.BlockSpec((2, rows, block), lambda i: (0, 0, i)),
+            pair,
             flat,
             pl.BlockSpec((1, HD), lambda i: (0, 0)),
-            *[flat] * 6,
+            *[pair] * 3,
             *[stats] * 3,
             pl.BlockSpec((rows, cols), lambda i: (0, 0)),
         ],
@@ -330,7 +333,7 @@
         compiler_params=params(),
         cost_estimate=cost(24 * rows * rows * cols, 24 * rows * cols, 3 * rows * rows * cols // HD),
         name="keys",
-    )(mask, kv, k_raw, gain, *q3, *g3, *s3, dq)
+    )(mask, kv, k_raw, gain, *qg3, *s3, dq)
 
 
 def input_grad_kernel(place_ref, da_ref, db_ref, w_ref, keep_ref, send_ref, acc_ref):
@@ -420,8 +423,8 @@
     return jnp.repeat(both, TILE, axis=1)
 
 
-def reduce4(own, others):
-    total = own.astype(F32)
+def added(first, *others):
+    total = first.astype(F32)
     for other in others:
         total = total + other.astype(F32)
     return total
@@ -438,53 +441,59 @@
     q_gain = q_gain.reshape(1, HD)
     k_gain = k_gain.reshape(1, HD)
 
-    g_low = permute(g, to_slab(1))
-    g_high = permute(g, to_slab(-1))
     kv, k_raw = project_kv(x, w, k_gain)
     kv_low = permute(kv, to_slab(1))
     kv_high = permute(kv, to_slab(-1))
-    q_hat, q_raw = project_q(x, w, q_gain)
-    q_low = permute(q_hat, to_slab(1))
-    q_high = permute(q_hat, to_slab(-1))
+    qg, q_raw = project_q(x, w, q_gain, g)
+    qg_low = permute(qg, to_slab(1))
+    qg_high = permute(qg, to_slab(-1))
 
     to_core, to_a0, to_a1, to_b0, to_b1, own_rows = spread_rows(x, place)
+    mask = tile_masks(neighbours, seq)
     core_rows = permute(to_core, flip(core=1))
+    kv_low, kv_high, to_a0, to_a1, mask = after(kv_low, kv_high, to_a0, to_a1, mask)
     a0 = permute(to_a0, flip(x_bits=1))
     a1 = permute(to_a1, flip(x_bits=1, core=1))
-    b0 = permute(to_b0, flip(y_bits=1))
-    b1 = permute(to_b1, flip(y_bits=1, core=1))
-
-    mask = tile_masks(neighbours, seq)
-    attn_out, dq, stats = queries(mask, q_hat, q_raw, q_gain, g, kv_low, kv, kv_high)
+
+    attn_out, dq, stats = queries(mask, qg, q_raw, q_gain, kv_low, kv, kv_high)
+    stats, core_rows, a0, a1, to_b0 = after(stats, core_rows, a0, a1, to_b0)
     s_low = permute(stats, to_slab(1))
     s_high = permute(stats, to_slab(-1))
+    b0 = permute(to_b0, flip(y_bits=1))
+    s_low, s_high, qg_low, qg_high, to_b1 = after(s_low, s_high, qg_low, qg_high, to_b1)
+    b1 = permute(to_b1, flip(y_bits=1, core=1))
     da, db = keys(
-        mask, kv, k_raw, k_gain, (q_low, q_hat, q_high), (g_low, g, g_high),
-        (s_low, stats, s_high), dq,
+        mask, kv, k_raw, k_gain, (qg_low, qg, qg_high), (s_low, stats, s_high), dq
     )
 
+    da, db, b0, b1 = after(da, db, b0, b1)
     dax = permute(da, flip(x_bits=1))
     dby = permute(db, flip(y_bits=1))
     dac = permute(da, flip(core=1))
     dbc = permute(db, flip(core=1))
     keep, send = input_grad(place, da, db, w)
-    got = permute(send, flip(head=1))
+    dax, dby, dac, dbc, send = after(dax, dby, dac, dbc, send)
     daxc = permute(dax, flip(core=1))
     dbyc = permute(dby, flip(core=1))
+    got = permute(send, flip(head=1))
 
     pa = weight_grad(0, (own_rows, core_rows, a0, a1), (da, dac, dax, daxc))
     pb = weight_grad(1, (own_rows, core_rows, b0, b1), (db, dbc, dby, dbyc))
-    ra = [permute(pa[k], to_y(k)) for k in (1, 3, 2)]
-    rb = [permute(pb[k], to_x(k)) for k in (1, 3, 2)]
-    sa = reduce4(pa[0], ra)
-    sb = reduce4(pb[0], rb)
-    ca = permute(sa[64:].astype(BF16), flip(x_bits=3))
-    cb = permute(sb[64:].astype(BF16), flip(y_bits=3))
-    ta = sa[:64] + ca.astype(F32)
-    tb = sb[:64] + cb.astype(F32)
+    ra0 = permute(pa[1], flip(y_bits=1))
+    ra1 = permute(pa[3], flip(y_bits=3))
+    rb0 = permute(pb[1], flip(x_bits=1))
+    rb1 = permute(pb[3], flip(x_bits=3))
+    ua0 = permute(added(pa[0][64:], ra0[64:]).astype(BF16), flip(y_bits=3))
+    ua1 = permute(added(pa[2][64:], ra1[64:]).astype(BF16), flip(y_bits=1))
+    ub0 = permute(added(pb[0][64:], rb0[64:]).astype(BF16), flip(x_bits=3))
+    ub1 = permute(added(pb[2][64:], rb1[64:]).astype(BF16), flip(x_bits=1))
+    ca = permute(added(pa[2][:64], ra1[:64], ua1).astype(BF16), flip(x_bits=3))
+    cb = permute(added(pb[2][:64], rb1[:64], ub1).astype(BF16), flip(y_bits=3))
+    ta = added(pa[0][:64], ra0[:64], ua0, ca)
+    tb = added(pb[0][:64], rb0[:64], ub0, cb)
     both = jnp.concatenate([ta, tb], axis=1).reshape(4, 16, -1).astype(BF16)
     rz = [permute(both[m], to_z(m)) for m in (1, 3, 2)]
-    total = reduce4(both[0], rz)
+    total = added(both[0], *rz)
     part = total.shape[1] // 6
     grad_w = jnp.stack(
         [

time: 164 us -> 143 us (0.87)
  waiting for transfers between devices: 49.5 us -> 33.1 us
  starting transfers between devices: 65.6 us -> 59.5 us
    ppermute x31, waiting for transfers between devices: 49.5 us -> 33.1 us  [permute(): return lax.ppermute(value, AXES, pairs)]
    ppermute x31, starting transfers between devices: 65.6 us -> 59.5 us  [permute(): return lax.ppermute(value, AXES, pairs)]
    unnamed x24 -> x30, local copies, waits for them, and re-layouts: 5.92 us -> 7.55 us
  transfers between devices with their start and end apart: 31 -> 31, of which waited for: 12 -> 13; matrix products, arithmetic and copies ran while one was open for 1% -> 1% of each run, Pallas kernels for 16% -> 23%
where the time goes in v2:
time: 143 us; the launch traced here: 142 us
  starting transfers between devices  59.5 us (42%)
  Pallas kernels  37.9 us (27%)
  waiting for transfers between devices  33.1 us (23%)
  local copies, waits for them, and re-layouts  7.97 us (6%)
  other arithmetic  2.29 us (2%)
    ppermute x31, starting transfers between devices, permute(): return lax.ppermute(value, AXES, pairs)  59.5 us
    ppermute x31, waiting for transfers between devices, permute(): return lax.ppermute(value, AXES, pairs)  33.1 us
    pallas_call x1, Pallas kernels, input_grad(): pl.pallas_call(input_grad_kernel, grid=(width // block,), in_specs=[pl.Bl...  8.21 us
    unnamed x30, local copies, waits for them, and re-layouts  7.55 us
    pallas_call x1, Pallas kernels, queries(): pl.pallas_call(queries_kernel, grid=(cols // block,), in_specs=[pl.BlockS...  7.51 us
    pallas_call x2, Pallas kernels, weight_grad(): pl.pallas_call(weight_grad_kernel, grid=(cols // block,), in_specs=specs,...  6.9 us
    pallas_call x1, Pallas kernels, keys(): pl.pallas_call(keys_kernel, grid=(cols // block,), in_specs=[pl.BlockSpec...  4.94 us
    pallas_call x1, Pallas kernels, project_kv(): pl.pallas_call(project_kv_kernel, grid=(cols // block,), in_specs=[pl.Blo...  4.88 us
  transfers between devices with their start and end apart: 31, of which 13 were waited for; matrix products, arithmetic and copies ran while one was open for 1% of the time, Pallas kernels for 23%

profile of v2, /device:TPU:6, one launch (start us, length us, event | category | flops | bytes accessed | tf_op | source)
XLA Modules:
  0.0 141.8 jit_solution(7286191600166834024)
XLA Ops:
  0.6 1.2 copy-done
  1.9 0.7 copy-done.3
  2.5 4.9 %project_kv.1 = (bf16[2,256,768]{2,1,0:T(8,128)(2,1)S(1)}, f32[256,768]{1,0:T(8,128)S(1)}) custom-call(bf16[256,2048]{1,0:T(8,128)(2,1)S(1)} %bitcast.21, bf16[3,2048,768]{2,1,0:T(8,128)(2,1)} %bitcast.29, bf16[3,2048,768]{2,1,0:T(8,128)(2,1)} %bitcast.30, f32[1,128]{1,0:T(1,128)S(1)} %bitcast.25), custom_call_target="tpu_custom_call" | custom-call | flops 1610612736 | bytes 6291456 | tf_op jit(solution)/shard_map/project_kv/pallas_call | solution.py:101
  7.4 2.8 %collective-permute-start = (bf16[2,256,768]{2,1,0:T(8,128)(2,1)S(1)}, bf16[2,256,768]{2,1,0:T(8,128)(2,1)}, u32[]{:S(2)}, u32[]{:S(2)}) collective-permute-start(bf16[2,256,768]{2,1,0:T(8,128)(2,1)S(1)} %get-tuple-element.52.own_ref.kv_ref), channel_id=1, source_target_pairs={{0,2},{1,3},{2,4},{3,5},{4,6},{5,7},{6,8},{7,9},{8,10},{9,11},{10,... | collective-permute-start | bytes 2359304 | tf_op jit(solution)/shard_map/ppermute | solution.py:34
  10.2 1.3 collective-permute-start.1
  11.5 3.7 %project_q.1 = (bf16[2,256,768]{2,1,0:T(8,128)(2,1)S(1)}, f32[256,768]{1,0:T(8,128)S(1)}) custom-call(bf16[256,2048]{1,0:T(8,128)(2,1)S(1)} %bitcast.22, bf16[3,2048,768]{2,1,0:T(8,128)(2,1)} %bitcast.31, f32[1,128]{1,0:T(1,128)S(1)} %bitcast.27, bf16[256,768]{1,0:T(8,128)(2,1)S(1)} %bitcast.24), custom_call_target="tpu_custom_call" | custom-call | flops 805306368 | bytes 3145728 | tf_op jit(solution)/shard_map/project_q/pallas_call | solution.py:137
  15.2 0.9 copy-done.6
  16.1 4.4 %collective-permute-start.7 = (bf16[2,256,768]{2,1,0:T(8,128)(2,1)S(1)}, bf16[2,256,768]{2,1,0:T(8,128)(2,1)}, u32[]{:S(2)}, u32[]{:S(2)}) collective-permute-start(bf16[2,256,768]{2,1,0:T(8,128)(2,1)S(1)} %get-tuple-element.56.qg_ref.own_ref), channel_id=1, source_target_pairs={{0,2},{1,3},{2,4},{3,5},{4,6},{5,7},{6,8},{7,9},{8,10},{9,11},{10,... | collective-permute-start | bytes 2359304 | tf_op jit(solution)/shard_map/ppermute | solution.py:34
  20.5 1.3 collective-permute-start.8
  21.9 1.8 %spread_rows.1 = (bf16[2,512,256]{2,1,0:T(8,128)(2,1)}, bf16[512,256]{1,0:T(8,128)(2,1)S(1)}, bf16[512,256]{1,0:T(8,128)(2,1)S(1)}, bf16[512,256]{1,0:T(8,128)(2...) custom-call(s32[5]{0:T(128)S(1)} %stack.35.place_ref, bf16[256,2048]{1,0:T(8,128)(2,1)S(1)} %bitcast.23), custom_call_target="tpu_custom_call" | custom-call | bytes 3145728 | tf_op jit(solution)/shard_map/spread_rows/pallas_call | solution.py:196
  23.7 0.8 copy-done.8
  24.5 0.7 copy-done.10
  25.2 0.7 copy-done.11
  25.9 0.7 copy-done.12
  26.6 0.7 copy-done.13
  27.4 1.5 %collective-permute-start.2 = (bf16[2,512,256]{2,1,0:T(8,128)(2,1)}, bf16[2,512,256]{2,1,0:T(8,128)(2,1)}, u32[]{:S(2)}, u32[]{:S(2)}) collective-permute-start(bf16[2,512,256]{2,1,0:T(8,128)(2,1)} %get-tuple-element.63), channel_id=1, source_target_pairs={{0,2},{1,3},{2,0},{3,1},{4,6},{5,7},{6,4},{7,5},{8,10},{9,11},{10,... | collective-permute-start | bytes 1572872 | tf_op jit(solution)/shard_map/ppermute | solution.py:34
  28.9 0.1 compare_reduce_fusion.1
  29.1 0.1 compare_reduce_fusion
  29.4 0.9 collective-permute-start.3
  30.3 0.5 collective-permute-start.4
  30.9 1.1 copy-done.7
  32.0 7.5 %queries.1 = (bf16[256,768]{1,0:T(8,128)(2,1)}, bf16[256,768]{1,0:T(8,128)(2,1)S(1)}, f32[6,8,256]{2,1,0:T(8,128)S(1)}) custom-call(f32[8,768]{1,0:T(8,128)S(1)} %reshape.45.mask_ref, bf16[2,256,768]{2,1,0:T(8,128)(2,1)S(1)} %get-tuple-element.56.qg_ref.own_ref, f32[256,768]{1,0:T(8,128)S(1)} %copy-done.7, f32[1,128]{1,0:T(1,128)S(1)} %bitcast.28, ...), custom_call_target="tpu_custom_call" | custom-call | flops 1207959552 | bytes 3932160 | tf_op jit(solution)/shard_map/queries/pallas_call | solution.py:255
  39.5 3.1 %collective-permute-done.4.refs_3_ = bf16[512,256]{1,0:T(8,128)(2,1)S(1)} collective-permute-done((bf16[512,256]{1,0:T(8,128)(2,1)}, bf16[512,256]{1,0:T(8,128)(2,1)S(1)}, u32[]{:S(2)}, u32[]{:S(2)}) %collective-permute-start.4) | collective-permute-done | bytes 262176 | tf_op jit(solution)/shard_map/ppermute | solution.py:34
  42.6 2.7 %collective-permute-start.5 = (f32[6,8,256]{2,1,0:T(8,128)S(1)}, f32[6,8,256]{2,1,0:T(8,128)S(1)}, u32[]{:S(2)}, u32[]{:S(2)}) collective-permute-start(f32[6,8,256]{2,1,0:T(8,128)S(1)} %get-tuple-element.67.so_ref), channel_id=1, source_target_pairs={{0,2},{1,3},{2,4},{3,5},{4,6},{5,7},{6,8},{7,9},{8,10},{9,11},{10,... | collective-permute-start | bytes 147464 | tf_op jit(solution)/shard_map/ppermute | solution.py:34
  45.3 1.3 collective-permute-start.6
  46.6 4.4 %collective-permute-start.9 = (bf16[512,256]{1,0:T(8,128)(2,1)}, bf16[512,256]{1,0:T(8,128)(2,1)S(1)}, u32[]{:S(2)}, u32[]{:S(2)}) collective-permute-start(bf16[512,256]{1,0:T(8,128)(2,1)} %copy-done.11), channel_id=1, source_target_pairs={{0,4},{1,5},{2,6},{3,7},{4,0},{5,1},{6,2},{7,3},{8,12},{9,13},{10,... | collective-permute-start | bytes 786440 | tf_op jit(solution)/shard_map/ppermute | solution.py:34
  51.0 2.9 %collective-permute-start.10 = (bf16[512,256]{1,0:T(8,128)(2,1)}, bf16[512,256]{1,0:T(8,128)(2,1)S(1)}, u32[]{:S(2)}, u32[]{:S(2)}) collective-permute-start(bf16[512,256]{1,0:T(8,128)(2,1)} %copy-done.10), channel_id=1, source_target_pairs={{0,6},{1,7},{2,4},{3,5},{4,2},{5,3},{6,0},{7,1},{8,14},{9,15},{10,... | collective-permute-start | bytes 786440 | tf_op jit(solution)/shard_map/ppermute | solution.py:34
  53.9 4.9 %keys.1 = (bf16[256,1152]{1,0:T(8,128)(2,1)S(1)}, bf16[256,1152]{1,0:T(8,128)(2,1)S(1)}) custom-call(f32[8,768]{1,0:T(8,128)S(1)} %reshape.45.mask_ref, bf16[2,256,768]{2,1,0:T(8,128)(2,1)S(1)} %get-tuple-element.52.own_ref.kv_ref, f32[256,768]{1,0:T(8,128)S(1)} %get-tuple-element.61.raw_ref, f32[1,128]{1,0:T(1,128)S(1)} %bitcast.26, ...), custom_call_target="tpu_custom_call" | custom-call | flops 1207959552 | bytes 4718592 | tf_op jit(solution)/shard_map/keys/pallas_call | solution.py:318
  58.8 0.2 collective-permute-done.9.refs_2_
  59.0 4.1 %collective-permute-done.10.refs_3_ = bf16[512,256]{1,0:T(8,128)(2,1)S(1)} collective-permute-done((bf16[512,256]{1,0:T(8,128)(2,1)}, bf16[512,256]{1,0:T(8,128)(2,1)S(1)}, u32[]{:S(2)}, u32[]{:S(2)}) %collective-permute-start.10) | collective-permute-done | bytes 262176 | tf_op jit(solution)/shard_map/ppermute | solution.py:34
  63.1 0.8 collective-permute-start.11
  63.9 0.8 collective-permute-start.12
  64.8 0.3 collective-permute-start.13
  65.0 0.2 collective-permute-start.14
  65.3 8.2 %input_grad.1 = (f32[128,2048]{1,0:T(8,128)S(1)}, bf16[128,2048]{1,0:T(8,128)(2,1)S(1)}) custom-call(s32[5]{0:T(128)S(1)} %stack.35.place_ref, bf16[256,1152]{1,0:T(8,128)(2,1)S(1)} %get-tuple-element.78.da_ref.refs_4_, bf16[256,1152]{1,0:T(8,128)(2,1)S(1)} %get-tuple-element.79.db_ref.refs_4_, bf16[3,2048,768]{2,1,0:T(8,128)(2,1)} %bitcast.32), custom_call_target="tpu_custom_call" | custom-call | flops 2415919104 | bytes 9437184 | tf_op jit(solution)/shard_map/input_grad/pallas_call | solution.py:358
  73.5 5.4 %collective-permute-done.11.refs_6_ = bf16[256,1152]{1,0:T(8,128)(2,1)S(1)} collective-permute-done((bf16[256,1152]{1,0:T(8,128)(2,1)S(1)}, bf16[256,1152]{1,0:T(8,128)(2,1)S(1)}, u32[]{:S(2)}, u32[]{:S(2)}) %collective-permute-start.11) | collective-permute-done | bytes 589856 | tf_op jit(solution)/shard_map/ppermute | solution.py:34
  78.9 0.5 collective-permute-done.12.refs_6_
  79.5 0.5 collective-permute-start.22
  80.0 1.5 %collective-permute-done.16.refs_7_ = bf16[256,1152]{1,0:T(8,128)(2,1)S(1)} collective-permute-done((bf16[256,1152]{1,0:T(8,128)(2,1)S(1)}, bf16[256,1152]{1,0:T(8,128)(2,1)S(1)}, u32[]{:S(2)}, u32[]{:S(2)}) %collective-permute-start.16) | collective-permute-done | bytes 589856 | tf_op jit(solution)/shard_map/ppermute | solution.py:34
  81.5 3.5 %weight_grad.2 = (bf16[128,1152]{1,0:T(8,128)(2,1)S(1)}, bf16[128,1152]{1,0:T(8,128)(2,1)S(1)}, bf16[128,1152]{1,0:T(8,128)(2,1)S(1)}, bf16[128,1152]{1,0:T(8,128)(2,1)S(1)}) custom-call(bf16[2,512,256]{2,1,0:T(8,128)(2,1)S(1)} %copy-done.9, bf16[2,512,256]{2,1,0:T(8,128)(2,1)} %collective-permute-done.2.refs_1_, ...), custom_call_target="tpu_custom_call" | custom-call | flops 1207959552 | bytes 4718592 | tf_op jit(solution)/shard_map/weight_grad/pallas_call | solution.py:401
  85.0 8.1 %collective-permute-start.19 = (bf16[128,1152]{1,0:T(8,128)(2,1)S(1)}, bf16[128,1152]{1,0:T(8,128)(2,1)S(1)}, u32[]{:S(2)}, u32[]{:S(2)}) collective-permute-start(bf16[128,1152]{1,0:T(8,128)(2,1)S(1)} %get-tuple-element.92), channel_id=1, source_target_pairs={{0,12},{1,13},{2,14},{3,15},{4,8},{5,9},{6,10},{7,11},{8,4},{9,5},... | collective-permute-start | bytes 884744 | tf_op jit(solution)/shard_map/ppermute | solution.py:34
  93.1 3.7 %collective-permute-start.15 = (bf16[128,2048]{1,0:T(8,128)(2,1)S(1)}, bf16[128,2048]{1,0:T(8,128)(2,1)S(1)}, u32[]{:S(2)}, u32[]{:S(2)}) collective-permute-start(bf16[128,2048]{1,0:T(8,128)(2,1)S(1)} %get-tuple-element.82), channel_id=1, source_target_pairs={{0,1},{1,0},{2,3},{3,2},{4,5},{5,4},{6,7},{7,6},{8,9},{9,8},{10,11... | collective-permute-start | bytes 1572872 | tf_op jit(solution)/shard_map/ppermute | solution.py:34
  96.8 0.4 collective-permute-start.17
  97.2 3.5 %weight_grad.3 = (bf16[128,1152]{1,0:T(8,128)(2,1)S(1)}, bf16[128,1152]{1,0:T(8,128)(2,1)S(1)}, bf16[128,1152]{1,0:T(8,128)(2,1)S(1)}, bf16[128,1152]{1,0:T(8,128)(2,1)S(1)}) custom-call(bf16[2,512,256]{2,1,0:T(8,128)(2,1)S(1)} %copy-done.9, bf16[2,512,256]{2,1,0:T(8,128)(2,1)} %collective-permute-done.2.refs_1_, ...), custom_call_target="tpu_custom_call" | custom-call | flops 1207959552 | bytes 4718592 | tf_op jit(solution)/shard_map/weight_grad/pallas_call | solution.py:401
  100.7 0.4 collective-permute-start.25
  101.1 1.0 collective-permute-start.23
  102.1 1.8 %collective-permute-start.20 = (bf16[64,1152]{1,0:T(8,128)(2,1)S(1)}, bf16[64,1152]{1,0:T(8,128)(2,1)S(1)}, u32[]{:S(2)}, u32[]{:S(2)}) collective-permute-start(bf16[64,1152]{1,0:T(8,128)(2,1)S(1)} %add_convert_fusion.7), channel_id=1, source_target_pairs={{0,4},{1,5},{2,6},{3,7},{4,0},{5,1},{6,2},{7,3},{8,12},{9,13},{10,... | collective-permute-start | bytes 442376 | tf_op jit(solution)/shard_map/ppermute | solution.py:34
  103.9 2.9 %collective-permute-done.17 = bf16[128,1152]{1,0:T(8,128)(2,1)S(1)} collective-permute-done((bf16[128,1152]{1,0:T(8,128)(2,1)S(1)}, bf16[128,1152]{1,0:T(8,128)(2,1)S(1)}, u32[]{:S(2)}, u32[]{:S(2)}) %collective-permute-start.17) | collective-permute-done | bytes 294944 | tf_op jit(solution)/shard_map/ppermute | solution.py:34
  106.8 0.1 collective-permute-start.18
  106.9 3.3 %collective-permute-done.25 = bf16[128,1152]{1,0:T(8,128)(2,1)S(1)} collective-permute-done((bf16[128,1152]{1,0:T(8,128)(2,1)S(1)}, bf16[128,1152]{1,0:T(8,128)(2,1)S(1)}, u32[]{:S(2)}, u32[]{:S(2)}) %collective-permute-start.25) | collective-permute-done | bytes 294944 | tf_op jit(solution)/shard_map/ppermute | solution.py:34
  110.2 0.1 collective-permute-start.26
  110.4 1.7 %collective-permute-start.24 = (bf16[64,1152]{1,0:T(8,128)(2,1)S(1)}, bf16[64,1152]{1,0:T(8,128)(2,1)S(1)}, u32[]{:S(2)}, u32[]{:S(2)}) collective-permute-start(bf16[64,1152]{1,0:T(8,128)(2,1)S(1)} %add_convert_fusion.4), channel_id=1, source_target_pairs={{0,192},{1,193},{2,194},{3,195},{4,196},{5,197},{6,198},{7,199},{8... | collective-permute-start | bytes 442376 | tf_op jit(solution)/shard_map/ppermute | solution.py:34
  112.1 1.7 %collective-permute-start.21 = (bf16[64,1152]{1,0:T(8,128)(2,1)S(1)}, bf16[64,1152]{1,0:T(8,128)(2,1)S(1)}, u32[]{:S(2)}, u32[]{:S(2)}) collective-permute-start(bf16[64,1152]{1,0:T(8,128)(2,1)S(1)} %add_convert_fusion.6), channel_id=1, source_target_pairs={{0,192},{1,193},{2,194},{3,195},{4,196},{5,197},{6,198},{7,199},{8... | collective-permute-start | bytes 442376 | tf_op jit(solution)/shard_map/ppermute | solution.py:34
  113.8 1.6 %collective-permute-done.26 = bf16[64,1152]{1,0:T(8,128)(2,1)S(1)} collective-permute-done((bf16[64,1152]{1,0:T(8,128)(2,1)S(1)}, bf16[64,1152]{1,0:T(8,128)(2,1)S(1)}, u32[]{:S(2)}, u32[]{:S(2)}) %collective-permute-start.26) | collective-permute-done | bytes 147488 | tf_op jit(solution)/shard_map/ppermute | solution.py:34
  115.5 1.1 collective-permute-start.27
  116.6 2.4 %collective-permute-done.21 = bf16[64,1152]{1,0:T(8,128)(2,1)S(1)} collective-permute-done((bf16[64,1152]{1,0:T(8,128)(2,1)S(1)}, bf16[64,1152]{1,0:T(8,128)(2,1)S(1)}, u32[]{:S(2)}, u32[]{:S(2)}) %collective-permute-start.21) | collective-permute-done | bytes 147488 | tf_op jit(solution)/shard_map/ppermute | solution.py:34
  119.0 2.9 %collective-permute-done.27 = bf16[64,1152]{1,0:T(8,128)(2,1)S(1)} collective-permute-done((bf16[64,1152]{1,0:T(8,128)(2,1)S(1)}, bf16[64,1152]{1,0:T(8,128)(2,1)S(1)}, u32[]{:S(2)}, u32[]{:S(2)}) %collective-permute-start.27) | collective-permute-done | bytes 147488 | tf_op jit(solution)/shard_map/ppermute | solution.py:34
  122.0 10.0 %collective-permute-start.30 = (bf16[16,2304]{1,0:T(8,128)(2,1)S(1)}, bf16[16,2304]{1,0:T(8,128)(2,1)S(1)}, u32[]{:S(2)}, u32[]{:S(2)}) collective-permute-start(bf16[16,2304]{1,0:T(8,128)(2,1)S(1)} %get-tuple-element.102), channel_id=1, source_target_pairs={{0,32},{1,33},{2,34},{3,35},{4,36},{5,37},{6,38},{7,39},{8,40},{9,... | collective-permute-start | bytes 221192 | tf_op jit(solution)/shard_map/ppermute | solution.py:34
  132.0 2.5 %collective-permute-start.29 = (bf16[16,2304]{1,0:T(8,128)(2,1)S(1)}, bf16[16,2304]{1,0:T(8,128)(2,1)S(1)}, u32[]{:S(2)}, u32[]{:S(2)}) collective-permute-start(bf16[16,2304]{1,0:T(8,128)(2,1)S(1)} %get-tuple-element.103), channel_id=1, source_target_pairs={{0,48},{1,49},{2,50},{3,51},{4,52},{5,53},{6,54},{7,55},{8,56},{9,... | collective-permute-start | bytes 221192 | tf_op jit(solution)/shard_map/ppermute | solution.py:34
  134.5 0.4 collective-permute-start.28
  134.9 0.9 fusion
  135.9 1.4 collective-permute-done.29
  137.3 3.8 %collective-permute-done.28 = bf16[16,2304]{1,0:T(8,128)(2,1)S(1)} collective-permute-done((bf16[16,2304]{1,0:T(8,128)(2,1)S(1)}, bf16[16,2304]{1,0:T(8,128)(2,1)S(1)}, u32[]{:S(2)}, u32[]{:S(2)}) %collective-permute-start.28) | collective-permute-done | bytes 73760 | tf_op jit(solution)/shard_map/ppermute | solution.py:34
  141.1 0.7 maximum_bitcast_fusion
  (63 shorter events, 1.0 us)
Async XLA Ops:
  0.6 1.2 copy-start
  1.9 0.7 copy-start.3
  2.5 9.0 %copy-start.2 = (bf16[1,256,768]{2,1,0:T(8,128)(2,1)S(1)}, bf16[1,256,768]{2,1,0:T(8,128)(2,1)}, u32[]{:S(2)}) copy-start(bf16[1,256,768]{2,1,0:T(8,128)(2,1)} %param.11) | copy-start | bytes 1179652
  2.5 9.0 %copy-start.5 = (f32[128]{0:T(128)S(1)}, f32[128]{0:T(128)}, u32[]{:S(2)}) copy-start(f32[128]{0:T(128)} %param.8) | copy-start | bytes 1540
  7.4 14.5 %copy-start.1 = (bf16[1,256,2048]{2,1,0:T(8,128)(2,1)S(1)}, bf16[1,256,2048]{2,1,0:T(8,128)(2,1)}, u32[]{:S(2)}) copy-start(bf16[1,256,2048]{2,1,0:T(8,128)(2,1)} %param.6) | copy-start | bytes 3145732
  7.4 21.4 %copy-start.14 = (s32[128,9]{0,1:T(8,128)S(1)}, s32[128,9]{0,1:T(8,128)}, u32[]{:S(2)}) copy-start(s32[128,9]{0,1:T(8,128)} %param.10) | copy-start | bytes 13828
  7.4 46.5 %copy-start.4 = (f32[128]{0:T(128)S(1)}, f32[128]{0:T(128)}, u32[]{:S(2)}) copy-start(f32[128]{0:T(128)} %param.9) | copy-start | bytes 1540
  7.4 22.0 %collective-permute-start = (bf16[2,256,768]{2,1,0:T(8,128)(2,1)S(1)}, bf16[2,256,768]{2,1,0:T(8,128)(2,1)}, u32[]{:S(2)}, u32[]{:S(2)}) collective-permute-start(bf16[2,256,768]{2,1,0:T(8,128)(2,1)S(1)} %get-tuple-element.52.own_ref.kv_ref), channel_id=1, source_target_pairs={{0,2},{1,3},{2,4},{3,5},{4,6},{5,7},{6,8},{7,9},{8,10},{9,11},{10,... | collective-permute-start | bytes 2359304 | tf_op jit(solution)/shard_map/ppermute | solution.py:34
  10.2 19.2 %collective-permute-start.1 = (bf16[2,256,768]{2,1,0:T(8,128)(2,1)S(1)}, bf16[2,256,768]{2,1,0:T(8,128)(2,1)}, u32[]{:S(2)}, u32[]{:S(2)}) collective-permute-start(bf16[2,256,768]{2,1,0:T(8,128)(2,1)S(1)} %get-tuple-element.52.own_ref.kv_ref), channel_id=1, source_target_pairs={{2,0},{3,1},{4,2},{5,3},{6,4},{7,5},{8,6},{9,7},{10,8},{11,9},{12,... | collective-permute-start | bytes 2359304 | tf_op jit(solution)/shard_map/ppermute | solution.py:34
  15.2 0.9 copy-start.6
  16.1 34.9 %collective-permute-start.7 = (bf16[2,256,768]{2,1,0:T(8,128)(2,1)S(1)}, bf16[2,256,768]{2,1,0:T(8,128)(2,1)}, u32[]{:S(2)}, u32[]{:S(2)}) collective-permute-start(bf16[2,256,768]{2,1,0:T(8,128)(2,1)S(1)} %get-tuple-element.56.qg_ref.own_ref), channel_id=1, source_target_pairs={{0,2},{1,3},{2,4},{3,5},{4,6},{5,7},{6,8},{7,9},{8,10},{9,11},{10,... | collective-permute-start | bytes 2359304 | tf_op jit(solution)/shard_map/ppermute | solution.py:34
  20.5 30.5 %collective-permute-start.8 = (bf16[2,256,768]{2,1,0:T(8,128)(2,1)S(1)}, bf16[2,256,768]{2,1,0:T(8,128)(2,1)}, u32[]{:S(2)}, u32[]{:S(2)}) collective-permute-start(bf16[2,256,768]{2,1,0:T(8,128)(2,1)S(1)} %get-tuple-element.56.qg_ref.own_ref), channel_id=1, source_target_pairs={{2,0},{3,1},{4,2},{5,3},{6,4},{7,5},{8,6},{9,7},{10,8},{11,9},{12,... | collective-permute-start | bytes 2359304 | tf_op jit(solution)/shard_map/ppermute | solution.py:34
  23.7 0.8 copy-start.8
  24.5 0.7 copy-start.10
  25.2 0.7 copy-start.11
  25.9 0.7 copy-start.12
  26.6 0.7 copy-start.13
  27.4 12.2 %collective-permute-start.2 = (bf16[2,512,256]{2,1,0:T(8,128)(2,1)}, bf16[2,512,256]{2,1,0:T(8,128)(2,1)}, u32[]{:S(2)}, u32[]{:S(2)}) collective-permute-start(bf16[2,512,256]{2,1,0:T(8,128)(2,1)} %get-tuple-element.63), channel_id=1, source_target_pairs={{0,2},{1,3},{2,0},{3,1},{4,6},{5,7},{6,4},{7,5},{8,10},{9,11},{10,... | collective-permute-start | bytes 1572872 | tf_op jit(solution)/shard_map/ppermute | solution.py:34
  29.4 10.1 %collective-permute-start.3 = (bf16[512,256]{1,0:T(8,128)(2,1)}, bf16[512,256]{1,0:T(8,128)(2,1)S(1)}, u32[]{:S(2)}, u32[]{:S(2)}) collective-permute-start(bf16[512,256]{1,0:T(8,128)(2,1)} %copy-done.13), channel_id=1, source_target_pairs={{0,64},{1,65},{2,66},{3,67},{4,68},{5,69},{6,70},{7,71},{8,72},{9,... | collective-permute-start | bytes 786440 | tf_op jit(solution)/shard_map/ppermute | solution.py:34
  30.3 12.3 %collective-permute-start.4 = (bf16[512,256]{1,0:T(8,128)(2,1)}, bf16[512,256]{1,0:T(8,128)(2,1)S(1)}, u32[]{:S(2)}, u32[]{:S(2)}) collective-permute-start(bf16[512,256]{1,0:T(8,128)(2,1)} %copy-done.12), channel_id=1, source_target_pairs={{0,66},{1,67},{2,64},{3,65},{4,70},{5,71},{6,68},{7,69},{8,74},{9,... | collective-permute-start | bytes 786440 | tf_op jit(solution)/shard_map/ppermute | solution.py:34
  30.9 1.1 copy-start.7
  32.0 49.5 %copy-start.9 = (bf16[2,512,256]{2,1,0:T(8,128)(2,1)S(1)}, bf16[2,512,256]{2,1,0:T(8,128)(2,1)}, u32[]{:S(2)}) copy-start(bf16[2,512,256]{2,1,0:T(8,128)(2,1)} %copy-done.8) | copy-start | bytes 1572868
  42.6 8.3 %collective-permute-start.5 = (f32[6,8,256]{2,1,0:T(8,128)S(1)}, f32[6,8,256]{2,1,0:T(8,128)S(1)}, u32[]{:S(2)}, u32[]{:S(2)}) collective-permute-start(f32[6,8,256]{2,1,0:T(8,128)S(1)} %get-tuple-element.67.so_ref), channel_id=1, source_target_pairs={{0,2},{1,3},{2,4},{3,5},{4,6},{5,7},{6,8},{7,9},{8,10},{9,11},{10,... | collective-permute-start | bytes 147464 | tf_op jit(solution)/shard_map/ppermute | solution.py:34
  45.3 5.7 %collective-permute-start.6 = (f32[6,8,256]{2,1,0:T(8,128)S(1)}, f32[6,8,256]{2,1,0:T(8,128)S(1)}, u32[]{:S(2)}, u32[]{:S(2)}) collective-permute-start(f32[6,8,256]{2,1,0:T(8,128)S(1)} %get-tuple-element.67.so_ref), channel_id=1, source_target_pairs={{2,0},{3,1},{4,2},{5,3},{6,4},{7,5},{8,6},{9,7},{10,8},{11,9},{12,... | collective-permute-start | bytes 147464 | tf_op jit(solution)/shard_map/ppermute | solution.py:34
  46.6 12.5 %collective-permute-start.9 = (bf16[512,256]{1,0:T(8,128)(2,1)}, bf16[512,256]{1,0:T(8,128)(2,1)S(1)}, u32[]{:S(2)}, u32[]{:S(2)}) collective-permute-start(bf16[512,256]{1,0:T(8,128)(2,1)} %copy-done.11), channel_id=1, source_target_pairs={{0,4},{1,5},{2,6},{3,7},{4,0},{5,1},{6,2},{7,3},{8,12},{9,13},{10,... | collective-permute-start | bytes 786440 | tf_op jit(solution)/shard_map/ppermute | solution.py:34
  51.0 12.2 %collective-permute-start.10 = (bf16[512,256]{1,0:T(8,128)(2,1)}, bf16[512,256]{1,0:T(8,128)(2,1)S(1)}, u32[]{:S(2)}, u32[]{:S(2)}) collective-permute-start(bf16[512,256]{1,0:T(8,128)(2,1)} %copy-done.10), channel_id=1, source_target_pairs={{0,6},{1,7},{2,4},{3,5},{4,2},{5,3},{6,0},{7,1},{8,14},{9,15},{10,... | collective-permute-start | bytes 786440 | tf_op jit(solution)/shard_map/ppermute | solution.py:34
  63.1 15.8 %collective-permute-start.11 = (bf16[256,1152]{1,0:T(8,128)(2,1)S(1)}, bf16[256,1152]{1,0:T(8,128)(2,1)S(1)}, u32[]{:S(2)}, u32[]{:S(2)}) collective-permute-start(bf16[256,1152]{1,0:T(8,128)(2,1)S(1)} %get-tuple-element.78.da_ref.refs_4_), channel_id=1, source_target_pairs={{0,64},{1,65},{2,66},{3,67},{4,68},{5,69},{6,70},{7,71},{8,72},{9,... | collective-permute-start | bytes 1769480 | tf_op jit(solution)/shard_map/ppermute | solution.py:34
  63.9 15.5 %collective-permute-start.12 = (bf16[256,1152]{1,0:T(8,128)(2,1)S(1)}, bf16[256,1152]{1,0:T(8,128)(2,1)S(1)}, u32[]{:S(2)}, u32[]{:S(2)}) collective-permute-start(bf16[256,1152]{1,0:T(8,128)(2,1)S(1)} %get-tuple-element.79.db_ref.refs_4_), channel_id=1, source_target_pairs={{0,4},{1,5},{2,6},{3,7},{4,0},{5,1},{6,2},{7,3},{8,12},{9,13},{10,... | collective-permute-start | bytes 1769480 | tf_op jit(solution)/shard_map/ppermute | solution.py:34
  64.8 14.7 %collective-permute-start.13 = (bf16[256,1152]{1,0:T(8,128)(2,1)S(1)}, bf16[256,1152]{1,0:T(8,128)(2,1)S(1)}, u32[]{:S(2)}, u32[]{:S(2)}) collective-permute-start(bf16[256,1152]{1,0:T(8,128)(2,1)S(1)} %get-tuple-element.78.da_ref.refs_4_), channel_id=1, source_target_pairs={{0,2},{1,3},{2,0},{3,1},{4,6},{5,7},{6,4},{7,5},{8,10},{9,11},{10,... | collective-permute-start | bytes 1769480 | tf_op jit(solution)/shard_map/ppermute | solution.py:34
  65.0 14.5 %collective-permute-start.14 = (bf16[256,1152]{1,0:T(8,128)(2,1)S(1)}, bf16[256,1152]{1,0:T(8,128)(2,1)S(1)}, u32[]{:S(2)}, u32[]{:S(2)}) collective-permute-start(bf16[256,1152]{1,0:T(8,128)(2,1)S(1)} %get-tuple-element.79.db_ref.refs_4_), channel_id=1, source_target_pairs={{0,2},{1,3},{2,0},{3,1},{4,6},{5,7},{6,4},{7,5},{8,10},{9,11},{10,... | collective-permute-start | bytes 1769480 | tf_op jit(solution)/shard_map/ppermute | solution.py:34
  79.5 2.0 %collective-permute-start.16 = (bf16[256,1152]{1,0:T(8,128)(2,1)S(1)}, bf16[256,1152]{1,0:T(8,128)(2,1)S(1)}, u32[]{:S(2)}, u32[]{:S(2)}) collective-permute-start(bf16[256,1152]{1,0:T(8,128)(2,1)S(1)} %collective-permute-done.11.refs_6_), channel_id=1, source_target_pairs={{0,2},{1,3},{2,0},{3,1},{4,6},{5,7},{6,4},{7,5},{8,10},{9,11},{10,... | collective-permute-start | bytes 1769480 | tf_op jit(solution)/shard_map/ppermute | solution.py:34
  79.5 17.7 %collective-permute-start.22 = (bf16[256,1152]{1,0:T(8,128)(2,1)S(1)}, bf16[256,1152]{1,0:T(8,128)(2,1)S(1)}, u32[]{:S(2)}, u32[]{:S(2)}) collective-permute-start(bf16[256,1152]{1,0:T(8,128)(2,1)S(1)} %collective-permute-done.12.refs_6_), channel_id=1, source_target_pairs={{0,2},{1,3},{2,0},{3,1},{4,6},{5,7},{6,4},{7,5},{8,10},{9,11},{10,... | collective-permute-start | bytes 1769480 | tf_op jit(solution)/shard_map/ppermute | solution.py:34
  85.0 17.1 %collective-permute-start.19 = (bf16[128,1152]{1,0:T(8,128)(2,1)S(1)}, bf16[128,1152]{1,0:T(8,128)(2,1)S(1)}, u32[]{:S(2)}, u32[]{:S(2)}) collective-permute-start(bf16[128,1152]{1,0:T(8,128)(2,1)S(1)} %get-tuple-element.92), channel_id=1, source_target_pairs={{0,12},{1,13},{2,14},{3,15},{4,8},{5,9},{6,10},{7,11},{8,4},{9,5},... | collective-permute-start | bytes 884744 | tf_op jit(solution)/shard_map/ppermute | solution.py:34
  93.1 41.8 %collective-permute-start.15 = (bf16[128,2048]{1,0:T(8,128)(2,1)S(1)}, bf16[128,2048]{1,0:T(8,128)(2,1)S(1)}, u32[]{:S(2)}, u32[]{:S(2)}) collective-permute-start(bf16[128,2048]{1,0:T(8,128)(2,1)S(1)} %get-tuple-element.82), channel_id=1, source_target_pairs={{0,1},{1,0},{2,3},{3,2},{4,5},{5,4},{6,7},{7,6},{8,9},{9,8},{10,11... | collective-permute-start | bytes 1572872 | tf_op jit(solution)/shard_map/ppermute | solution.py:34
  96.8 9.9 %collective-permute-start.17 = (bf16[128,1152]{1,0:T(8,128)(2,1)S(1)}, bf16[128,1152]{1,0:T(8,128)(2,1)S(1)}, u32[]{:S(2)}, u32[]{:S(2)}) collective-permute-start(bf16[128,1152]{1,0:T(8,128)(2,1)S(1)} %get-tuple-element.90), channel_id=1, source_target_pairs={{0,4},{1,5},{2,6},{3,7},{4,0},{5,1},{6,2},{7,3},{8,12},{9,13},{10,... | collective-permute-start | bytes 884744 | tf_op jit(solution)/shard_map/ppermute | solution.py:34
  100.7 9.5 %collective-permute-start.25 = (bf16[128,1152]{1,0:T(8,128)(2,1)S(1)}, bf16[128,1152]{1,0:T(8,128)(2,1)S(1)}, u32[]{:S(2)}, u32[]{:S(2)}) collective-permute-start(bf16[128,1152]{1,0:T(8,128)(2,1)S(1)} %get-tuple-element.100), channel_id=1, source_target_pairs={{0,192},{1,193},{2,194},{3,195},{4,196},{5,197},{6,198},{7,199},{8... | collective-permute-start | bytes 884744 | tf_op jit(solution)/shard_map/ppermute | solution.py:34
  101.1 9.2 %collective-permute-start.23 = (bf16[128,1152]{1,0:T(8,128)(2,1)S(1)}, bf16[128,1152]{1,0:T(8,128)(2,1)S(1)}, u32[]{:S(2)}, u32[]{:S(2)}) collective-permute-start(bf16[128,1152]{1,0:T(8,128)(2,1)S(1)} %get-tuple-element.98), channel_id=1, source_target_pairs={{0,64},{1,65},{2,66},{3,67},{4,68},{5,69},{6,70},{7,71},{8,72},{9,... | collective-permute-start | bytes 884744 | tf_op jit(solution)/shard_map/ppermute | solution.py:34
  102.1 9.9 %collective-permute-start.20 = (bf16[64,1152]{1,0:T(8,128)(2,1)S(1)}, bf16[64,1152]{1,0:T(8,128)(2,1)S(1)}, u32[]{:S(2)}, u32[]{:S(2)}) collective-permute-start(bf16[64,1152]{1,0:T(8,128)(2,1)S(1)} %add_convert_fusion.7), channel_id=1, source_target_pairs={{0,4},{1,5},{2,6},{3,7},{4,0},{5,1},{6,2},{7,3},{8,12},{9,13},{10,... | collective-permute-start | bytes 442376 | tf_op jit(solution)/shard_map/ppermute | solution.py:34
  106.8 9.8 %collective-permute-start.18 = (bf16[64,1152]{1,0:T(8,128)(2,1)S(1)}, bf16[64,1152]{1,0:T(8,128)(2,1)S(1)}, u32[]{:S(2)}, u32[]{:S(2)}) collective-permute-start(bf16[64,1152]{1,0:T(8,128)(2,1)S(1)} %add_convert_fusion.8), channel_id=1, source_target_pairs={{0,12},{1,13},{2,14},{3,15},{4,8},{5,9},{6,10},{7,11},{8,4},{9,5},... | collective-permute-start | bytes 442376 | tf_op jit(solution)/shard_map/ppermute | solution.py:34
  110.2 5.2 %collective-permute-start.26 = (bf16[64,1152]{1,0:T(8,128)(2,1)S(1)}, bf16[64,1152]{1,0:T(8,128)(2,1)S(1)}, u32[]{:S(2)}, u32[]{:S(2)}) collective-permute-start(bf16[64,1152]{1,0:T(8,128)(2,1)S(1)} %add_convert_fusion.3), channel_id=1, source_target_pairs={{0,64},{1,65},{2,66},{3,67},{4,68},{5,69},{6,70},{7,71},{8,72},{9,... | collective-permute-start | bytes 442376 | tf_op jit(solution)/shard_map/ppermute | solution.py:34
  110.4 8.7 %collective-permute-start.24 = (bf16[64,1152]{1,0:T(8,128)(2,1)S(1)}, bf16[64,1152]{1,0:T(8,128)(2,1)S(1)}, u32[]{:S(2)}, u32[]{:S(2)}) collective-permute-start(bf16[64,1152]{1,0:T(8,128)(2,1)S(1)} %add_convert_fusion.4), channel_id=1, source_target_pairs={{0,192},{1,193},{2,194},{3,195},{4,196},{5,197},{6,198},{7,199},{8... | collective-permute-start | bytes 442376 | tf_op jit(solution)/shard_map/ppermute | solution.py:34
  112.1 6.8 %collective-permute-start.21 = (bf16[64,1152]{1,0:T(8,128)(2,1)S(1)}, bf16[64,1152]{1,0:T(8,128)(2,1)S(1)}, u32[]{:S(2)}, u32[]{:S(2)}) collective-permute-start(bf16[64,1152]{1,0:T(8,128)(2,1)S(1)} %add_convert_fusion.6), channel_id=1, source_target_pairs={{0,192},{1,193},{2,194},{3,195},{4,196},{5,197},{6,198},{7,199},{8... | collective-permute-start | bytes 442376 | tf_op jit(solution)/shard_map/ppermute | solution.py:34
  115.5 6.4 %collective-permute-start.27 = (bf16[64,1152]{1,0:T(8,128)(2,1)S(1)}, bf16[64,1152]{1,0:T(8,128)(2,1)S(1)}, u32[]{:S(2)}, u32[]{:S(2)}) collective-permute-start(bf16[64,1152]{1,0:T(8,128)(2,1)S(1)} %add_convert_fusion.2), channel_id=1, source_target_pairs={{0,12},{1,13},{2,14},{3,15},{4,8},{5,9},{6,10},{7,11},{8,4},{9,5},... | collective-permute-start | bytes 442376 | tf_op jit(solution)/shard_map/ppermute | solution.py:34
  122.0 13.8 %collective-permute-start.30 = (bf16[16,2304]{1,0:T(8,128)(2,1)S(1)}, bf16[16,2304]{1,0:T(8,128)(2,1)S(1)}, u32[]{:S(2)}, u32[]{:S(2)}) collective-permute-start(bf16[16,2304]{1,0:T(8,128)(2,1)S(1)} %get-tuple-element.102), channel_id=1, source_target_pairs={{0,32},{1,33},{2,34},{3,35},{4,36},{5,37},{6,38},{7,39},{8,40},{9,... | collective-permute-start | bytes 221192 | tf_op jit(solution)/shard_map/ppermute | solution.py:34
  132.0 5.3 %collective-permute-start.29 = (bf16[16,2304]{1,0:T(8,128)(2,1)S(1)}, bf16[16,2304]{1,0:T(8,128)(2,1)S(1)}, u32[]{:S(2)}, u32[]{:S(2)}) collective-permute-start(bf16[16,2304]{1,0:T(8,128)(2,1)S(1)} %get-tuple-element.103), channel_id=1, source_target_pairs={{0,48},{1,49},{2,50},{3,51},{4,52},{5,53},{6,54},{7,55},{8,56},{9,... | collective-permute-start | bytes 221192 | tf_op jit(solution)/shard_map/ppermute | solution.py:34
  134.5 6.5 %collective-permute-start.28 = (bf16[16,2304]{1,0:T(8,128)(2,1)S(1)}, bf16[16,2304]{1,0:T(8,128)(2,1)S(1)}, u32[]{:S(2)}, u32[]{:S(2)}) collective-permute-start(bf16[16,2304]{1,0:T(8,128)(2,1)S(1)} %get-tuple-element.101), channel_id=1, source_target_pairs={{0,16},{1,17},{2,18},{3,19},{4,20},{5,21},{6,22},{7,23},{8,24},{9,... | collective-permute-start | bytes 221192 | tf_op jit(solution)/shard_map/ppermute | solution.py:34

commit v3 on v2

--- a/solution.py
+++ b/solution.py
@@ -16,7 +16,6 @@
 AXES = ("dp", "seq", "head")
 SCALE = 1.0 / math.sqrt(HD)
 EXP2_SCALE = SCALE * math.log2(math.e)
-VMEM_LIMIT = 48 * 1024 * 1024
 
 
 def permute(value, target):
@@ -24,10 +23,7 @@
     for x in range(4):
         for seq in range(32):
             for head in range(2):
-                place = target(x, seq // 8, (seq // 2) % 4, seq % 2, head)
-                if place is None:
-                    continue
-                x2, zh2, y2, c2, h2 = place
+                x2, zh2, y2, c2, h2 = target(x, seq // 8, (seq // 2) % 4, seq % 2, head)
                 pairs.append(
                     (x * 64 + seq * 2 + head, x2 * 64 + (zh2 * 8 + y2 * 2 + c2) * 2 + h2)
                 )
@@ -38,22 +34,13 @@
     return lax.optimization_barrier(values)
 
 
-def to_slab(step):
-    def target(x, zh, y, c, h):
-        seq = zh * 8 + y * 2 + c + step
-        if not 0 <= seq < 32:
-            return None
-        return (x, seq // 8, (seq // 2) % 4, seq % 2, h)
-
-    return target
-
-
-def to_x(step):
-    return lambda x, zh, y, c, h: ((x + step) % 4, zh, y, c, h)
-
-
-def to_y(step):
-    return lambda x, zh, y, c, h: (x, zh, (y + step) % 4, c, h)
+def to_mate(x, zh, y, c, h):
+    return (x, zh, y, 1 - c, h)
+
+
+def to_far(x, zh, y, c, h):
+    seq = (zh * 8 + y * 2 + c + (1 if c else -1)) % 32
+    return (x, seq // 8, (seq // 2) % 4, seq % 2, h)
 
 
 def to_z(step):
@@ -64,8 +51,8 @@
     return lambda x, zh, y, c, h: (x ^ x_bits, zh, y ^ y_bits, c ^ core, h ^ head)
 
 
-def params(**more):
-    return pltpu.CompilerParams(vmem_limit_bytes=VMEM_LIMIT, **more)
+def params(mib):
+    return pltpu.CompilerParams(vmem_limit_bytes=mib * 1024 * 1024)
 
 
 def cost(flops, moved, trans=0):
@@ -115,7 +102,7 @@
             jax.ShapeDtypeStruct((2, rows, cols), BF16),
             jax.ShapeDtypeStruct((rows, cols), F32),
         ],
-        compiler_params=params(),
+        compiler_params=params(48),
         cost_estimate=cost(4 * rows * width * cols, 4 * width * cols),
         name="project_kv",
     )(x, w, w, gain)
@@ -151,14 +138,19 @@
             jax.ShapeDtypeStruct((2, rows, cols), BF16),
             jax.ShapeDtypeStruct((rows, cols), F32),
         ],
-        compiler_params=params(),
+        compiler_params=params(48),
         cost_estimate=cost(2 * rows * width * cols, 2 * width * cols),
         name="project_q",
     )(x, w, gain, g)
 
 
 def spread_rows_kernel(place_ref, x_ref, core_ref, a0_ref, a1_ref, b0_ref, b1_ref, own_ref, xt_ref):
-    xt_ref[...] = x_ref[...].T
+    step = pl.program_id(0)
+
+    @pl.when(step == 0)
+    def _():
+        xt_ref[...] = x_ref[...].T
+
     x = place_ref[0]
     zh = place_ref[1]
     y = place_ref[2]
@@ -167,11 +159,11 @@
     def source(xx, zz, yy, cc):
         return xt_ref[pl.ds(pl.multiple_of((((xx * 4 + zz) * 4 + yy) * 2 + cc) * 16, 16), 16), :]
 
-    for part, (s, order) in enumerate(((0, (0, 3)), (0, (1, 2)), (1, (0, 1)), (1, (3, 2)))):
+    def fill(s, order):
         for k in range(2):
             for m in range(4):
                 zz = lax.rem(zh + m, 4)
-                row = ((part * 2 + k) * 4 + m) * 16
+                row = (k * 4 + m) * 16
                 rows = slice(row, row + 16)
                 for near in range(2):
                     pair = (0, 3)[s] ^ (1 - near)
@@ -186,20 +178,28 @@
                             (a0_ref, a1_ref)[cc][rows, :] = from_a
                             (b0_ref, b1_ref)[cc][rows, :] = from_b
 
+    for part, (s, order) in enumerate(((0, (0, 3)), (0, (1, 2)), (1, (0, 1)), (1, (3, 2)))):
+        pl.when(step == part)(functools.partial(fill, s, order))
+
 
 def spread_rows(x, place):
     tokens, width = x.shape
     rows = width // 4
     one = jax.ShapeDtypeStruct((rows, tokens), BF16)
     two = jax.ShapeDtypeStruct((2, rows, tokens), BF16)
-    vmem = pl.BlockSpec(memory_space=pltpu.VMEM)
+    one_spec = pl.BlockSpec((rows // 4, tokens), lambda i: (i, 0))
+    two_spec = pl.BlockSpec((2, rows // 4, tokens), lambda i: (0, i, 0))
     return pl.pallas_call(
         spread_rows_kernel,
-        in_specs=[pl.BlockSpec(memory_space=pltpu.SMEM), vmem],
-        out_specs=[vmem] * 6,
+        grid=(4,),
+        in_specs=[
+            pl.BlockSpec(memory_space=pltpu.SMEM),
+            pl.BlockSpec((tokens, width), lambda i: (0, 0)),
+        ],
+        out_specs=[two_spec, one_spec, one_spec, one_spec, one_spec, two_spec],
         out_shape=[two, one, one, one, one, two],
         scratch_shapes=[pltpu.VMEM((width, tokens), BF16)],
-        compiler_params=params(),
+        compiler_params=params(48),
         cost_estimate=cost(0, 6 * tokens * width),
         name="spread_rows",
     )(place, x)
@@ -220,7 +220,7 @@
 
 
 def queries_kernel(
-    mask_ref, qg_ref, raw_ref, gain_ref, low_ref, own_ref, high_ref,
+    mask_ref, qg_ref, raw_ref, gain_ref, far_ref, own_ref, mate_ref,
     out_ref, dq_ref, stats_ref, full_ref,
 ):
     @pl.when(pl.program_id(0) == 0)
@@ -231,8 +231,8 @@
         cols = slice(i * HD, (i + 1) * HD)
         q = qg_ref[0, :, cols]
         g = qg_ref[1, :, cols]
-        keys = jnp.concatenate([low_ref[0, :, cols], own_ref[0, :, cols], high_ref[0, :, cols]], 0)
-        values = jnp.concatenate([low_ref[1, :, cols], own_ref[1, :, cols], high_ref[1, :, cols]], 0)
+        keys = jnp.concatenate([far_ref[0, :, cols], own_ref[0, :, cols], mate_ref[0, :, cols]], 0)
+        values = jnp.concatenate([far_ref[1, :, cols], own_ref[1, :, cols], mate_ref[1, :, cols]], 0)
         expo = jnp.exp2(dot(q, keys, NT) * EXP2_SCALE) * full_ref[...]
         inverse = 1.0 / jnp.sum(expo, axis=-1, keepdims=True)
         probs = expo * inverse
@@ -247,7 +247,7 @@
         stats_ref[i] = both.T[:8, :]
 
 
-def queries(mask, qg, q_raw, gain, low, own, high):
+def queries(mask, qg, q_raw, gain, far, own, mate):
     rows, cols = q_raw.shape
     block = 2 * HD
     flat = pl.BlockSpec((rows, block), lambda i: (0, i))
@@ -271,14 +271,14 @@
             jax.ShapeDtypeStruct((cols // HD, 8, rows), F32),
         ],
         scratch_shapes=[pltpu.VMEM((rows, 3 * rows), F32)],
-        compiler_params=params(),
+        compiler_params=params(48),
         cost_estimate=cost(24 * rows * rows * cols, 20 * rows * cols, 3 * rows * rows * cols // HD),
         name="queries",
-    )(mask, qg, q_raw, gain, low, own, high)
+    )(mask, qg, q_raw, gain, far, own, mate)
 
 
 def keys_kernel(
-    mask_ref, kv_ref, raw_ref, gain_ref, low_ref, own_ref, high_ref,
+    mask_ref, kv_ref, raw_ref, gain_ref, far_ref, own_ref, mate_ref,
     sl_ref, so_ref, sh_ref, dq_ref, da_ref, db_ref, full_ref,
 ):
     step = pl.program_id(0)
@@ -295,8 +295,8 @@
         cols = slice(i * HD, (i + 1) * HD)
         key = kv_ref[0, :, cols]
         value = kv_ref[1, :, cols]
-        q_wide = jnp.concatenate([low_ref[0, :, cols], own_ref[0, :, cols], high_ref[0, :, cols]], 0)
-        g_wide = jnp.concatenate([low_ref[1, :, cols], own_ref[1, :, cols], high_ref[1, :, cols]], 0)
+        q_wide = jnp.concatenate([far_ref[0, :, cols], own_ref[0, :, cols], mate_ref[0, :, cols]], 0)
+        g_wide = jnp.concatenate([far_ref[1, :, cols], own_ref[1, :, cols], mate_ref[1, :, cols]], 0)
         stats = jnp.concatenate([sl_ref[i], so_ref[i], sh_ref[i]], axis=1)
         probs = jnp.exp2(dot(key, q_wide, NT) * EXP2_SCALE) * full_ref[...] * stats[0:1, :]
         d_value = dot(probs.astype(BF16), g_wide, NN)
@@ -330,7 +330,7 @@
         out_specs=[wide, wide],
         out_shape=[jax.ShapeDtypeStruct((rows, cols * 3 // 2), BF16)] * 2,
         scratch_shapes=[pltpu.VMEM((rows, 3 * rows), F32)],
-        compiler_params=params(),
+        compiler_params=params(48),
         cost_estimate=cost(24 * rows * rows * cols, 24 * rows * cols, 3 * rows * rows * cols // HD),
         name="keys",
     )(mask, kv, k_raw, gain, *qg3, *s3, dq)
@@ -370,7 +370,7 @@
             jax.ShapeDtypeStruct((rows // 2, width), BF16),
         ],
         scratch_shapes=[pltpu.VMEM((rows, block), F32)],
-        compiler_params=params(),
+        compiler_params=params(48),
         cost_estimate=cost(6 * rows * width * cols, 6 * width * cols),
         name="input_grad",
     )(place, da, db, w)
@@ -404,7 +404,7 @@
         in_specs=specs,
         out_specs=[pl.BlockSpec((128, block), lambda i: (0, i))] * 4,
         out_shape=[jax.ShapeDtypeStruct((128, cols), BF16)] * 4,
-        compiler_params=params(),
+        compiler_params=params(48),
         cost_estimate=cost(8 * 512 * tokens * cols, 4 * 512 * cols + 8 * tokens * cols),
         name="weight_grad",
     )(*lhs, *rhs)
@@ -413,12 +413,15 @@
 def tile_masks(neighbours, seq):
     tiles = neighbours.shape[0]
     padded = jnp.pad(neighbours, ((4, 4), (0, 0)), constant_values=-1)
-    window = lax.dynamic_slice_in_dim(padded, seq * 4, 12, 0)
-    own = seq * 4 + jnp.arange(4, dtype=jnp.int32)
-    near = seq * 4 - 4 + jnp.arange(12, dtype=jnp.int32)
-    by_query = jnp.any(window[4:8, :, None] == near[None, None, :], axis=1)
-    by_query = by_query & ((near >= 0) & (near < tiles))[None, :]
-    by_key = jnp.any(window[None, :, :] == own[:, None, None], axis=2)
+    core = seq % 2
+    slabs = (seq + 2 * core - 1, seq, seq + 1 - 2 * core)
+    rows = [lax.dynamic_slice_in_dim(padded, (slab + 1) * 4, 4, 0) for slab in slabs]
+    tile = jnp.arange(4, dtype=jnp.int32)
+    ids = jnp.concatenate([slab * 4 + tile for slab in slabs])
+    by_query = jnp.any(rows[1][:, :, None] == ids[None, None, :], axis=1)
+    by_query = by_query & ((ids >= 0) & (ids < tiles))[None, :]
+    window = jnp.concatenate(rows, axis=0)
+    by_key = jnp.any(window[None, :, :] == (seq * 4 + tile)[:, None, None], axis=2)
     both = jnp.concatenate([by_query, by_key], axis=0).astype(F32)
     return jnp.repeat(both, TILE, axis=1)
 
@@ -442,29 +445,29 @@
     k_gain = k_gain.reshape(1, HD)
 
     kv, k_raw = project_kv(x, w, k_gain)
-    kv_low = permute(kv, to_slab(1))
-    kv_high = permute(kv, to_slab(-1))
+    kv_far = permute(kv, to_far)
+    kv_mate = permute(kv, to_mate)
     qg, q_raw = project_q(x, w, q_gain, g)
-    qg_low = permute(qg, to_slab(1))
-    qg_high = permute(qg, to_slab(-1))
+    qg_far = permute(qg, to_far)
+    qg_mate = permute(qg, to_mate)
 
     to_core, to_a0, to_a1, to_b0, to_b1, own_rows = spread_rows(x, place)
     mask = tile_masks(neighbours, seq)
+    to_core, to_a0, to_a1, kv_mate, qg_mate, mask = after(
+        to_core, to_a0, to_a1, kv_mate, qg_mate, mask
+    )
     core_rows = permute(to_core, flip(core=1))
-    kv_low, kv_high, to_a0, to_a1, mask = after(kv_low, kv_high, to_a0, to_a1, mask)
     a0 = permute(to_a0, flip(x_bits=1))
     a1 = permute(to_a1, flip(x_bits=1, core=1))
-
-    attn_out, dq, stats = queries(mask, qg, q_raw, q_gain, kv_low, kv, kv_high)
-    stats, core_rows, a0, a1, to_b0 = after(stats, core_rows, a0, a1, to_b0)
-    s_low = permute(stats, to_slab(1))
-    s_high = permute(stats, to_slab(-1))
+    kv_far, core_rows, to_b0, to_b1 = after(kv_far, core_rows, to_b0, to_b1)
     b0 = permute(to_b0, flip(y_bits=1))
-    s_low, s_high, qg_low, qg_high, to_b1 = after(s_low, s_high, qg_low, qg_high, to_b1)
     b1 = permute(to_b1, flip(y_bits=1, core=1))
-    da, db = keys(
-        mask, kv, k_raw, k_gain, (qg_low, qg, qg_high), (s_low, stats, s_high), dq
-    )
+
+    attn_out, dq, stats = queries(mask, qg, q_raw, q_gain, kv_far, kv, kv_mate)
+    stats, a0, a1 = after(stats, a0, a1)
+    s_far = permute(stats, to_far)
+    s_mate = permute(stats, to_mate)
+    da, db = keys(mask, kv, k_raw, k_gain, (qg_far, qg, qg_mate), (s_far, stats, s_mate), dq)
 
     da, db, b0, b1 = after(da, db, b0, b1)
     dax = permute(da, flip(x_bits=1))

time: 143 us -> 122 us (0.85)
  starting transfers between devices: 59.5 us -> 45.3 us
  waiting for transfers between devices: 33.1 us -> 28.4 us
  Pallas kernels: 37.9 us -> 35.6 us
    ppermute x31, starting transfers between devices: 59.5 us -> 45.3 us  [permute(): return lax.ppermute(value, AXES, pairs)]
    ppermute x31, waiting for transfers between devices: 33.1 us -> 28.4 us  [permute(): return lax.ppermute(value, AXES, pairs)]
    pallas_call x2, Pallas kernels: 6.9 us -> 5.09 us  [weight_grad(): pl.pallas_call(weight_grad_kernel, grid=(cols // block,), in_specs=specs,...]
    unnamed x30 -> x32, local copies, waits for them, and re-layouts: 7.55 us -> 8.28 us
  transfers between devices with their start and end apart: 31 -> 31, of which waited for: 13 -> 12; matrix products, arithmetic and copies ran while one was open for 1% -> 2% of each run, Pallas kernels for 23% -> 25%
where the time goes in v3:
time: 122 us; the launch traced here: 121 us
  starting transfers between devices  45.3 us (37%)
  Pallas kernels  35.6 us (29%)
  waiting for transfers between devices  28.4 us (23%)
  local copies, waits for them, and re-layouts  8.64 us (7%)
  other arithmetic  2.41 us (2%)
    ppermute x31, starting transfers between devices, permute(): return lax.ppermute(value, AXES, pairs)  45.3 us
    ppermute x31, waiting for transfers between devices, permute(): return lax.ppermute(value, AXES, pairs)  28.4 us
    unnamed x32, local copies, waits for them, and re-layouts  8.28 us
    pallas_call x1, Pallas kernels, input_grad(): pl.pallas_call(input_grad_kernel, grid=(width // block,), in_specs=[pl.Bl...  8.17 us
    pallas_call x1, Pallas kernels, queries(): pl.pallas_call(queries_kernel, grid=(cols // block,), in_specs=[pl.BlockS...  7.47 us
    pallas_call x2, Pallas kernels, weight_grad(): pl.pallas_call(weight_grad_kernel, grid=(cols // block,), in_specs=specs,...  5.09 us
    pallas_call x1, Pallas kernels, keys(): pl.pallas_call(keys_kernel, grid=(cols // block,), in_specs=[pl.BlockSpec...  4.94 us
    pallas_call x1, Pallas kernels, project_kv(): pl.pallas_call(project_kv_kernel, grid=(cols // block,), in_specs=[pl.Blo...  4.85 us
  transfers between devices with their start and end apart: 31, of which 12 were waited for; matrix products, arithmetic and copies ran while one was open for 2% of the time, Pallas kernels for 25%

profile of v3, /device:TPU:6, one launch (start us, length us, event | category | flops | bytes accessed | tf_op | source)
XLA Modules:
  0.0 121.3 jit_solution(14245367123672304064)
XLA Ops:
  0.6 1.2 %copy-done = bf16[1,256,2048]{2,1,0:T(8,128)(2,1)S(1)} copy-done((bf16[1,256,2048]{2,1,0:T(8,128)(2,1)S(1)}, bf16[1,256,2048]{2,1,0:T(8,128)(2,1)}, u32[]{:S(2)}) %copy-start) | copy-done | bytes 1048600
  1.9 0.7 copy-done.3
  2.5 4.8 %project_kv.1 = (bf16[2,256,768]{2,1,0:T(8,128)(2,1)S(1)}, f32[256,768]{1,0:T(8,128)S(1)}) custom-call(bf16[256,2048]{1,0:T(8,128)(2,1)S(1)} %bitcast.21, bf16[3,2048,768]{2,1,0:T(8,128)(2,1)} %bitcast.29, bf16[3,2048,768]{2,1,0:T(8,128)(2,1)} %bitcast.30, f32[1,128]{1,0:T(1,128)S(1)} %bitcast.25), custom_call_target="tpu_custom_call" | custom-call | flops 1610612736 | bytes 6291456 | tf_op jit(solution)/shard_map/project_kv/pallas_call | solution.py:88
  7.4 0.1 collective-permute-start
  7.5 8.9 %collective-permute-start.2 = (bf16[2,256,768]{2,1,0:T(8,128)(2,1)S(1)}, bf16[2,256,768]{2,1,0:T(8,128)(2,1)}, u32[]{:S(2)}, u32[]{:S(2)}) collective-permute-start(bf16[2,256,768]{2,1,0:T(8,128)(2,1)S(1)} %get-tuple-element.53.own_ref.kv_ref), channel_id=1, source_target_pairs={{0,62},{1,63},{2,4},{3,5},{4,2},{5,3},{6,8},{7,9},{8,6},{9,7},{10,... | collective-permute-start | bytes 2359304 | tf_op jit(solution)/shard_map/ppermute | solution.py:30
  16.4 3.6 %project_q.1 = (bf16[2,256,768]{2,1,0:T(8,128)(2,1)S(1)}, f32[256,768]{1,0:T(8,128)S(1)}) custom-call(bf16[256,2048]{1,0:T(8,128)(2,1)S(1)} %bitcast.22, bf16[3,2048,768]{2,1,0:T(8,128)(2,1)} %bitcast.31, f32[1,128]{1,0:T(1,128)S(1)} %bitcast.27, bf16[256,768]{1,0:T(8,128)(2,1)S(1)} %bitcast.24), custom_call_target="tpu_custom_call" | custom-call | flops 805306368 | bytes 3145728 | tf_op jit(solution)/shard_map/project_q/pallas_call | solution.py:124
  20.0 0.9 copy-done.6
  20.9 0.9 collective-permute-start.4
  21.8 0.1 pad_dynamic-slice_fusion.1
  21.9 0.1 compare_and_fusion
  21.9 0.1 compare_reduce_fusion.1
  22.0 0.1 pad_add_fusion
  22.1 0.1 stack.35.place_ref
  22.2 1.5 %spread_rows.1 = (bf16[2,512,256]{2,1,0:T(8,128)(2,1)S(1)}, bf16[512,256]{1,0:T(8,128)(2,1)S(1)}, bf16[512,256]{1,0:T(8,128)(2,1)S(1)}, bf16[512,256]{1,0:T(8,12...) custom-call(s32[5]{0:T(128)S(1)} %stack.35.place_ref, bf16[256,2048]{1,0:T(8,128)(2,1)S(1)} %bitcast.23), custom_call_target="tpu_custom_call" | custom-call | bytes 3145728 | tf_op jit(solution)/shard_map/spread_rows/pallas_call | solution.py:192
  23.7 0.8 copy-done.8
  24.5 0.8 copy-done.10
  25.3 0.7 copy-done.11
  26.0 0.7 copy-done.12
  26.7 0.7 copy-done.13
  27.4 0.7 copy-done.14
  28.1 0.1 compare_reduce_fusion
  28.2 0.1 broadcast_in_dim.6
  28.3 0.1 reshape.69.mask_ref
  28.4 0.1 collective-permute-start.3
  28.5 0.9 collective-permute-start.5
  29.4 1.0 collective-permute-start.6
  30.3 5.4 %collective-permute-done.2.far_ref = bf16[2,256,768]{2,1,0:T(8,128)(2,1)} collective-permute-done((bf16[2,256,768]{2,1,0:T(8,128)(2,1)S(1)}, bf16[2,256,768]{2,1,0:T(8,128)(2,1)}, u32[]{:S(2)}, u32[]{:S(2)}) %collective-permute-start.2) | collective-permute-done | bytes 786464 | tf_op jit(solution)/shard_map/ppermute | solution.py:30
  35.8 1.1 copy-done.7
  36.9 7.5 %queries.1 = (bf16[256,768]{1,0:T(8,128)(2,1)}, bf16[256,768]{1,0:T(8,128)(2,1)S(1)}, f32[6,8,256]{2,1,0:T(8,128)S(1)}) custom-call(f32[8,768]{1,0:T(8,128)S(1)} %reshape.69.mask_ref, bf16[2,256,768]{2,1,0:T(8,128)(2,1)S(1)} %get-tuple-element.54.qg_ref.own_ref, f32[256,768]{1,0:T(8,128)S(1)} %copy-done.7, f32[1,128]{1,0:T(1,128)S(1)} %bitcast.28, ...), custom_call_target="tpu_custom_call" | custom-call | flops 1207959552 | bytes 3932160 | tf_op jit(solution)/shard_map/queries/pallas_call | solution.py:255
  44.4 7.6 %collective-permute-start.7 = (f32[6,8,256]{2,1,0:T(8,128)S(1)}, f32[6,8,256]{2,1,0:T(8,128)S(1)}, u32[]{:S(2)}, u32[]{:S(2)}) collective-permute-start(f32[6,8,256]{2,1,0:T(8,128)S(1)} %get-tuple-element.68.so_ref), channel_id=1, source_target_pairs={{0,62},{1,63},{2,4},{3,5},{4,2},{5,3},{6,8},{7,9},{8,6},{9,7},{10,... | collective-permute-start | bytes 147464 | tf_op jit(solution)/shard_map/ppermute | solution.py:30
  52.0 2.2 %collective-permute-done.7.sl_ref = f32[6,8,256]{2,1,0:T(8,128)S(1)} collective-permute-done((f32[6,8,256]{2,1,0:T(8,128)S(1)}, f32[6,8,256]{2,1,0:T(8,128)S(1)}, u32[]{:S(2)}, u32[]{:S(2)}) %collective-permute-start.7) | collective-permute-done | bytes 49184 | tf_op jit(solution)/shard_map/ppermute | solution.py:30
  54.2 4.9 %keys.1 = (bf16[256,1152]{1,0:T(8,128)(2,1)S(1)}, bf16[256,1152]{1,0:T(8,128)(2,1)S(1)}) custom-call(f32[8,768]{1,0:T(8,128)S(1)} %reshape.69.mask_ref, bf16[2,256,768]{2,1,0:T(8,128)(2,1)S(1)} %get-tuple-element.53.own_ref.kv_ref, f32[256,768]{1,0:T(8,128)S(1)} %get-tuple-element.63.raw_ref, f32[1,128]{1,0:T(1,128)S(1)} %bitcast.26, ...), custom_call_target="tpu_custom_call" | custom-call | flops 1207959552 | bytes 4718592 | tf_op jit(solution)/shard_map/keys/pallas_call | solution.py:318
  59.2 0.9 collective-permute-start.11
  60.1 0.5 collective-permute-start.14
  60.6 8.2 %input_grad.1 = (f32[128,2048]{1,0:T(8,128)S(1)}, bf16[128,2048]{1,0:T(8,128)(2,1)S(1)}) custom-call(s32[5]{0:T(128)S(1)} %stack.35.place_ref, bf16[256,1152]{1,0:T(8,128)(2,1)S(1)} %get-tuple-element.74.da_ref.refs_4_, bf16[256,1152]{1,0:T(8,128)(2,1)S(1)} %get-tuple-element.75.db_ref.refs_4_, bf16[3,2048,768]{2,1,0:T(8,128)(2,1)} %bitcast.32), custom_call_target="tpu_custom_call" | custom-call | flops 2415919104 | bytes 9437184 | tf_op jit(solution)/shard_map/input_grad/pallas_call | solution.py:358
  68.8 4.9 %collective-permute-done.11.refs_6_ = bf16[256,1152]{1,0:T(8,128)(2,1)S(1)} collective-permute-done((bf16[256,1152]{1,0:T(8,128)(2,1)S(1)}, bf16[256,1152]{1,0:T(8,128)(2,1)S(1)}, u32[]{:S(2)}, u32[]{:S(2)}) %collective-permute-start.11) | collective-permute-done | bytes 589856 | tf_op jit(solution)/shard_map/ppermute | solution.py:30
  73.7 0.6 collective-permute-done.12.refs_6_
  74.3 0.5 collective-permute-start.22
  74.8 1.5 %collective-permute-done.16.refs_7_ = bf16[256,1152]{1,0:T(8,128)(2,1)S(1)} collective-permute-done((bf16[256,1152]{1,0:T(8,128)(2,1)S(1)}, bf16[256,1152]{1,0:T(8,128)(2,1)S(1)}, u32[]{:S(2)}, u32[]{:S(2)}) %collective-permute-start.16) | collective-permute-done | bytes 589856 | tf_op jit(solution)/shard_map/ppermute | solution.py:30
  76.3 2.6 %weight_grad.2 = (bf16[128,1152]{1,0:T(8,128)(2,1)S(1)}, bf16[128,1152]{1,0:T(8,128)(2,1)S(1)}, bf16[128,1152]{1,0:T(8,128)(2,1)S(1)}, bf16[128,1152]{1,0:T(8,128)(2,1)S(1)}) custom-call(bf16[2,512,256]{2,1,0:T(8,128)(2,1)S(1)} %copy-done.9, bf16[2,512,256]{2,1,0:T(8,128)(2,1)S(1)} %collective-permute-done.3.refs_1_, ...), custom_call_target="tpu_custom_call" | custom-call | flops 1207959552 | bytes 4718592 | tf_op jit(solution)/shard_map/weight_grad/pallas_call | solution.py:401
  78.8 0.1 collective-permute-start.19
  79.0 5.3 %collective-permute-start.15 = (bf16[128,2048]{1,0:T(8,128)(2,1)S(1)}, bf16[128,2048]{1,0:T(8,128)(2,1)S(1)}, u32[]{:S(2)}, u32[]{:S(2)}) collective-permute-start(bf16[128,2048]{1,0:T(8,128)(2,1)S(1)} %get-tuple-element.78), channel_id=1, source_target_pairs={{0,1},{1,0},{2,3},{3,2},{4,5},{5,4},{6,7},{7,6},{8,9},{9,8},{10,11... | collective-permute-start | bytes 1572872 | tf_op jit(solution)/shard_map/ppermute | solution.py:30
  84.3 0.3 collective-permute-start.17
  84.6 2.5 %weight_grad.3 = (bf16[128,1152]{1,0:T(8,128)(2,1)S(1)}, bf16[128,1152]{1,0:T(8,128)(2,1)S(1)}, bf16[128,1152]{1,0:T(8,128)(2,1)S(1)}, bf16[128,1152]{1,0:T(8,128)(2,1)S(1)}) custom-call(bf16[2,512,256]{2,1,0:T(8,128)(2,1)S(1)} %copy-done.9, bf16[2,512,256]{2,1,0:T(8,128)(2,1)S(1)} %collective-permute-done.3.refs_1_, ...), custom_call_target="tpu_custom_call" | custom-call | flops 1207959552 | bytes 4718592 | tf_op jit(solution)/shard_map/weight_grad/pallas_call | solution.py:401
  87.1 1.2 %collective-permute-start.25 = (bf16[128,1152]{1,0:T(8,128)(2,1)S(1)}, bf16[128,1152]{1,0:T(8,128)(2,1)S(1)}, u32[]{:S(2)}, u32[]{:S(2)}) collective-permute-start(bf16[128,1152]{1,0:T(8,128)(2,1)S(1)} %get-tuple-element.96), channel_id=1, source_target_pairs={{0,192},{1,193},{2,194},{3,195},{4,196},{5,197},{6,198},{7,199},{8... | collective-permute-start | bytes 884744 | tf_op jit(solution)/shard_map/ppermute | solution.py:30
  88.3 0.2 collective-permute-start.23
  88.5 0.7 collective-permute-done.19
  89.2 1.1 collective-permute-start.20
  90.4 3.8 %collective-permute-done.17 = bf16[128,1152]{1,0:T(8,128)(2,1)S(1)} collective-permute-done((bf16[128,1152]{1,0:T(8,128)(2,1)S(1)}, bf16[128,1152]{1,0:T(8,128)(2,1)S(1)}, u32[]{:S(2)}, u32[]{:S(2)}) %collective-permute-start.17) | collective-permute-done | bytes 294944 | tf_op jit(solution)/shard_map/ppermute | solution.py:30
  94.2 3.3 %collective-permute-start.18 = (bf16[64,1152]{1,0:T(8,128)(2,1)S(1)}, bf16[64,1152]{1,0:T(8,128)(2,1)S(1)}, u32[]{:S(2)}, u32[]{:S(2)}) collective-permute-start(bf16[64,1152]{1,0:T(8,128)(2,1)S(1)} %add_convert_fusion.8), channel_id=1, source_target_pairs={{0,12},{1,13},{2,14},{3,15},{4,8},{5,9},{6,10},{7,11},{8,4},{9,5},... | collective-permute-start | bytes 442376 | tf_op jit(solution)/shard_map/ppermute | solution.py:30
  97.5 1.3 %collective-permute-start.26 = (bf16[64,1152]{1,0:T(8,128)(2,1)S(1)}, bf16[64,1152]{1,0:T(8,128)(2,1)S(1)}, u32[]{:S(2)}, u32[]{:S(2)}) collective-permute-start(bf16[64,1152]{1,0:T(8,128)(2,1)S(1)} %add_convert_fusion.3), channel_id=1, source_target_pairs={{0,64},{1,65},{2,66},{3,67},{4,68},{5,69},{6,70},{7,71},{8,72},{9,... | collective-permute-start | bytes 442376 | tf_op jit(solution)/shard_map/ppermute | solution.py:30
  98.9 0.1 collective-permute-start.24
  99.0 3.3 %collective-permute-start.21 = (bf16[64,1152]{1,0:T(8,128)(2,1)S(1)}, bf16[64,1152]{1,0:T(8,128)(2,1)S(1)}, u32[]{:S(2)}, u32[]{:S(2)}) collective-permute-start(bf16[64,1152]{1,0:T(8,128)(2,1)S(1)} %add_convert_fusion.6), channel_id=1, source_target_pairs={{0,192},{1,193},{2,194},{3,195},{4,196},{5,197},{6,198},{7,199},{8... | collective-permute-start | bytes 442376 | tf_op jit(solution)/shard_map/ppermute | solution.py:30
  102.3 0.4 collective-permute-done.26
  102.8 2.4 %collective-permute-start.27 = (bf16[64,1152]{1,0:T(8,128)(2,1)S(1)}, bf16[64,1152]{1,0:T(8,128)(2,1)S(1)}, u32[]{:S(2)}, u32[]{:S(2)}) collective-permute-start(bf16[64,1152]{1,0:T(8,128)(2,1)S(1)} %add_convert_fusion.2), channel_id=1, source_target_pairs={{0,12},{1,13},{2,14},{3,15},{4,8},{5,9},{6,10},{7,11},{8,4},{9,5},... | collective-permute-start | bytes 442376 | tf_op jit(solution)/shard_map/ppermute | solution.py:30
  105.2 1.7 %collective-permute-done.21 = bf16[64,1152]{1,0:T(8,128)(2,1)S(1)} collective-permute-done((bf16[64,1152]{1,0:T(8,128)(2,1)S(1)}, bf16[64,1152]{1,0:T(8,128)(2,1)S(1)}, u32[]{:S(2)}, u32[]{:S(2)}) %collective-permute-start.21) | collective-permute-done | bytes 147488 | tf_op jit(solution)/shard_map/ppermute | solution.py:30
  107.0 2.3 %collective-permute-done.27 = bf16[64,1152]{1,0:T(8,128)(2,1)S(1)} collective-permute-done((bf16[64,1152]{1,0:T(8,128)(2,1)S(1)}, bf16[64,1152]{1,0:T(8,128)(2,1)S(1)}, u32[]{:S(2)}, u32[]{:S(2)}) %collective-permute-start.27) | collective-permute-done | bytes 147488 | tf_op jit(solution)/shard_map/ppermute | solution.py:30
  109.4 2.5 %collective-permute-start.30 = (bf16[16,2304]{1,0:T(8,128)(2,1)S(1)}, bf16[16,2304]{1,0:T(8,128)(2,1)S(1)}, u32[]{:S(2)}, u32[]{:S(2)}) collective-permute-start(bf16[16,2304]{1,0:T(8,128)(2,1)S(1)} %get-tuple-element.100), channel_id=1, source_target_pairs={{0,32},{1,33},{2,34},{3,35},{4,36},{5,37},{6,38},{7,39},{8,40},{9,... | collective-permute-start | bytes 221192 | tf_op jit(solution)/shard_map/ppermute | solution.py:30
  111.8 1.8 %collective-permute-start.29 = (bf16[16,2304]{1,0:T(8,128)(2,1)S(1)}, bf16[16,2304]{1,0:T(8,128)(2,1)S(1)}, u32[]{:S(2)}, u32[]{:S(2)}) collective-permute-start(bf16[16,2304]{1,0:T(8,128)(2,1)S(1)} %get-tuple-element.101), channel_id=1, source_target_pairs={{0,48},{1,49},{2,50},{3,51},{4,52},{5,53},{6,54},{7,55},{8,56},{9,... | collective-permute-start | bytes 221192 | tf_op jit(solution)/shard_map/ppermute | solution.py:30
  113.6 1.1 collective-permute-start.28
  114.8 0.9 fusion
  115.7 3.1 %collective-permute-done.30 = bf16[16,2304]{1,0:T(8,128)(2,1)S(1)} collective-permute-done((bf16[16,2304]{1,0:T(8,128)(2,1)S(1)}, bf16[16,2304]{1,0:T(8,128)(2,1)S(1)}, u32[]{:S(2)}, u32[]{:S(2)}) %collective-permute-start.30) | collective-permute-done | bytes 73760 | tf_op jit(solution)/shard_map/ppermute | solution.py:30
  118.8 1.8 %collective-permute-done.28 = bf16[16,2304]{1,0:T(8,128)(2,1)S(1)} collective-permute-done((bf16[16,2304]{1,0:T(8,128)(2,1)S(1)}, bf16[16,2304]{1,0:T(8,128)(2,1)S(1)}, u32[]{:S(2)}, u32[]{:S(2)}) %collective-permute-start.28) | collective-permute-done | bytes 73760 | tf_op jit(solution)/shard_map/ppermute | solution.py:30
  120.7 0.7 maximum_bitcast_fusion
  (65 shorter events, 0.6 us)
Async XLA Ops:
  0.6 1.2 %copy-start = (bf16[1,256,2048]{2,1,0:T(8,128)(2,1)S(1)}, bf16[1,256,2048]{2,1,0:T(8,128)(2,1)}, u32[]{:S(2)}) copy-start(bf16[1,256,2048]{2,1,0:T(8,128)(2,1)} %param.6) | copy-start | bytes 3145732
  1.9 0.7 copy-start.3
  2.5 13.9 %copy-start.2 = (bf16[1,256,768]{2,1,0:T(8,128)(2,1)S(1)}, bf16[1,256,768]{2,1,0:T(8,128)(2,1)}, u32[]{:S(2)}) copy-start(bf16[1,256,768]{2,1,0:T(8,128)(2,1)} %param.11) | copy-start | bytes 1179652
  2.5 13.9 %copy-start.5 = (f32[128]{0:T(128)S(1)}, f32[128]{0:T(128)}, u32[]{:S(2)}) copy-start(f32[128]{0:T(128)} %param.8) | copy-start | bytes 1540
  7.4 14.4 %copy-start.15 = (s32[128,9]{0,1:T(8,128)S(1)}, s32[128,9]{0,1:T(8,128)}, u32[]{:S(2)}) copy-start(s32[128,9]{0,1:T(8,128)} %param.10) | copy-start | bytes 13828
  7.4 14.8 %copy-start.1 = (bf16[1,256,2048]{2,1,0:T(8,128)(2,1)S(1)}, bf16[1,256,2048]{2,1,0:T(8,128)(2,1)}, u32[]{:S(2)}) copy-start(bf16[1,256,2048]{2,1,0:T(8,128)(2,1)} %param.6) | copy-start | bytes 3145732
  7.4 46.8 %copy-start.4 = (f32[128]{0:T(128)S(1)}, f32[128]{0:T(128)}, u32[]{:S(2)}) copy-start(f32[128]{0:T(128)} %param.9) | copy-start | bytes 1540
  7.4 21.0 %collective-permute-start = (bf16[2,256,768]{2,1,0:T(8,128)(2,1)S(1)}, bf16[2,256,768]{2,1,0:T(8,128)(2,1)}, u32[]{:S(2)}, u32[]{:S(2)}) collective-permute-start(bf16[2,256,768]{2,1,0:T(8,128)(2,1)S(1)} %get-tuple-element.53.own_ref.kv_ref), channel_id=1, source_target_pairs={{0,2},{1,3},{2,0},{3,1},{4,6},{5,7},{6,4},{7,5},{8,10},{9,11},{10,... | collective-permute-start | bytes 2359304 | tf_op jit(solution)/shard_map/ppermute | solution.py:30
  7.5 28.3 %collective-permute-start.2 = (bf16[2,256,768]{2,1,0:T(8,128)(2,1)S(1)}, bf16[2,256,768]{2,1,0:T(8,128)(2,1)}, u32[]{:S(2)}, u32[]{:S(2)}) collective-permute-start(bf16[2,256,768]{2,1,0:T(8,128)(2,1)S(1)} %get-tuple-element.53.own_ref.kv_ref), channel_id=1, source_target_pairs={{0,62},{1,63},{2,4},{3,5},{4,2},{5,3},{6,8},{7,9},{8,6},{9,7},{10,... | collective-permute-start | bytes 2359304 | tf_op jit(solution)/shard_map/ppermute | solution.py:30
  20.0 0.9 copy-start.6
  20.9 7.5 %collective-permute-start.1 = (bf16[2,256,768]{2,1,0:T(8,128)(2,1)S(1)}, bf16[2,256,768]{2,1,0:T(8,128)(2,1)}, u32[]{:S(2)}, u32[]{:S(2)}) collective-permute-start(bf16[2,256,768]{2,1,0:T(8,128)(2,1)S(1)} %get-tuple-element.54.qg_ref.own_ref), channel_id=1, source_target_pairs={{0,2},{1,3},{2,0},{3,1},{4,6},{5,7},{6,4},{7,5},{8,10},{9,11},{10,... | collective-permute-start | bytes 2359304 | tf_op jit(solution)/shard_map/ppermute | solution.py:30
  20.9 31.1 %collective-permute-start.4 = (bf16[2,256,768]{2,1,0:T(8,128)(2,1)S(1)}, bf16[2,256,768]{2,1,0:T(8,128)(2,1)}, u32[]{:S(2)}, u32[]{:S(2)}) collective-permute-start(bf16[2,256,768]{2,1,0:T(8,128)(2,1)S(1)} %get-tuple-element.54.qg_ref.own_ref), channel_id=1, source_target_pairs={{0,62},{1,63},{2,4},{3,5},{4,2},{5,3},{6,8},{7,9},{8,6},{9,7},{10,... | collective-permute-start | bytes 2359304 | tf_op jit(solution)/shard_map/ppermute | solution.py:30
  23.7 0.8 copy-start.8
  24.5 0.8 copy-start.10
  25.3 0.7 copy-start.11
  26.0 0.7 copy-start.12
  26.7 0.7 copy-start.13
  27.4 0.7 copy-start.14
  28.4 7.4 %collective-permute-start.3 = (bf16[2,512,256]{2,1,0:T(8,128)(2,1)}, bf16[2,512,256]{2,1,0:T(8,128)(2,1)S(1)}, u32[]{:S(2)}, u32[]{:S(2)}) collective-permute-start(bf16[2,512,256]{2,1,0:T(8,128)(2,1)} %copy-done.10), channel_id=1, source_target_pairs={{0,2},{1,3},{2,0},{3,1},{4,6},{5,7},{6,4},{7,5},{8,10},{9,11},{10,... | collective-permute-start | bytes 1572872 | tf_op jit(solution)/shard_map/ppermute | solution.py:30
  28.5 15.9 %collective-permute-start.5 = (bf16[512,256]{1,0:T(8,128)(2,1)}, bf16[512,256]{1,0:T(8,128)(2,1)S(1)}, u32[]{:S(2)}, u32[]{:S(2)}) collective-permute-start(bf16[512,256]{1,0:T(8,128)(2,1)} %copy-done.14), channel_id=1, source_target_pairs={{0,64},{1,65},{2,66},{3,67},{4,68},{5,69},{6,70},{7,71},{8,72},{9,... | collective-permute-start | bytes 786440 | tf_op jit(solution)/shard_map/ppermute | solution.py:30
  29.4 15.0 %collective-permute-start.6 = (bf16[512,256]{1,0:T(8,128)(2,1)}, bf16[512,256]{1,0:T(8,128)(2,1)S(1)}, u32[]{:S(2)}, u32[]{:S(2)}) collective-permute-start(bf16[512,256]{1,0:T(8,128)(2,1)} %copy-done.13), channel_id=1, source_target_pairs={{0,66},{1,67},{2,64},{3,65},{4,70},{5,71},{6,68},{7,69},{8,74},{9,... | collective-permute-start | bytes 786440 | tf_op jit(solution)/shard_map/ppermute | solution.py:30
  35.8 23.4 %collective-permute-start.9 = (bf16[512,256]{1,0:T(8,128)(2,1)}, bf16[512,256]{1,0:T(8,128)(2,1)S(1)}, u32[]{:S(2)}, u32[]{:S(2)}) collective-permute-start(bf16[512,256]{1,0:T(8,128)(2,1)} %copy-done.12), channel_id=1, source_target_pairs={{0,4},{1,5},{2,6},{3,7},{4,0},{5,1},{6,2},{7,3},{8,12},{9,13},{10,... | collective-permute-start | bytes 786440 | tf_op jit(solution)/shard_map/ppermute | solution.py:30
  35.8 23.4 %collective-permute-start.10 = (bf16[512,256]{1,0:T(8,128)(2,1)}, bf16[512,256]{1,0:T(8,128)(2,1)S(1)}, u32[]{:S(2)}, u32[]{:S(2)}) collective-permute-start(bf16[512,256]{1,0:T(8,128)(2,1)} %copy-done.11), channel_id=1, source_target_pairs={{0,6},{1,7},{2,4},{3,5},{4,2},{5,3},{6,0},{7,1},{8,14},{9,15},{10,... | collective-permute-start | bytes 786440 | tf_op jit(solution)/shard_map/ppermute | solution.py:30
  35.8 1.1 copy-start.7
  36.9 39.4 %copy-start.9 = (bf16[2,512,256]{2,1,0:T(8,128)(2,1)S(1)}, bf16[2,512,256]{2,1,0:T(8,128)(2,1)}, u32[]{:S(2)}) copy-start(bf16[2,512,256]{2,1,0:T(8,128)(2,1)} %copy-done.8) | copy-start | bytes 1572868
  44.4 9.8 %collective-permute-start.7 = (f32[6,8,256]{2,1,0:T(8,128)S(1)}, f32[6,8,256]{2,1,0:T(8,128)S(1)}, u32[]{:S(2)}, u32[]{:S(2)}) collective-permute-start(f32[6,8,256]{2,1,0:T(8,128)S(1)} %get-tuple-element.68.so_ref), channel_id=1, source_target_pairs={{0,62},{1,63},{2,4},{3,5},{4,2},{5,3},{6,8},{7,9},{8,6},{9,7},{10,... | collective-permute-start | bytes 147464 | tf_op jit(solution)/shard_map/ppermute | solution.py:30
  52.0 2.2 %collective-permute-start.8 = (f32[6,8,256]{2,1,0:T(8,128)S(1)}, f32[6,8,256]{2,1,0:T(8,128)S(1)}, u32[]{:S(2)}, u32[]{:S(2)}) collective-permute-start(f32[6,8,256]{2,1,0:T(8,128)S(1)} %get-tuple-element.68.so_ref), channel_id=1, source_target_pairs={{0,2},{1,3},{2,0},{3,1},{4,6},{5,7},{6,4},{7,5},{8,10},{9,11},{10,... | collective-permute-start | bytes 147464 | tf_op jit(solution)/shard_map/ppermute | solution.py:30
  59.2 14.5 %collective-permute-start.11 = (bf16[256,1152]{1,0:T(8,128)(2,1)S(1)}, bf16[256,1152]{1,0:T(8,128)(2,1)S(1)}, u32[]{:S(2)}, u32[]{:S(2)}) collective-permute-start(bf16[256,1152]{1,0:T(8,128)(2,1)S(1)} %get-tuple-element.74.da_ref.refs_4_), channel_id=1, source_target_pairs={{0,64},{1,65},{2,66},{3,67},{4,68},{5,69},{6,70},{7,71},{8,72},{9,... | collective-permute-start | bytes 1769480 | tf_op jit(solution)/shard_map/ppermute | solution.py:30
  60.1 14.2 %collective-permute-start.12 = (bf16[256,1152]{1,0:T(8,128)(2,1)S(1)}, bf16[256,1152]{1,0:T(8,128)(2,1)S(1)}, u32[]{:S(2)}, u32[]{:S(2)}) collective-permute-start(bf16[256,1152]{1,0:T(8,128)(2,1)S(1)} %get-tuple-element.75.db_ref.refs_4_), channel_id=1, source_target_pairs={{0,4},{1,5},{2,6},{3,7},{4,0},{5,1},{6,2},{7,3},{8,12},{9,13},{10,... | collective-permute-start | bytes 1769480 | tf_op jit(solution)/shard_map/ppermute | solution.py:30
  60.1 14.2 %collective-permute-start.13 = (bf16[256,1152]{1,0:T(8,128)(2,1)S(1)}, bf16[256,1152]{1,0:T(8,128)(2,1)S(1)}, u32[]{:S(2)}, u32[]{:S(2)}) collective-permute-start(bf16[256,1152]{1,0:T(8,128)(2,1)S(1)} %get-tuple-element.74.da_ref.refs_4_), channel_id=1, source_target_pairs={{0,2},{1,3},{2,0},{3,1},{4,6},{5,7},{6,4},{7,5},{8,10},{9,11},{10,... | collective-permute-start | bytes 1769480 | tf_op jit(solution)/shard_map/ppermute | solution.py:30
  60.1 14.2 %collective-permute-start.14 = (bf16[256,1152]{1,0:T(8,128)(2,1)S(1)}, bf16[256,1152]{1,0:T(8,128)(2,1)S(1)}, u32[]{:S(2)}, u32[]{:S(2)}) collective-permute-start(bf16[256,1152]{1,0:T(8,128)(2,1)S(1)} %get-tuple-element.75.db_ref.refs_4_), channel_id=1, source_target_pairs={{0,2},{1,3},{2,0},{3,1},{4,6},{5,7},{6,4},{7,5},{8,10},{9,11},{10,... | collective-permute-start | bytes 1769480 | tf_op jit(solution)/shard_map/ppermute | solution.py:30
  74.3 2.0 %collective-permute-start.16 = (bf16[256,1152]{1,0:T(8,128)(2,1)S(1)}, bf16[256,1152]{1,0:T(8,128)(2,1)S(1)}, u32[]{:S(2)}, u32[]{:S(2)}) collective-permute-start(bf16[256,1152]{1,0:T(8,128)(2,1)S(1)} %collective-permute-done.11.refs_6_), channel_id=1, source_target_pairs={{0,2},{1,3},{2,0},{3,1},{4,6},{5,7},{6,4},{7,5},{8,10},{9,11},{10,... | collective-permute-start | bytes 1769480 | tf_op jit(solution)/shard_map/ppermute | solution.py:30
  74.3 10.3 %collective-permute-start.22 = (bf16[256,1152]{1,0:T(8,128)(2,1)S(1)}, bf16[256,1152]{1,0:T(8,128)(2,1)S(1)}, u32[]{:S(2)}, u32[]{:S(2)}) collective-permute-start(bf16[256,1152]{1,0:T(8,128)(2,1)S(1)} %collective-permute-done.12.refs_6_), channel_id=1, source_target_pairs={{0,2},{1,3},{2,0},{3,1},{4,6},{5,7},{6,4},{7,5},{8,10},{9,11},{10,... | collective-permute-start | bytes 1769480 | tf_op jit(solution)/shard_map/ppermute | solution.py:30
  78.8 10.3 %collective-permute-start.19 = (bf16[128,1152]{1,0:T(8,128)(2,1)S(1)}, bf16[128,1152]{1,0:T(8,128)(2,1)S(1)}, u32[]{:S(2)}, u32[]{:S(2)}) collective-permute-start(bf16[128,1152]{1,0:T(8,128)(2,1)S(1)} %get-tuple-element.88), channel_id=1, source_target_pairs={{0,12},{1,13},{2,14},{3,15},{4,8},{5,9},{6,10},{7,11},{8,4},{9,5},... | collective-permute-start | bytes 884744 | tf_op jit(solution)/shard_map/ppermute | solution.py:30
  79.0 35.8 %collective-permute-start.15 = (bf16[128,2048]{1,0:T(8,128)(2,1)S(1)}, bf16[128,2048]{1,0:T(8,128)(2,1)S(1)}, u32[]{:S(2)}, u32[]{:S(2)}) collective-permute-start(bf16[128,2048]{1,0:T(8,128)(2,1)S(1)} %get-tuple-element.78), channel_id=1, source_target_pairs={{0,1},{1,0},{2,3},{3,2},{4,5},{5,4},{6,7},{7,6},{8,9},{9,8},{10,11... | collective-permute-start | bytes 1572872 | tf_op jit(solution)/shard_map/ppermute | solution.py:30
  84.3 9.9 %collective-permute-start.17 = (bf16[128,1152]{1,0:T(8,128)(2,1)S(1)}, bf16[128,1152]{1,0:T(8,128)(2,1)S(1)}, u32[]{:S(2)}, u32[]{:S(2)}) collective-permute-start(bf16[128,1152]{1,0:T(8,128)(2,1)S(1)} %get-tuple-element.86), channel_id=1, source_target_pairs={{0,4},{1,5},{2,6},{3,7},{4,0},{5,1},{6,2},{7,3},{8,12},{9,13},{10,... | collective-permute-start | bytes 884744 | tf_op jit(solution)/shard_map/ppermute | solution.py:30
  87.1 10.4 %collective-permute-start.25 = (bf16[128,1152]{1,0:T(8,128)(2,1)S(1)}, bf16[128,1152]{1,0:T(8,128)(2,1)S(1)}, u32[]{:S(2)}, u32[]{:S(2)}) collective-permute-start(bf16[128,1152]{1,0:T(8,128)(2,1)S(1)} %get-tuple-element.96), channel_id=1, source_target_pairs={{0,192},{1,193},{2,194},{3,195},{4,196},{5,197},{6,198},{7,199},{8... | collective-permute-start | bytes 884744 | tf_op jit(solution)/shard_map/ppermute | solution.py:30
  88.3 10.5 %collective-permute-start.23 = (bf16[128,1152]{1,0:T(8,128)(2,1)S(1)}, bf16[128,1152]{1,0:T(8,128)(2,1)S(1)}, u32[]{:S(2)}, u32[]{:S(2)}) collective-permute-start(bf16[128,1152]{1,0:T(8,128)(2,1)S(1)} %get-tuple-element.94), channel_id=1, source_target_pairs={{0,64},{1,65},{2,66},{3,67},{4,68},{5,69},{6,70},{7,71},{8,72},{9,... | collective-permute-start | bytes 884744 | tf_op jit(solution)/shard_map/ppermute | solution.py:30
  89.2 9.7 %collective-permute-start.20 = (bf16[64,1152]{1,0:T(8,128)(2,1)S(1)}, bf16[64,1152]{1,0:T(8,128)(2,1)S(1)}, u32[]{:S(2)}, u32[]{:S(2)}) collective-permute-start(bf16[64,1152]{1,0:T(8,128)(2,1)S(1)} %add_convert_fusion.7), channel_id=1, source_target_pairs={{0,4},{1,5},{2,6},{3,7},{4,0},{5,1},{6,2},{7,3},{8,12},{9,13},{10,... | collective-permute-start | bytes 442376 | tf_op jit(solution)/shard_map/ppermute | solution.py:30
  94.2 11.0 %collective-permute-start.18 = (bf16[64,1152]{1,0:T(8,128)(2,1)S(1)}, bf16[64,1152]{1,0:T(8,128)(2,1)S(1)}, u32[]{:S(2)}, u32[]{:S(2)}) collective-permute-start(bf16[64,1152]{1,0:T(8,128)(2,1)S(1)} %add_convert_fusion.8), channel_id=1, source_target_pairs={{0,12},{1,13},{2,14},{3,15},{4,8},{5,9},{6,10},{7,11},{8,4},{9,5},... | collective-permute-start | bytes 442376 | tf_op jit(solution)/shard_map/ppermute | solution.py:30
  97.5 5.2 %collective-permute-start.26 = (bf16[64,1152]{1,0:T(8,128)(2,1)S(1)}, bf16[64,1152]{1,0:T(8,128)(2,1)S(1)}, u32[]{:S(2)}, u32[]{:S(2)}) collective-permute-start(bf16[64,1152]{1,0:T(8,128)(2,1)S(1)} %add_convert_fusion.3), channel_id=1, source_target_pairs={{0,64},{1,65},{2,66},{3,67},{4,68},{5,69},{6,70},{7,71},{8,72},{9,... | collective-permute-start | bytes 442376 | tf_op jit(solution)/shard_map/ppermute | solution.py:30
  98.9 8.1 %collective-permute-start.24 = (bf16[64,1152]{1,0:T(8,128)(2,1)S(1)}, bf16[64,1152]{1,0:T(8,128)(2,1)S(1)}, u32[]{:S(2)}, u32[]{:S(2)}) collective-permute-start(bf16[64,1152]{1,0:T(8,128)(2,1)S(1)} %add_convert_fusion.4), channel_id=1, source_target_pairs={{0,192},{1,193},{2,194},{3,195},{4,196},{5,197},{6,198},{7,199},{8... | collective-permute-start | bytes 442376 | tf_op jit(solution)/shard_map/ppermute | solution.py:30
  99.0 7.8 %collective-permute-start.21 = (bf16[64,1152]{1,0:T(8,128)(2,1)S(1)}, bf16[64,1152]{1,0:T(8,128)(2,1)S(1)}, u32[]{:S(2)}, u32[]{:S(2)}) collective-permute-start(bf16[64,1152]{1,0:T(8,128)(2,1)S(1)} %add_convert_fusion.6), channel_id=1, source_target_pairs={{0,192},{1,193},{2,194},{3,195},{4,196},{5,197},{6,198},{7,199},{8... | collective-permute-start | bytes 442376 | tf_op jit(solution)/shard_map/ppermute | solution.py:30
  102.8 6.4 %collective-permute-start.27 = (bf16[64,1152]{1,0:T(8,128)(2,1)S(1)}, bf16[64,1152]{1,0:T(8,128)(2,1)S(1)}, u32[]{:S(2)}, u32[]{:S(2)}) collective-permute-start(bf16[64,1152]{1,0:T(8,128)(2,1)S(1)} %add_convert_fusion.2), channel_id=1, source_target_pairs={{0,12},{1,13},{2,14},{3,15},{4,8},{5,9},{6,10},{7,11},{8,4},{9,5},... | collective-permute-start | bytes 442376 | tf_op jit(solution)/shard_map/ppermute | solution.py:30
  109.4 9.4 %collective-permute-start.30 = (bf16[16,2304]{1,0:T(8,128)(2,1)S(1)}, bf16[16,2304]{1,0:T(8,128)(2,1)S(1)}, u32[]{:S(2)}, u32[]{:S(2)}) collective-permute-start(bf16[16,2304]{1,0:T(8,128)(2,1)S(1)} %get-tuple-element.100), channel_id=1, source_target_pairs={{0,32},{1,33},{2,34},{3,35},{4,36},{5,37},{6,38},{7,39},{8,40},{9,... | collective-permute-start | bytes 221192 | tf_op jit(solution)/shard_map/ppermute | solution.py:30
  111.8 7.0 %collective-permute-start.29 = (bf16[16,2304]{1,0:T(8,128)(2,1)S(1)}, bf16[16,2304]{1,0:T(8,128)(2,1)S(1)}, u32[]{:S(2)}, u32[]{:S(2)}) collective-permute-start(bf16[16,2304]{1,0:T(8,128)(2,1)S(1)} %get-tuple-element.101), channel_id=1, source_target_pairs={{0,48},{1,49},{2,50},{3,51},{4,52},{5,53},{6,54},{7,55},{8,56},{9,... | collective-permute-start | bytes 221192 | tf_op jit(solution)/shard_map/ppermute | solution.py:30
  113.6 6.9 %collective-permute-start.28 = (bf16[16,2304]{1,0:T(8,128)(2,1)S(1)}, bf16[16,2304]{1,0:T(8,128)(2,1)S(1)}, u32[]{:S(2)}, u32[]{:S(2)}) collective-permute-start(bf16[16,2304]{1,0:T(8,128)(2,1)S(1)} %get-tuple-element.99), channel_id=1, source_target_pairs={{0,16},{1,17},{2,18},{3,19},{4,20},{5,21},{6,22},{7,23},{8,24},{9,... | collective-permute-start | bytes 221192 | tf_op jit(solution)/shard_map/ppermute | solution.py:30

commit v4 on v3

--- a/solution.py
+++ b/solution.py
@@ -102,7 +102,7 @@
             jax.ShapeDtypeStruct((2, rows, cols), BF16),
             jax.ShapeDtypeStruct((rows, cols), F32),
         ],
-        compiler_params=params(48),
+        compiler_params=params(62),
         cost_estimate=cost(4 * rows * width * cols, 4 * width * cols),
         name="project_kv",
     )(x, w, w, gain)
@@ -249,7 +249,7 @@
 
 def queries(mask, qg, q_raw, gain, far, own, mate):
     rows, cols = q_raw.shape
-    block = 2 * HD
+    block = 3 * HD
     flat = pl.BlockSpec((rows, block), lambda i: (0, i))
     pair = pl.BlockSpec((2, rows, block), lambda i: (0, 0, i))
     return pl.pallas_call(
@@ -264,7 +264,7 @@
             pair,
             pair,
         ],
-        out_specs=[flat, flat, pl.BlockSpec((2, 8, rows), lambda i: (i, 0, 0))],
+        out_specs=[flat, flat, pl.BlockSpec((3, 8, rows), lambda i: (i, 0, 0))],
         out_shape=[
             jax.ShapeDtypeStruct((rows, cols), BF16),
             jax.ShapeDtypeStruct((rows, cols), BF16),
@@ -310,10 +310,10 @@
 
 def keys(mask, kv, k_raw, gain, qg3, s3, dq):
     rows, cols = k_raw.shape
-    block = 2 * HD
+    block = 3 * HD
     flat = pl.BlockSpec((rows, block), lambda i: (0, i))
     pair = pl.BlockSpec((2, rows, block), lambda i: (0, 0, i))
-    stats = pl.BlockSpec((2, 8, rows), lambda i: (i, 0, 0))
+    stats = pl.BlockSpec((3, 8, rows), lambda i: (i, 0, 0))
     wide = pl.BlockSpec((rows, cols * 3 // 2), lambda i: (0, 0))
     return pl.pallas_call(
         keys_kernel,

time: 122 us -> 121 us (level)
  waiting for transfers between devices: 28.4 us -> 26.7 us
  Pallas kernels: 35.6 us -> 37.3 us
    ppermute x31, waiting for transfers between devices: 28.4 us -> 26.7 us  [permute(): return lax.ppermute(value, AXES, pairs)]
    pallas_call x1, Pallas kernels: 4.85 us -> 6.12 us  [project_kv(): pl.pallas_call(project_kv_kernel, grid=(cols // block,), in_specs=[pl.Blo...]
  transfers between devices with their start and end apart: 31 -> 31, of which waited for: 12 -> 13; matrix products, arithmetic and copies ran while one was open for 2% -> 2% of each run, Pallas kernels for 25% -> 26%
where the time goes in v4:
time: 121 us; the launch traced here: 120 us
  starting transfers between devices  45 us (37%)
  Pallas kernels  37.3 us (31%)
  waiting for transfers between devices  26.7 us (22%)
  local copies, waits for them, and re-layouts  7.82 us (6%)
  other arithmetic  2.41 us (2%)
    ppermute x31, starting transfers between devices, permute(): return lax.ppermute(value, AXES, pairs)  45 us
    ppermute x31, waiting for transfers between devices, permute(): return lax.ppermute(value, AXES, pairs)  26.7 us
    pallas_call x1, Pallas kernels, input_grad(): pl.pallas_call(input_grad_kernel, grid=(width // block,), in_specs=[pl.Bl...  8.17 us
    unnamed x32, local copies, waits for them, and re-layouts  7.46 us
    pallas_call x1, Pallas kernels, queries(): pl.pallas_call(queries_kernel, grid=(cols // block,), in_specs=[pl.BlockS...  7.22 us
    pallas_call x1, Pallas kernels, project_kv(): pl.pallas_call(project_kv_kernel, grid=(cols // block,), in_specs=[pl.Blo...  6.12 us
    pallas_call x2, Pallas kernels, weight_grad(): pl.pallas_call(weight_grad_kernel, grid=(cols // block,), in_specs=specs,...  5.09 us
    pallas_call x1, Pallas kernels, keys(): pl.pallas_call(keys_kernel, grid=(cols // block,), in_specs=[pl.BlockSpec...  4.86 us
  transfers between devices with their start and end apart: 31, of which 13 were waited for; matrix products, arithmetic and copies ran while one was open for 2% of the time, Pallas kernels for 26%

profile of v4, /device:TPU:6, one launch (start us, length us, event | category | flops | bytes accessed | tf_op | source)
XLA Modules:
  0.0 120.2 jit_solution(2847714932846835258)
XLA Ops:
  0.7 6.1 %project_kv.1 = (bf16[2,256,768]{2,1,0:T(8,128)(2,1)}, f32[256,768]{1,0:T(8,128)}) custom-call(bf16[256,2048]{1,0:T(8,128)(2,1)} %bitcast.21, bf16[3,2048,768]{2,1,0:T(8,128)(2,1)} %bitcast.29, bf16[3,2048,768]{2,1,0:T(8,128)(2,1)} %bitcast.30, f32[1,128]{1,0:T(1,128)} %bitcast.25), custom_call_target="tpu_custom_call" | custom-call | flops 1610612736 | bytes 6291456 | tf_op jit(solution)/shard_map/project_kv/pallas_call | solution.py:88
  6.8 0.1 collective-permute-start
  6.9 8.9 %collective-permute-start.2 = (bf16[2,256,768]{2,1,0:T(8,128)(2,1)}, bf16[2,256,768]{2,1,0:T(8,128)(2,1)}, u32[]{:S(2)}, u32[]{:S(2)}) collective-permute-start(bf16[2,256,768]{2,1,0:T(8,128)(2,1)} %get-tuple-element.53.own_ref.kv_ref), channel_id=1, source_target_pairs={{0,62},{1,63},{2,4},{3,5},{4,2},{5,3},{6,8},{7,9},{8,6},{9,7},{10,... | collective-permute-start | bytes 2359304 | tf_op jit(solution)/shard_map/ppermute | solution.py:30
  15.8 1.0 copy-done.3
  16.8 4.4 %project_q.1 = (bf16[2,256,768]{2,1,0:T(8,128)(2,1)}, f32[256,768]{1,0:T(8,128)S(1)}) custom-call(bf16[256,2048]{1,0:T(8,128)(2,1)S(1)} %bitcast.22, bf16[3,2048,768]{2,1,0:T(8,128)(2,1)} %bitcast.31, f32[1,128]{1,0:T(1,128)S(1)} %bitcast.27, bf16[256,768]{1,0:T(8,128)(2,1)S(1)} %bitcast.24), custom_call_target="tpu_custom_call" | custom-call | flops 805306368 | bytes 3145728 | tf_op jit(solution)/shard_map/project_q/pallas_call | solution.py:124
  21.1 0.9 copy-done.6
  22.0 0.9 collective-permute-start.4
  22.9 0.1 pad_dynamic-slice_fusion.1
  23.0 0.1 compare_and_fusion
  23.1 0.1 compare_reduce_fusion.1
  23.2 0.1 pad_add_fusion
  23.2 0.1 stack.35.place_ref
  23.3 1.5 %spread_rows.1 = (bf16[2,512,256]{2,1,0:T(8,128)(2,1)S(1)}, bf16[512,256]{1,0:T(8,128)(2,1)S(1)}, bf16[512,256]{1,0:T(8,128)(2,1)S(1)}, bf16[512,256]{1,0:T(8,12...) custom-call(s32[5]{0:T(128)S(1)} %stack.35.place_ref, bf16[256,2048]{1,0:T(8,128)(2,1)S(1)} %bitcast.23), custom_call_target="tpu_custom_call" | custom-call | bytes 3145728 | tf_op jit(solution)/shard_map/spread_rows/pallas_call | solution.py:192
  24.9 0.8 copy-done.8
  25.6 0.8 copy-done.10
  26.4 0.7 copy-done.11
  27.1 0.7 copy-done.12
  27.8 0.7 copy-done.13
  28.6 0.7 copy-done.14
  29.3 0.1 compare_reduce_fusion
  29.4 0.1 broadcast_in_dim.6
  29.5 0.1 reshape.69.mask_ref
  29.6 0.1 collective-permute-start.3
  29.7 0.9 collective-permute-start.5
  30.6 1.0 collective-permute-start.6
  31.5 4.0 %collective-permute-done.2.far_ref = bf16[2,256,768]{2,1,0:T(8,128)(2,1)} collective-permute-done((bf16[2,256,768]{2,1,0:T(8,128)(2,1)}, bf16[2,256,768]{2,1,0:T(8,128)(2,1)}, u32[]{:S(2)}, u32[]{:S(2)}) %collective-permute-start.2) | collective-permute-done | bytes 786464 | tf_op jit(solution)/shard_map/ppermute | solution.py:30
  35.5 1.1 copy-done.7
  36.6 7.2 %queries.1 = (bf16[256,768]{1,0:T(8,128)(2,1)}, bf16[256,768]{1,0:T(8,128)(2,1)S(1)}, f32[6,8,256]{2,1,0:T(8,128)S(1)}) custom-call(f32[8,768]{1,0:T(8,128)S(1)} %reshape.69.mask_ref, bf16[2,256,768]{2,1,0:T(8,128)(2,1)} %get-tuple-element.54.qg_ref.own_ref, f32[256,768]{1,0:T(8,128)S(1)} %copy-done.7, f32[1,128]{1,0:T(1,128)S(1)} %bitcast.28, ...), custom_call_target="tpu_custom_call" | custom-call | flops 1207959552 | bytes 3932160 | tf_op jit(solution)/shard_map/queries/pallas_call | solution.py:255
  43.9 7.5 %collective-permute-start.7 = (f32[6,8,256]{2,1,0:T(8,128)S(1)}, f32[6,8,256]{2,1,0:T(8,128)S(1)}, u32[]{:S(2)}, u32[]{:S(2)}) collective-permute-start(f32[6,8,256]{2,1,0:T(8,128)S(1)} %get-tuple-element.68.so_ref), channel_id=1, source_target_pairs={{0,62},{1,63},{2,4},{3,5},{4,2},{5,3},{6,8},{7,9},{8,6},{9,7},{10,... | collective-permute-start | bytes 147464 | tf_op jit(solution)/shard_map/ppermute | solution.py:30
  51.4 1.8 %collective-permute-done.7.sl_ref = f32[6,8,256]{2,1,0:T(8,128)S(1)} collective-permute-done((f32[6,8,256]{2,1,0:T(8,128)S(1)}, f32[6,8,256]{2,1,0:T(8,128)S(1)}, u32[]{:S(2)}, u32[]{:S(2)}) %collective-permute-start.7) | collective-permute-done | bytes 49184 | tf_op jit(solution)/shard_map/ppermute | solution.py:30
  53.2 4.9 %keys.1 = (bf16[256,1152]{1,0:T(8,128)(2,1)S(1)}, bf16[256,1152]{1,0:T(8,128)(2,1)S(1)}) custom-call(f32[8,768]{1,0:T(8,128)S(1)} %reshape.69.mask_ref, bf16[2,256,768]{2,1,0:T(8,128)(2,1)S(1)} %copy-done.1, f32[256,768]{1,0:T(8,128)S(1)} %copy-done.2, f32[1,128]{1,0:T(1,128)S(1)} %bitcast.26, bf16[2,256,768]{2,1,0:T(8,128)(2,1)} %collective-permute-done.4.far_ref, ...), custom_call_target="tpu_custom_call" | custom-call | flops 1207959552 | bytes 4718592 | tf_op jit(solution)/shard_map/keys/pallas_call | solution.py:318
  58.1 0.9 collective-permute-start.11
  59.0 0.5 collective-permute-start.14
  59.5 8.2 %input_grad.1 = (f32[128,2048]{1,0:T(8,128)S(1)}, bf16[128,2048]{1,0:T(8,128)(2,1)S(1)}) custom-call(s32[5]{0:T(128)S(1)} %stack.35.place_ref, bf16[256,1152]{1,0:T(8,128)(2,1)S(1)} %get-tuple-element.74.da_ref.refs_4_, bf16[256,1152]{1,0:T(8,128)(2,1)S(1)} %get-tuple-element.75.db_ref.refs_4_, bf16[3,2048,768]{2,1,0:T(8,128)(2,1)} %bitcast.32), custom_call_target="tpu_custom_call" | custom-call | flops 2415919104 | bytes 9437184 | tf_op jit(solution)/shard_map/input_grad/pallas_call | solution.py:358
  67.7 5.3 %collective-permute-done.11.refs_6_ = bf16[256,1152]{1,0:T(8,128)(2,1)S(1)} collective-permute-done((bf16[256,1152]{1,0:T(8,128)(2,1)S(1)}, bf16[256,1152]{1,0:T(8,128)(2,1)S(1)}, u32[]{:S(2)}, u32[]{:S(2)}) %collective-permute-start.11) | collective-permute-done | bytes 589856 | tf_op jit(solution)/shard_map/ppermute | solution.py:30
  73.0 0.6 collective-permute-done.12.refs_6_
  73.5 0.5 collective-permute-start.22
  74.0 1.5 %collective-permute-done.16.refs_7_ = bf16[256,1152]{1,0:T(8,128)(2,1)S(1)} collective-permute-done((bf16[256,1152]{1,0:T(8,128)(2,1)S(1)}, bf16[256,1152]{1,0:T(8,128)(2,1)S(1)}, u32[]{:S(2)}, u32[]{:S(2)}) %collective-permute-start.16) | collective-permute-done | bytes 589856 | tf_op jit(solution)/shard_map/ppermute | solution.py:30
  75.5 2.6 %weight_grad.2 = (bf16[128,1152]{1,0:T(8,128)(2,1)S(1)}, bf16[128,1152]{1,0:T(8,128)(2,1)S(1)}, bf16[128,1152]{1,0:T(8,128)(2,1)S(1)}, bf16[128,1152]{1,0:T(8,128)(2,1)S(1)}) custom-call(bf16[2,512,256]{2,1,0:T(8,128)(2,1)S(1)} %copy-done.9, bf16[2,512,256]{2,1,0:T(8,128)(2,1)S(1)} %collective-permute-done.3.refs_1_, ...), custom_call_target="tpu_custom_call" | custom-call | flops 1207959552 | bytes 4718592 | tf_op jit(solution)/shard_map/weight_grad/pallas_call | solution.py:401
  78.1 0.1 collective-permute-start.19
  78.2 4.1 %collective-permute-start.15 = (bf16[128,2048]{1,0:T(8,128)(2,1)S(1)}, bf16[128,2048]{1,0:T(8,128)(2,1)S(1)}, u32[]{:S(2)}, u32[]{:S(2)}) collective-permute-start(bf16[128,2048]{1,0:T(8,128)(2,1)S(1)} %get-tuple-element.78), channel_id=1, source_target_pairs={{0,1},{1,0},{2,3},{3,2},{4,5},{5,4},{6,7},{7,6},{8,9},{9,8},{10,11... | collective-permute-start | bytes 1572872 | tf_op jit(solution)/shard_map/ppermute | solution.py:30
  82.3 0.3 collective-permute-start.17
  82.6 2.5 %weight_grad.3 = (bf16[128,1152]{1,0:T(8,128)(2,1)S(1)}, bf16[128,1152]{1,0:T(8,128)(2,1)S(1)}, bf16[128,1152]{1,0:T(8,128)(2,1)S(1)}, bf16[128,1152]{1,0:T(8,128)(2,1)S(1)}) custom-call(bf16[2,512,256]{2,1,0:T(8,128)(2,1)S(1)} %copy-done.9, bf16[2,512,256]{2,1,0:T(8,128)(2,1)S(1)} %collective-permute-done.3.refs_1_, ...), custom_call_target="tpu_custom_call" | custom-call | flops 1207959552 | bytes 4718592 | tf_op jit(solution)/shard_map/weight_grad/pallas_call | solution.py:401
  85.1 1.3 %collective-permute-start.25 = (bf16[128,1152]{1,0:T(8,128)(2,1)S(1)}, bf16[128,1152]{1,0:T(8,128)(2,1)S(1)}, u32[]{:S(2)}, u32[]{:S(2)}) collective-permute-start(bf16[128,1152]{1,0:T(8,128)(2,1)S(1)} %get-tuple-element.96), channel_id=1, source_target_pairs={{0,192},{1,193},{2,194},{3,195},{4,196},{5,197},{6,198},{7,199},{8... | collective-permute-start | bytes 884744 | tf_op jit(solution)/shard_map/ppermute | solution.py:30
  86.4 0.1 collective-permute-start.23
  86.5 1.9 %collective-permute-done.19 = bf16[128,1152]{1,0:T(8,128)(2,1)S(1)} collective-permute-done((bf16[128,1152]{1,0:T(8,128)(2,1)S(1)}, bf16[128,1152]{1,0:T(8,128)(2,1)S(1)}, u32[]{:S(2)}, u32[]{:S(2)}) %collective-permute-start.19) | collective-permute-done | bytes 294944 | tf_op jit(solution)/shard_map/ppermute | solution.py:30
  88.5 0.1 collective-permute-start.20
  88.6 3.1 %collective-permute-done.17 = bf16[128,1152]{1,0:T(8,128)(2,1)S(1)} collective-permute-done((bf16[128,1152]{1,0:T(8,128)(2,1)S(1)}, bf16[128,1152]{1,0:T(8,128)(2,1)S(1)}, u32[]{:S(2)}, u32[]{:S(2)}) %collective-permute-start.17) | collective-permute-done | bytes 294944 | tf_op jit(solution)/shard_map/ppermute | solution.py:30
  91.7 3.8 %collective-permute-start.18 = (bf16[64,1152]{1,0:T(8,128)(2,1)S(1)}, bf16[64,1152]{1,0:T(8,128)(2,1)S(1)}, u32[]{:S(2)}, u32[]{:S(2)}) collective-permute-start(bf16[64,1152]{1,0:T(8,128)(2,1)S(1)} %add_convert_fusion.8), channel_id=1, source_target_pairs={{0,12},{1,13},{2,14},{3,15},{4,8},{5,9},{6,10},{7,11},{8,4},{9,5},... | collective-permute-start | bytes 442376 | tf_op jit(solution)/shard_map/ppermute | solution.py:30
  95.6 1.3 %collective-permute-start.26 = (bf16[64,1152]{1,0:T(8,128)(2,1)S(1)}, bf16[64,1152]{1,0:T(8,128)(2,1)S(1)}, u32[]{:S(2)}, u32[]{:S(2)}) collective-permute-start(bf16[64,1152]{1,0:T(8,128)(2,1)S(1)} %add_convert_fusion.3), channel_id=1, source_target_pairs={{0,64},{1,65},{2,66},{3,67},{4,68},{5,69},{6,70},{7,71},{8,72},{9,... | collective-permute-start | bytes 442376 | tf_op jit(solution)/shard_map/ppermute | solution.py:30
  96.9 0.3 collective-permute-start.24
  97.3 3.3 %collective-permute-start.21 = (bf16[64,1152]{1,0:T(8,128)(2,1)S(1)}, bf16[64,1152]{1,0:T(8,128)(2,1)S(1)}, u32[]{:S(2)}, u32[]{:S(2)}) collective-permute-start(bf16[64,1152]{1,0:T(8,128)(2,1)S(1)} %add_convert_fusion.6), channel_id=1, source_target_pairs={{0,192},{1,193},{2,194},{3,195},{4,196},{5,197},{6,198},{7,199},{8... | collective-permute-start | bytes 442376 | tf_op jit(solution)/shard_map/ppermute | solution.py:30
  100.6 0.2 collective-permute-done.26
  100.9 2.4 %collective-permute-start.27 = (bf16[64,1152]{1,0:T(8,128)(2,1)S(1)}, bf16[64,1152]{1,0:T(8,128)(2,1)S(1)}, u32[]{:S(2)}, u32[]{:S(2)}) collective-permute-start(bf16[64,1152]{1,0:T(8,128)(2,1)S(1)} %add_convert_fusion.2), channel_id=1, source_target_pairs={{0,12},{1,13},{2,14},{3,15},{4,8},{5,9},{6,10},{7,11},{8,4},{9,5},... | collective-permute-start | bytes 442376 | tf_op jit(solution)/shard_map/ppermute | solution.py:30
  103.2 1.9 %collective-permute-done.21 = bf16[64,1152]{1,0:T(8,128)(2,1)S(1)} collective-permute-done((bf16[64,1152]{1,0:T(8,128)(2,1)S(1)}, bf16[64,1152]{1,0:T(8,128)(2,1)S(1)}, u32[]{:S(2)}, u32[]{:S(2)}) %collective-permute-start.21) | collective-permute-done | bytes 147488 | tf_op jit(solution)/shard_map/ppermute | solution.py:30
  105.2 2.1 %collective-permute-done.27 = bf16[64,1152]{1,0:T(8,128)(2,1)S(1)} collective-permute-done((bf16[64,1152]{1,0:T(8,128)(2,1)S(1)}, bf16[64,1152]{1,0:T(8,128)(2,1)S(1)}, u32[]{:S(2)}, u32[]{:S(2)}) %collective-permute-start.27) | collective-permute-done | bytes 147488 | tf_op jit(solution)/shard_map/ppermute | solution.py:30
  107.4 3.8 %collective-permute-start.30 = (bf16[16,2304]{1,0:T(8,128)(2,1)S(1)}, bf16[16,2304]{1,0:T(8,128)(2,1)S(1)}, u32[]{:S(2)}, u32[]{:S(2)}) collective-permute-start(bf16[16,2304]{1,0:T(8,128)(2,1)S(1)} %get-tuple-element.100), channel_id=1, source_target_pairs={{0,32},{1,33},{2,34},{3,35},{4,36},{5,37},{6,38},{7,39},{8,40},{9,... | collective-permute-start | bytes 221192 | tf_op jit(solution)/shard_map/ppermute | solution.py:30
  111.2 1.8 %collective-permute-start.29 = (bf16[16,2304]{1,0:T(8,128)(2,1)S(1)}, bf16[16,2304]{1,0:T(8,128)(2,1)S(1)}, u32[]{:S(2)}, u32[]{:S(2)}) collective-permute-start(bf16[16,2304]{1,0:T(8,128)(2,1)S(1)} %get-tuple-element.101), channel_id=1, source_target_pairs={{0,48},{1,49},{2,50},{3,51},{4,52},{5,53},{6,54},{7,55},{8,56},{9,... | collective-permute-start | bytes 221192 | tf_op jit(solution)/shard_map/ppermute | solution.py:30
  113.0 1.1 collective-permute-start.28
  114.1 0.9 fusion
  115.0 0.8 collective-permute-done.30
  115.9 1.7 %collective-permute-done.29 = bf16[16,2304]{1,0:T(8,128)(2,1)S(1)} collective-permute-done((bf16[16,2304]{1,0:T(8,128)(2,1)S(1)}, bf16[16,2304]{1,0:T(8,128)(2,1)S(1)}, u32[]{:S(2)}, u32[]{:S(2)}) %collective-permute-start.29) | collective-permute-done | bytes 73760 | tf_op jit(solution)/shard_map/ppermute | solution.py:30
  117.6 1.9 %collective-permute-done.28 = bf16[16,2304]{1,0:T(8,128)(2,1)S(1)} collective-permute-done((bf16[16,2304]{1,0:T(8,128)(2,1)S(1)}, bf16[16,2304]{1,0:T(8,128)(2,1)S(1)}, u32[]{:S(2)}, u32[]{:S(2)}) %collective-permute-start.28) | collective-permute-done | bytes 73760 | tf_op jit(solution)/shard_map/ppermute | solution.py:30
  119.6 0.7 maximum_bitcast_fusion
  (65 shorter events, 0.6 us)
Async XLA Ops:
  0.6 15.1 %copy-start = (bf16[1,256,2048]{2,1,0:T(8,128)(2,1)S(1)}, bf16[1,256,2048]{2,1,0:T(8,128)(2,1)}, u32[]{:S(2)}) copy-start(bf16[1,256,2048]{2,1,0:T(8,128)(2,1)} %param.6) | copy-start | bytes 3145732
  0.6 15.1 %copy-start.5 = (f32[128]{0:T(128)S(1)}, f32[128]{0:T(128)}, u32[]{:S(2)}) copy-start(f32[128]{0:T(128)} %param.8) | copy-start | bytes 1540
  0.7 22.2 %copy-start.15 = (s32[128,9]{0,1:T(8,128)S(1)}, s32[128,9]{0,1:T(8,128)}, u32[]{:S(2)}) copy-start(s32[128,9]{0,1:T(8,128)} %param.10) | copy-start | bytes 13828
  0.7 52.5 %copy-start.4 = (f32[128]{0:T(128)S(1)}, f32[128]{0:T(128)}, u32[]{:S(2)}) copy-start(f32[128]{0:T(128)} %param.9) | copy-start | bytes 1540
  6.8 28.7 %copy-start.1 = (bf16[2,256,768]{2,1,0:T(8,128)(2,1)S(1)}, bf16[2,256,768]{2,1,0:T(8,128)(2,1)}, u32[]{:S(2)}) copy-start(bf16[2,256,768]{2,1,0:T(8,128)(2,1)} %get-tuple-element.53.own_ref.kv_ref) | copy-start | bytes 2359300
  6.8 46.4 %copy-start.2 = (f32[256,768]{1,0:T(8,128)S(1)}, f32[256,768]{1,0:T(8,128)}, u32[]{:S(2)}) copy-start(f32[256,768]{1,0:T(8,128)} %get-tuple-element.63.raw_ref) | copy-start | bytes 2359300
  6.8 22.7 %collective-permute-start = (bf16[2,256,768]{2,1,0:T(8,128)(2,1)}, bf16[2,256,768]{2,1,0:T(8,128)(2,1)}, u32[]{:S(2)}, u32[]{:S(2)}) collective-permute-start(bf16[2,256,768]{2,1,0:T(8,128)(2,1)} %get-tuple-element.53.own_ref.kv_ref), channel_id=1, source_target_pairs={{0,2},{1,3},{2,0},{3,1},{4,6},{5,7},{6,4},{7,5},{8,10},{9,11},{10,... | collective-permute-start | bytes 2359304 | tf_op jit(solution)/shard_map/ppermute | solution.py:30
  6.9 28.6 %collective-permute-start.2 = (bf16[2,256,768]{2,1,0:T(8,128)(2,1)}, bf16[2,256,768]{2,1,0:T(8,128)(2,1)}, u32[]{:S(2)}, u32[]{:S(2)}) collective-permute-start(bf16[2,256,768]{2,1,0:T(8,128)(2,1)} %get-tuple-element.53.own_ref.kv_ref), channel_id=1, source_target_pairs={{0,62},{1,63},{2,4},{3,5},{4,2},{5,3},{6,8},{7,9},{8,6},{9,7},{10,... | collective-permute-start | bytes 2359304 | tf_op jit(solution)/shard_map/ppermute | solution.py:30
  15.8 1.0 copy-start.3
  21.1 0.9 copy-start.6
  22.0 7.5 %collective-permute-start.1 = (bf16[2,256,768]{2,1,0:T(8,128)(2,1)}, bf16[2,256,768]{2,1,0:T(8,128)(2,1)}, u32[]{:S(2)}, u32[]{:S(2)}) collective-permute-start(bf16[2,256,768]{2,1,0:T(8,128)(2,1)} %get-tuple-element.54.qg_ref.own_ref), channel_id=1, source_target_pairs={{0,2},{1,3},{2,0},{3,1},{4,6},{5,7},{6,4},{7,5},{8,10},{9,11},{10,... | collective-permute-start | bytes 2359304 | tf_op jit(solution)/shard_map/ppermute | solution.py:30
  22.0 29.4 %collective-permute-start.4 = (bf16[2,256,768]{2,1,0:T(8,128)(2,1)}, bf16[2,256,768]{2,1,0:T(8,128)(2,1)}, u32[]{:S(2)}, u32[]{:S(2)}) collective-permute-start(bf16[2,256,768]{2,1,0:T(8,128)(2,1)} %get-tuple-element.54.qg_ref.own_ref), channel_id=1, source_target_pairs={{0,62},{1,63},{2,4},{3,5},{4,2},{5,3},{6,8},{7,9},{8,6},{9,7},{10,... | collective-permute-start | bytes 2359304 | tf_op jit(solution)/shard_map/ppermute | solution.py:30
  24.8 0.8 copy-start.8
  25.6 0.8 copy-start.10
  26.4 0.7 copy-start.11
  27.1 0.7 copy-start.12
  27.8 0.7 copy-start.13
  28.6 0.7 copy-start.14
  29.6 5.9 %collective-permute-start.3 = (bf16[2,512,256]{2,1,0:T(8,128)(2,1)}, bf16[2,512,256]{2,1,0:T(8,128)(2,1)S(1)}, u32[]{:S(2)}, u32[]{:S(2)}) collective-permute-start(bf16[2,512,256]{2,1,0:T(8,128)(2,1)} %copy-done.10), channel_id=1, source_target_pairs={{0,2},{1,3},{2,0},{3,1},{4,6},{5,7},{6,4},{7,5},{8,10},{9,11},{10,... | collective-permute-start | bytes 1572872 | tf_op jit(solution)/shard_map/ppermute | solution.py:30
  29.7 14.2 %collective-permute-start.5 = (bf16[512,256]{1,0:T(8,128)(2,1)}, bf16[512,256]{1,0:T(8,128)(2,1)S(1)}, u32[]{:S(2)}, u32[]{:S(2)}) collective-permute-start(bf16[512,256]{1,0:T(8,128)(2,1)} %copy-done.14), channel_id=1, source_target_pairs={{0,64},{1,65},{2,66},{3,67},{4,68},{5,69},{6,70},{7,71},{8,72},{9,... | collective-permute-start | bytes 786440 | tf_op jit(solution)/shard_map/ppermute | solution.py:30
  30.6 13.3 %collective-permute-start.6 = (bf16[512,256]{1,0:T(8,128)(2,1)}, bf16[512,256]{1,0:T(8,128)(2,1)S(1)}, u32[]{:S(2)}, u32[]{:S(2)}) collective-permute-start(bf16[512,256]{1,0:T(8,128)(2,1)} %copy-done.13), channel_id=1, source_target_pairs={{0,66},{1,67},{2,64},{3,65},{4,70},{5,71},{6,68},{7,69},{8,74},{9,... | collective-permute-start | bytes 786440 | tf_op jit(solution)/shard_map/ppermute | solution.py:30
  35.5 22.6 %collective-permute-start.9 = (bf16[512,256]{1,0:T(8,128)(2,1)}, bf16[512,256]{1,0:T(8,128)(2,1)S(1)}, u32[]{:S(2)}, u32[]{:S(2)}) collective-permute-start(bf16[512,256]{1,0:T(8,128)(2,1)} %copy-done.12), channel_id=1, source_target_pairs={{0,4},{1,5},{2,6},{3,7},{4,0},{5,1},{6,2},{7,3},{8,12},{9,13},{10,... | collective-permute-start | bytes 786440 | tf_op jit(solution)/shard_map/ppermute | solution.py:30
  35.5 22.6 %collective-permute-start.10 = (bf16[512,256]{1,0:T(8,128)(2,1)}, bf16[512,256]{1,0:T(8,128)(2,1)S(1)}, u32[]{:S(2)}, u32[]{:S(2)}) collective-permute-start(bf16[512,256]{1,0:T(8,128)(2,1)} %copy-done.11), channel_id=1, source_target_pairs={{0,6},{1,7},{2,4},{3,5},{4,2},{5,3},{6,0},{7,1},{8,14},{9,15},{10,... | collective-permute-start | bytes 786440 | tf_op jit(solution)/shard_map/ppermute | solution.py:30
  35.5 1.1 copy-start.7
  36.6 38.9 %copy-start.9 = (bf16[2,512,256]{2,1,0:T(8,128)(2,1)S(1)}, bf16[2,512,256]{2,1,0:T(8,128)(2,1)}, u32[]{:S(2)}) copy-start(bf16[2,512,256]{2,1,0:T(8,128)(2,1)} %copy-done.8) | copy-start | bytes 1572868
  43.9 9.3 %collective-permute-start.7 = (f32[6,8,256]{2,1,0:T(8,128)S(1)}, f32[6,8,256]{2,1,0:T(8,128)S(1)}, u32[]{:S(2)}, u32[]{:S(2)}) collective-permute-start(f32[6,8,256]{2,1,0:T(8,128)S(1)} %get-tuple-element.68.so_ref), channel_id=1, source_target_pairs={{0,62},{1,63},{2,4},{3,5},{4,2},{5,3},{6,8},{7,9},{8,6},{9,7},{10,... | collective-permute-start | bytes 147464 | tf_op jit(solution)/shard_map/ppermute | solution.py:30
  51.4 1.8 %collective-permute-start.8 = (f32[6,8,256]{2,1,0:T(8,128)S(1)}, f32[6,8,256]{2,1,0:T(8,128)S(1)}, u32[]{:S(2)}, u32[]{:S(2)}) collective-permute-start(f32[6,8,256]{2,1,0:T(8,128)S(1)} %get-tuple-element.68.so_ref), channel_id=1, source_target_pairs={{0,2},{1,3},{2,0},{3,1},{4,6},{5,7},{6,4},{7,5},{8,10},{9,11},{10,... | collective-permute-start | bytes 147464 | tf_op jit(solution)/shard_map/ppermute | solution.py:30
  58.1 14.9 %collective-permute-start.11 = (bf16[256,1152]{1,0:T(8,128)(2,1)S(1)}, bf16[256,1152]{1,0:T(8,128)(2,1)S(1)}, u32[]{:S(2)}, u32[]{:S(2)}) collective-permute-start(bf16[256,1152]{1,0:T(8,128)(2,1)S(1)} %get-tuple-element.74.da_ref.refs_4_), channel_id=1, source_target_pairs={{0,64},{1,65},{2,66},{3,67},{4,68},{5,69},{6,70},{7,71},{8,72},{9,... | collective-permute-start | bytes 1769480 | tf_op jit(solution)/shard_map/ppermute | solution.py:30
  59.0 14.5 %collective-permute-start.12 = (bf16[256,1152]{1,0:T(8,128)(2,1)S(1)}, bf16[256,1152]{1,0:T(8,128)(2,1)S(1)}, u32[]{:S(2)}, u32[]{:S(2)}) collective-permute-start(bf16[256,1152]{1,0:T(8,128)(2,1)S(1)} %get-tuple-element.75.db_ref.refs_4_), channel_id=1, source_target_pairs={{0,4},{1,5},{2,6},{3,7},{4,0},{5,1},{6,2},{7,3},{8,12},{9,13},{10,... | collective-permute-start | bytes 1769480 | tf_op jit(solution)/shard_map/ppermute | solution.py:30
  59.0 14.5 %collective-permute-start.13 = (bf16[256,1152]{1,0:T(8,128)(2,1)S(1)}, bf16[256,1152]{1,0:T(8,128)(2,1)S(1)}, u32[]{:S(2)}, u32[]{:S(2)}) collective-permute-start(bf16[256,1152]{1,0:T(8,128)(2,1)S(1)} %get-tuple-element.74.da_ref.refs_4_), channel_id=1, source_target_pairs={{0,2},{1,3},{2,0},{3,1},{4,6},{5,7},{6,4},{7,5},{8,10},{9,11},{10,... | collective-permute-start | bytes 1769480 | tf_op jit(solution)/shard_map/ppermute | solution.py:30
  59.0 14.5 %collective-permute-start.14 = (bf16[256,1152]{1,0:T(8,128)(2,1)S(1)}, bf16[256,1152]{1,0:T(8,128)(2,1)S(1)}, u32[]{:S(2)}, u32[]{:S(2)}) collective-permute-start(bf16[256,1152]{1,0:T(8,128)(2,1)S(1)} %get-tuple-element.75.db_ref.refs_4_), channel_id=1, source_target_pairs={{0,2},{1,3},{2,0},{3,1},{4,6},{5,7},{6,4},{7,5},{8,10},{9,11},{10,... | collective-permute-start | bytes 1769480 | tf_op jit(solution)/shard_map/ppermute | solution.py:30
  73.5 2.0 %collective-permute-start.16 = (bf16[256,1152]{1,0:T(8,128)(2,1)S(1)}, bf16[256,1152]{1,0:T(8,128)(2,1)S(1)}, u32[]{:S(2)}, u32[]{:S(2)}) collective-permute-start(bf16[256,1152]{1,0:T(8,128)(2,1)S(1)} %collective-permute-done.11.refs_6_), channel_id=1, source_target_pairs={{0,2},{1,3},{2,0},{3,1},{4,6},{5,7},{6,4},{7,5},{8,10},{9,11},{10,... | collective-permute-start | bytes 1769480 | tf_op jit(solution)/shard_map/ppermute | solution.py:30
  73.5 9.1 %collective-permute-start.22 = (bf16[256,1152]{1,0:T(8,128)(2,1)S(1)}, bf16[256,1152]{1,0:T(8,128)(2,1)S(1)}, u32[]{:S(2)}, u32[]{:S(2)}) collective-permute-start(bf16[256,1152]{1,0:T(8,128)(2,1)S(1)} %collective-permute-done.12.refs_6_), channel_id=1, source_target_pairs={{0,2},{1,3},{2,0},{3,1},{4,6},{5,7},{6,4},{7,5},{8,10},{9,11},{10,... | collective-permute-start | bytes 1769480 | tf_op jit(solution)/shard_map/ppermute | solution.py:30
  78.1 10.3 %collective-permute-start.19 = (bf16[128,1152]{1,0:T(8,128)(2,1)S(1)}, bf16[128,1152]{1,0:T(8,128)(2,1)S(1)}, u32[]{:S(2)}, u32[]{:S(2)}) collective-permute-start(bf16[128,1152]{1,0:T(8,128)(2,1)S(1)} %get-tuple-element.88), channel_id=1, source_target_pairs={{0,12},{1,13},{2,14},{3,15},{4,8},{5,9},{6,10},{7,11},{8,4},{9,5},... | collective-permute-start | bytes 884744 | tf_op jit(solution)/shard_map/ppermute | solution.py:30
  78.2 35.9 %collective-permute-start.15 = (bf16[128,2048]{1,0:T(8,128)(2,1)S(1)}, bf16[128,2048]{1,0:T(8,128)(2,1)S(1)}, u32[]{:S(2)}, u32[]{:S(2)}) collective-permute-start(bf16[128,2048]{1,0:T(8,128)(2,1)S(1)} %get-tuple-element.78), channel_id=1, source_target_pairs={{0,1},{1,0},{2,3},{3,2},{4,5},{5,4},{6,7},{7,6},{8,9},{9,8},{10,11... | collective-permute-start | bytes 1572872 | tf_op jit(solution)/shard_map/ppermute | solution.py:30
  82.3 9.3 %collective-permute-start.17 = (bf16[128,1152]{1,0:T(8,128)(2,1)S(1)}, bf16[128,1152]{1,0:T(8,128)(2,1)S(1)}, u32[]{:S(2)}, u32[]{:S(2)}) collective-permute-start(bf16[128,1152]{1,0:T(8,128)(2,1)S(1)} %get-tuple-element.86), channel_id=1, source_target_pairs={{0,4},{1,5},{2,6},{3,7},{4,0},{5,1},{6,2},{7,3},{8,12},{9,13},{10,... | collective-permute-start | bytes 884744 | tf_op jit(solution)/shard_map/ppermute | solution.py:30
  85.1 10.4 %collective-permute-start.25 = (bf16[128,1152]{1,0:T(8,128)(2,1)S(1)}, bf16[128,1152]{1,0:T(8,128)(2,1)S(1)}, u32[]{:S(2)}, u32[]{:S(2)}) collective-permute-start(bf16[128,1152]{1,0:T(8,128)(2,1)S(1)} %get-tuple-element.96), channel_id=1, source_target_pairs={{0,192},{1,193},{2,194},{3,195},{4,196},{5,197},{6,198},{7,199},{8... | collective-permute-start | bytes 884744 | tf_op jit(solution)/shard_map/ppermute | solution.py:30
  86.4 10.4 %collective-permute-start.23 = (bf16[128,1152]{1,0:T(8,128)(2,1)S(1)}, bf16[128,1152]{1,0:T(8,128)(2,1)S(1)}, u32[]{:S(2)}, u32[]{:S(2)}) collective-permute-start(bf16[128,1152]{1,0:T(8,128)(2,1)S(1)} %get-tuple-element.94), channel_id=1, source_target_pairs={{0,64},{1,65},{2,66},{3,67},{4,68},{5,69},{6,70},{7,71},{8,72},{9,... | collective-permute-start | bytes 884744 | tf_op jit(solution)/shard_map/ppermute | solution.py:30
  88.5 8.7 %collective-permute-start.20 = (bf16[64,1152]{1,0:T(8,128)(2,1)S(1)}, bf16[64,1152]{1,0:T(8,128)(2,1)S(1)}, u32[]{:S(2)}, u32[]{:S(2)}) collective-permute-start(bf16[64,1152]{1,0:T(8,128)(2,1)S(1)} %add_convert_fusion.7), channel_id=1, source_target_pairs={{0,4},{1,5},{2,6},{3,7},{4,0},{5,1},{6,2},{7,3},{8,12},{9,13},{10,... | collective-permute-start | bytes 442376 | tf_op jit(solution)/shard_map/ppermute | solution.py:30
  91.7 11.5 %collective-permute-start.18 = (bf16[64,1152]{1,0:T(8,128)(2,1)S(1)}, bf16[64,1152]{1,0:T(8,128)(2,1)S(1)}, u32[]{:S(2)}, u32[]{:S(2)}) collective-permute-start(bf16[64,1152]{1,0:T(8,128)(2,1)S(1)} %add_convert_fusion.8), channel_id=1, source_target_pairs={{0,12},{1,13},{2,14},{3,15},{4,8},{5,9},{6,10},{7,11},{8,4},{9,5},... | collective-permute-start | bytes 442376 | tf_op jit(solution)/shard_map/ppermute | solution.py:30
  95.6 5.2 %collective-permute-start.26 = (bf16[64,1152]{1,0:T(8,128)(2,1)S(1)}, bf16[64,1152]{1,0:T(8,128)(2,1)S(1)}, u32[]{:S(2)}, u32[]{:S(2)}) collective-permute-start(bf16[64,1152]{1,0:T(8,128)(2,1)S(1)} %add_convert_fusion.3), channel_id=1, source_target_pairs={{0,64},{1,65},{2,66},{3,67},{4,68},{5,69},{6,70},{7,71},{8,72},{9,... | collective-permute-start | bytes 442376 | tf_op jit(solution)/shard_map/ppermute | solution.py:30
  96.9 8.3 %collective-permute-start.24 = (bf16[64,1152]{1,0:T(8,128)(2,1)S(1)}, bf16[64,1152]{1,0:T(8,128)(2,1)S(1)}, u32[]{:S(2)}, u32[]{:S(2)}) collective-permute-start(bf16[64,1152]{1,0:T(8,128)(2,1)S(1)} %add_convert_fusion.4), channel_id=1, source_target_pairs={{0,192},{1,193},{2,194},{3,195},{4,196},{5,197},{6,198},{7,199},{8... | collective-permute-start | bytes 442376 | tf_op jit(solution)/shard_map/ppermute | solution.py:30
  97.3 7.8 %collective-permute-start.21 = (bf16[64,1152]{1,0:T(8,128)(2,1)S(1)}, bf16[64,1152]{1,0:T(8,128)(2,1)S(1)}, u32[]{:S(2)}, u32[]{:S(2)}) collective-permute-start(bf16[64,1152]{1,0:T(8,128)(2,1)S(1)} %add_convert_fusion.6), channel_id=1, source_target_pairs={{0,192},{1,193},{2,194},{3,195},{4,196},{5,197},{6,198},{7,199},{8... | collective-permute-start | bytes 442376 | tf_op jit(solution)/shard_map/ppermute | solution.py:30
  100.9 6.4 %collective-permute-start.27 = (bf16[64,1152]{1,0:T(8,128)(2,1)S(1)}, bf16[64,1152]{1,0:T(8,128)(2,1)S(1)}, u32[]{:S(2)}, u32[]{:S(2)}) collective-permute-start(bf16[64,1152]{1,0:T(8,128)(2,1)S(1)} %add_convert_fusion.2), channel_id=1, source_target_pairs={{0,12},{1,13},{2,14},{3,15},{4,8},{5,9},{6,10},{7,11},{8,4},{9,5},... | collective-permute-start | bytes 442376 | tf_op jit(solution)/shard_map/ppermute | solution.py:30
  107.4 8.5 %collective-permute-start.30 = (bf16[16,2304]{1,0:T(8,128)(2,1)S(1)}, bf16[16,2304]{1,0:T(8,128)(2,1)S(1)}, u32[]{:S(2)}, u32[]{:S(2)}) collective-permute-start(bf16[16,2304]{1,0:T(8,128)(2,1)S(1)} %get-tuple-element.100), channel_id=1, source_target_pairs={{0,32},{1,33},{2,34},{3,35},{4,36},{5,37},{6,38},{7,39},{8,40},{9,... | collective-permute-start | bytes 221192 | tf_op jit(solution)/shard_map/ppermute | solution.py:30
  111.2 6.3 %collective-permute-start.29 = (bf16[16,2304]{1,0:T(8,128)(2,1)S(1)}, bf16[16,2304]{1,0:T(8,128)(2,1)S(1)}, u32[]{:S(2)}, u32[]{:S(2)}) collective-permute-start(bf16[16,2304]{1,0:T(8,128)(2,1)S(1)} %get-tuple-element.101), channel_id=1, source_target_pairs={{0,48},{1,49},{2,50},{3,51},{4,52},{5,53},{6,54},{7,55},{8,56},{9,... | collective-permute-start | bytes 221192 | tf_op jit(solution)/shard_map/ppermute | solution.py:30
  113.0 6.5 %collective-permute-start.28 = (bf16[16,2304]{1,0:T(8,128)(2,1)S(1)}, bf16[16,2304]{1,0:T(8,128)(2,1)S(1)}, u32[]{:S(2)}, u32[]{:S(2)}) collective-permute-start(bf16[16,2304]{1,0:T(8,128)(2,1)S(1)} %get-tuple-element.99), channel_id=1, source_target_pairs={{0,16},{1,17},{2,18},{3,19},{4,20},{5,21},{6,22},{7,23},{8,24},{9,... | collective-permute-start | bytes 221192 | tf_op jit(solution)/shard_map/ppermute | solution.py:30
